TPU v7x, 512 devices: a whole 4x8x8 slice. The times are simulated.
512 devices in a mesh: seq: 128 (over y, z_lo, x), ch: 4 (over z_hi, core).
Axes of the slice: x: 4, y: 8, z: 8 (z_hi: 2, z_lo: 4; z = z_hi * 4 + z_lo), core: 2. Of those that a mesh axis runs over, the one named last changes fastest.
Arguments:
- inputs: bfloat16 [256, 32768], P('ch', 'seq'), may hold values from -120 to 120
- clip_len: int32 [16], replicated, may hold values from 1 to 8192, 32768 in all
- clip_order: int32 [16], replicated, may hold values from 0 to 15, each once
- in_proj: bfloat16 [3, 256, 256], P(None, 'ch'), may hold values from -0.375 to 0.375
- out_proj: bfloat16 [256, 256], P(None, 'ch'), may hold values from -0.375 to 0.375
- filt_in: float32 [33, 64], replicated, may hold values from -4 to 4
- filt_out: float32 [2, 256, 64], P(None, 'ch'), may hold values from -0.75 to 0.75
- decay_rate: float32 [2, 256], P(None, 'ch'), may hold values from 0.2 to 1092.2667
- skip_gain: float32 [2, 256], P(None, 'ch'), may hold values from -4 to 4
- cotangent: bfloat16 [256, 32768], P('ch', 'seq'), may hold values from -6 to 6
Outputs:
- mixed: bfloat16 [256, 32768], P('ch', 'seq')
- grad_inputs: bfloat16 [256, 32768], P('ch', 'seq')
- grad_in_proj: float32 [3, 256, 256], P(None, 'ch')
- grad_out_proj: float32 [256, 256], P(None, 'ch')
- grad_filter: float32 [2, 256, 64], P(None, 'ch')
- grad_skip: float32 [2, 256], P(None, 'ch')
Inputs may be any that keep to these rules, and one draw needn't show every extreme that they name: `clip_len`: the lengths sum to 32768. `clip_order`: each clip appears once.
All inputs are finite; a program needn't handle non-finite values.
Results may differ from a plain program's by a relative error of at most 0.02.
Values may be sent and summed in bfloat16 or wider, within the bound.
No kernel may reach another device: no remote copies, remote signals or barrier semaphores. Data moves between devices by JAX's collectives and lax.ppermute only.
A program may use at most 128 MiB of HBM per device.

v0:
```python
import math

import jax
import jax.numpy as jnp
from jax import lax
from jax.sharding import PartitionSpec as P

EPSILON = 1e-05
HIGHEST_PRECISION = lax.Precision.HIGHEST


def rotation_table(out_count, in_count, modulus, orientation):
    out_index = lax.broadcasted_iota(jnp.int32, (out_count, in_count), 0)
    in_index = lax.broadcasted_iota(jnp.int32, (out_count, in_count), 1)
    angles = (
        orientation * 2.0 * math.pi / modulus * (out_index * in_index % modulus).astype(jnp.float32)
    )
    cosines = jnp.cos(angles)
    sines = jnp.sin(angles)
    return jnp.stack([jnp.stack([cosines, -sines], -1), jnp.stack([sines, cosines], -1)], 1)


def rotate(values, cosines, sines):
    real_part = values[:, :, 0]
    imag_part = values[:, :, 1]
    return jnp.stack(
        [cosines * real_part - sines * imag_part, sines * real_part + cosines * imag_part], 2
    )


def complex_product(first, second):
    return rotate(first, second[:, :, 0], second[:, :, 1])


def conjugate_product(first, second):
    return rotate(first, second[:, :, 0], -second[:, :, 1])


def column_swap(values):
    return lax.all_to_all(
        values.astype(jnp.bfloat16), "seq", split_axis=1, concat_axis=0, tiled=True
    ).astype(values.dtype)


def row_swap(values):
    return lax.all_to_all(
        values.astype(jnp.bfloat16), "seq", split_axis=0, concat_axis=1, tiled=True
    ).astype(values.dtype)


def channel_fold(values, update, initial):
    return update(initial, lax.all_gather(values, "ch", axis=0, tiled=True), jnp.int32(0))


def channel_reduce(term, rows):
    return lax.psum_scatter(
        term(jnp.int32(0), lax.axis_size("ch") * rows).astype(jnp.bfloat16),
        "ch",
        scatter_dimension=0,
        tiled=True,
    ).astype(jnp.float32)


def time_total(values):
    return lax.psum(values, "seq")


def filter_values(positions, total_len, filt_in, filt_out, decay_rate):
    bands = jnp.arange(1, filt_in.shape[0] // 2 + 1, dtype=jnp.int32)
    phases = (positions[:, :, None] * bands % total_len).astype(jnp.float32) * (
        2.0 * math.pi / total_len
    )
    ramp = positions.astype(jnp.float32) / total_len
    features = jnp.concatenate([ramp[:, :, None], jnp.cos(phases), jnp.sin(phases)], 2)
    hidden = jnp.sin(jnp.einsum("abf,fe->abe", features, filt_in, precision=HIGHEST_PRECISION))
    window = jnp.exp(-decay_rate[None, None] * ramp[:, :, None, None]) * total_len ** (-0.5)
    shapes = jnp.einsum("abe,ice->abic", hidden, filt_out, precision=HIGHEST_PRECISION) * window
    return (hidden, window, shapes.reshape(positions.shape[0], positions.shape[1], -1))


def shards(
    inputs,
    clip_len,
    clip_order,
    in_proj,
    out_proj,
    filt_in,
    filt_out,
    decay_rate,
    skip_gain,
    cotangent,
):
    devices = lax.axis_size("seq")
    rank = lax.axis_index("seq")
    channels = inputs.shape[0]
    local_len = inputs.shape[1]
    total_len = local_len * devices
    first_len = local_len // 2
    first_block = first_len // devices
    second_len = 4 * devices
    half_second = 2 * devices
    period = 2 * total_len
    width = in_proj.shape[2]
    hidden_width = filt_out.shape[2]
    forward_second = rotation_table(second_len, half_second, second_len, -1.0)[:, :, :, 0]
    forward_first = rotation_table(first_len, first_len, first_len, -1.0)
    inverse_first = rotation_table(first_len, first_len, first_len, 1.0)
    inverse_second = rotation_table(half_second, second_len, second_len, 1.0) * (1.0 / period)
    twist_rows = lax.broadcasted_iota(jnp.int32, (second_len, first_block), 0)
    twist_columns = (
        lax.broadcasted_iota(jnp.int32, (second_len, first_block), 1) + rank * first_block
    )
    twist = 2.0 * math.pi / period * (twist_rows * twist_columns % period).astype(jnp.float32)
    twist_cos = jnp.cos(twist)[:, :, None]
    twist_sin = jnp.sin(twist)[:, :, None]

    def to_spectrum(blocks):
        rows = jnp.einsum("kpn,nbw->kbpw", forward_second, blocks, precision=HIGHEST_PRECISION)
        columns = row_swap(rotate(rows, twist_cos, -twist_sin))
        return jnp.einsum("kpnq,anqw->akpw", forward_first, columns, precision=HIGHEST_PRECISION)

    def to_blocks(spectrum):
        columns = jnp.einsum(
            "npkq,akqw->anpw", inverse_first, spectrum, precision=HIGHEST_PRECISION
        )
        rows = rotate(column_swap(columns), twist_cos, twist_sin)
        return jnp.einsum("nkq,kbqw->nbw", inverse_second[:, 0], rows, precision=HIGHEST_PRECISION)

    def pair_blocks(spectrum, filter_spec, data_spec):
        with_filter = conjugate_product(spectrum, filter_spec)
        with_data = conjugate_product(spectrum, data_spec)
        result = to_blocks(jnp.concatenate([with_filter, with_data], 3))
        return result

    lengths = jnp.take(clip_len, clip_order)
    starts = jnp.cumsum(lengths, dtype=jnp.int32) - lengths
    positions = rank * local_len + jnp.arange(local_len, dtype=jnp.int32)
    member = (
        (positions[:, None] >= starts[None, :]) & (positions[:, None] < (starts + lengths)[None, :])
    ).astype(jnp.float32)

    def project_rows(carry, piece, start):
        partial_sum = jnp.einsum("icd,dt->tic", in_proj, piece, preferred_element_type=jnp.float32)
        squares = jnp.sum(jnp.square(piece.astype(jnp.float32)), 0)
        return (partial_sum, squares)

    raw, squares = channel_fold(
        inputs,
        project_rows,
        (jnp.zeros((local_len, 3, channels), jnp.float32), jnp.zeros((local_len,), jnp.float32)),
    )
    power = time_total(jnp.dot(squares, member, precision=HIGHEST_PRECISION))
    inverse_rms = lax.rsqrt(power / (width * lengths.astype(jnp.float32)) + EPSILON)
    scale = jnp.dot(member, inverse_rms, precision=HIGHEST_PRECISION)
    projected = lax.optimization_barrier((raw * scale[:, None, None]).astype(jnp.bfloat16))
    skip_one = skip_gain[0]
    skip_two = skip_gain[1]
    series = projected.reshape(2, first_len, 3 * channels)
    value_in = series[:, :, :channels].astype(jnp.float32)
    gate_one = series[:, :, channels : 2 * channels].astype(jnp.float32)
    gate_two = series[:, :, 2 * channels :].astype(jnp.float32)
    time_positions = (
        rank * local_len
        + lax.broadcasted_iota(jnp.int32, (2, first_len), 0) * first_len
        + lax.broadcasted_iota(jnp.int32, (2, first_len), 1)
    )
    hidden, window, shapes = filter_values(time_positions, total_len, filt_in, filt_out, decay_rate)
    spectra = to_spectrum(column_swap(jnp.concatenate([value_in, shapes], 2)))
    value_spec = spectra[:, :, :, :channels]
    filter_one = spectra[:, :, :, channels : 2 * channels]
    filter_two = spectra[:, :, :, 2 * channels :]
    carry_one = row_swap(to_blocks(complex_product(value_spec, filter_one))) + skip_one * value_in
    level_one = gate_one * carry_one
    level_spec = to_spectrum(column_swap(level_one))
    carry_two = row_swap(to_blocks(complex_product(level_spec, filter_two))) + skip_two * level_one
    gated = (gate_two * carry_two).astype(jnp.bfloat16)
    flat_gated = gated.reshape(local_len, channels)

    def mixed_term(start, count):
        return jnp.einsum("dc,tc->dt", out_proj, flat_gated, preferred_element_type=jnp.float32)

    mixed = channel_reduce(mixed_term, channels).astype(jnp.bfloat16)

    def cotangent_rows(carry, piece, start):
        back_sum = jnp.einsum("dc,dt->tc", out_proj, piece, preferred_element_type=jnp.float32)
        block = jnp.einsum("dt,tc->dc", piece, flat_gated, preferred_element_type=jnp.float32)
        return (back_sum, block)

    out_grad, out_weight = channel_fold(
        cotangent,
        cotangent_rows,
        (jnp.zeros((local_len, channels), jnp.float32), jnp.zeros((width, channels), jnp.float32)),
    )
    out_grad = out_grad.reshape(2, first_len, channels)
    scaled_two = gate_two * out_grad
    gate_two_grad = out_grad * carry_two
    pair_two = row_swap(pair_blocks(to_spectrum(column_swap(scaled_two)), filter_two, level_spec))
    level_grad = pair_two[:, :, :channels] + skip_two * scaled_two
    skip_two_grad = jnp.sum(scaled_two * level_one, (0, 1))
    scaled_one = gate_one * level_grad
    gate_one_grad = level_grad * carry_one
    pair_one = row_swap(pair_blocks(to_spectrum(column_swap(scaled_one)), filter_one, value_spec))
    value_grad = pair_one[:, :, :channels] + skip_one * scaled_one
    skip_one_grad = jnp.sum(scaled_one * value_in, (0, 1))
    front_grads = jnp.concatenate([value_grad, gate_one_grad], 2)
    shape_grads = jnp.stack([pair_one[:, :, channels:], pair_two[:, :, channels:]], 2) * window
    filter_grad = jnp.einsum("abe,abic->ice", hidden, shape_grads, precision=HIGHEST_PRECISION)
    stacked = jnp.concatenate([front_grads, gate_two_grad], 2).reshape(local_len, 3, channels)
    scaled_grad = (stacked * scale[:, None, None]).astype(jnp.bfloat16)
    skip_grad = jnp.stack([skip_one_grad, skip_two_grad])

    def input_term(start, count):
        return jnp.einsum("icd,tic->dt", in_proj, scaled_grad, preferred_element_type=jnp.float32)

    grad_inputs = channel_reduce(input_term, channels).astype(jnp.bfloat16)

    def weight_rows(carry, piece, start):
        block = jnp.einsum("tic,dt->icd", scaled_grad, piece, preferred_element_type=jnp.float32)
        return block

    in_weight = channel_fold(inputs, weight_rows, jnp.zeros((3, channels, width), jnp.float32))
    local_grads = jnp.concatenate(
        [
            in_weight.reshape(-1),
            out_weight.reshape(-1),
            filter_grad.reshape(-1),
            skip_grad.reshape(-1),
        ]
    )
    totals = time_total(local_grads) * total_len ** (-0.5)
    first_cut = 3 * channels * width
    second_cut = first_cut + width * channels
    third_cut = second_cut + 2 * channels * hidden_width
    return (
        mixed,
        grad_inputs,
        totals[:first_cut].reshape(3, channels, width),
        totals[first_cut:second_cut].reshape(width, channels),
        totals[second_cut:third_cut].reshape(2, channels, hidden_width),
        totals[third_cut:].reshape(2, channels),
    )


def solution(mesh):
    return jax.shard_map(
        shards,
        mesh=mesh,
        in_specs=(
            P("ch", "seq"),
            P(),
            P(),
            P(None, "ch", None),
            P(None, "ch"),
            P(),
            P(None, "ch", None),
            P(None, "ch"),
            P(None, "ch"),
            P("ch", "seq"),
        ),
        out_specs=(
            P("ch", "seq"),
            P("ch", "seq"),
            P(None, "ch", None),
            P(None, "ch"),
            P(None, "ch", None),
            P(None, "ch"),
        ),
        check_vma=False,
    )
```

profile of v0, /device:TPU:32, one launch (start us, length us, event | category | flops | bytes accessed | tf_op | source)
XLA Modules:
  0.0 2037.3 jit_solution(10189790905141497934)
XLA Ops:
  8.3 13.0 all_gather.7
  23.1 367.1 %psum.14 = f32[16]{0:T(128)S(1)} all-reduce(f32[16]{0:T(128)S(1)} %convolution_bitcast_fusion.20), channel_id=1, replica_groups=mesh['seq'=128,'ch'=4] {'seq'}, use_global_device_ids=true, to_apply=%region_2.3 | all-reduce | flops 16 | bytes 128 | tf_op jit(solution)/shard_map/psum | solution.py:65
  394.5 8.9 all-to-all-start
  413.5 12.6 all-to-all-start.1
  443.7 10.6 all-to-all-start.2
  454.3 9.9 all_gather.8
  473.5 14.3 all-to-all-start.3
  488.0 8.0 all-to-all-done.3
  502.1 10.3 all-to-all-start.8
  513.2 6.8 all-to-all-done.8
  520.7 11.3 all-to-all-start.4
  544.5 11.2 all-to-all-start.9
  563.5 11.7 all-to-all-start.5
  593.7 11.1 all-to-all-start.6
  612.5 10.1 all-to-all-start.10
  634.3 14.9 all-to-all-start.7
  657.0 10.2 all-to-all-start.11
  678.7 17.4 all_to_all.204
  697.2 17.8 all_to_all.205
  718.2 10.6 all-to-all-start.14
  729.6 8.3 all-to-all-done.14
  740.2 10.3 all-to-all-start.15
  751.0 7.2 all-to-all-done.15
  765.8 1258.9 %all-reduce.2.cloned.1.call-done = f32[73856]{0:T(1024)} async-done(((f32[73856]{0:T(1024)}), f32[73856]{0:T(1024)}) %all-reduce.2.cloned.1.call-update) | async-done | bytes 295440 | tf_op jit(solution)/shard_map/psum | solution.py:65
  (293 shorter events, 147.6 us)
Async XLA Ops:
  8.0 382.5 %copy-start = (bf16[3,64,256]{2,1,0:T(8,128)(2,1)S(1)}, bf16[3,64,256]{2,1,0:T(8,128)(2,1)}, u32[]{:S(2)}) copy-start(bf16[3,64,256]{2,1,0:T(8,128)(2,1)} %param.13) | copy-start | bytes 294916
  8.3 384.4 %copy-start.46 = (f32[2,128]{1,0:T(2,128)}, f32[2,128]{1,0:T(2,128)S(1)}, u32[]{:S(2)}) copy-start(f32[2,128]{1,0:T(2,128)S(1)} %convert_multiply_fusion.6) | copy-start | bytes 3076
  21.2 369.2 %copy-start.3 = (bf16[256,256]{1,0:T(8,128)(2,1)}, bf16[256,256]{1,0:T(8,128)(2,1)S(1)}, u32[]{:S(2)}) copy-start(bf16[256,256]{1,0:T(8,128)(2,1)S(1)} %all_gather.7) | copy-start | bytes 393220
  394.5 16.8 all-to-all-start
  413.5 23.6 %all-to-all-start.1 = ((bf16[512,1,2,192]{3,2,1,0:T(2,128)(2,1)}), bf16[512,1,2,192]{3,2,1,0:T(2,128)(2,1)}, u32[]{:S(2)}, u32[]{:S(2)}) async-start(bf16[512,1,2,192]{3,2,1,0:T(2,128)(2,1)} %copy.86), calls=%async_computation.1 | async-start | bytes 1048576 | tf_op jit(solution)/shard_map/all_to_all | solution.py:46
  426.9 13.7 copy-start.6
  426.9 13.7 copy-start.10
  443.7 21.2 %all-to-all-start.2 = ((bf16[128,2,256]{2,1,0:T(2,128)(2,1)}), bf16[128,2,256]{2,1,0:T(2,128)(2,1)S(1)}, u32[]{:S(2)}, u32[]{:S(2)}) async-start(bf16[128,2,256]{2,1,0:T(2,128)(2,1)} %reshape.996), calls=%async_computation.2 | async-start | bytes 262144 | tf_op jit(solution)/shard_map/all_to_all | solution.py:40
  464.2 23.6 %copy-start.14 = (bf16[256,256]{1,0:T(8,128)(2,1)}, bf16[256,256]{1,0:T(8,128)(2,1)S(1)}, u32[]{:S(2)}) copy-start(bf16[256,256]{1,0:T(8,128)(2,1)S(1)} %all_gather.8) | copy-start | bytes 393220
  473.5 14.3 copy-start.38
  473.5 22.5 %all-to-all-start.3 = ((bf16[256,1,64]{2,1,0:T(2,128)(2,1)}), bf16[256,1,64]{2,1,0:T(2,128)(2,1)}, u32[]{:S(2)}, u32[]{:S(2)}) async-start(bf16[256,1,64]{2,1,0:T(2,128)(2,1)} %copy.93), calls=%async_computation.3 | async-start | bytes 262144 | tf_op jit(solution)/shard_map/all_to_all | solution.py:46
  502.1 17.9 all-to-all-start.8
  520.7 19.0 all-to-all-start.4
  544.5 19.0 all-to-all-start.9
  563.5 19.4 all-to-all-start.5
  593.7 18.8 all-to-all-start.6
  612.5 21.8 %all-to-all-start.10 = ((bf16[4,128,2,128]{3,2,0,1:T(2,128)(2,1)}), bf16[4,128,2,128]{3,2,0,1:T(2,128)(2,1)S(1)}, u32[]{:S(2)}, u32[]{:S(2)}) async-start(bf16[4,128,2,128]{3,2,0,1:T(2,128)(2,1)} %copy.113), calls=%async_computation.10 | async-start | bytes 524288 | tf_op jit(solution)/shard_map/all_to_all | solution.py:40
  634.3 22.7 %all-to-all-start.7 = ((bf16[256,1,64]{2,1,0:T(2,128)(2,1)}), bf16[256,1,64]{2,1,0:T(2,128)(2,1)}, u32[]{:S(2)}, u32[]{:S(2)}) async-start(bf16[256,1,64]{2,1,0:T(2,128)(2,1)} %copy.104), calls=%async_computation.7 | async-start | bytes 262144 | tf_op jit(solution)/shard_map/all_to_all | solution.py:46
  657.0 17.8 all-to-all-start.11
  718.2 19.7 all-to-all-start.14
  740.2 18.0 all-to-all-start.15
  750.5 1274.1 %all-reduce.2.cloned.1.call-start = ((), (), s32[]{:S(2)}) async-start(), calls=%async_computation.18 | async-start | bytes 598016 | tf_op jit(solution)/shard_map/psum | solution.py:65
  763.0 1266.4 %reduce-scatter.7.cloned.1.call-start = ((), (), s32[]{:S(2)}) async-start(), calls=%async_computation.19 | async-start | bytes 163840
  764.7 1264.7 %reduce-scatter.9.cloned.1.call-start = ((), (), s32[]{:S(2)}) async-start(), calls=%async_computation.20 | async-start | bytes 163840
  (50 other events, 138.3 us)
Sparse Core Ops, SparseCore 0:
  763.1 1261.5 all-reduce.1
Sparse Core Ops, SparseCore 1:
  767.0 39.9 reduce-scatter.6
  810.6 36.9 reduce-scatter.8
where the time goes:
time: 2050 us; the launch traced here: 2040 us
  waiting for transfers between devices  1330 us (65%)
  blocking collectives  425 us (21%)
  starting transfers between devices  158 us (8%)
  local copies, waits for them, and re-layouts  58.5 us (3%)
  other arithmetic  29.3 us (1%)
    psum x1, waiting for transfers between devices, time_total(): return lax.psum(values, 'seq')  1260 us
    psum x1, blocking collectives, time_total(): return lax.psum(values, 'seq')  367 us
    all_to_all x7, starting transfers between devices, row_swap(): lax.all_to_all(values.astype(jnp.bfloat16), 'seq', split_axis=0, concat_a...  85.2 us
    all_to_all x7, starting transfers between devices, column_swap(): lax.all_to_all(values.astype(jnp.bfloat16), 'seq', split_axis=1, concat_a...  72.9 us
    all_to_all x7, waiting for transfers between devices, row_swap(): lax.all_to_all(values.astype(jnp.bfloat16), 'seq', split_axis=0, concat_a...  42 us
  transfers between devices with their start and end apart: 17, of which 13 were waited for; matrix products, arithmetic and copies ran while one was open for 2% of the time, Pallas kernels for 0%

commit v1 on v0

v1 whole, which is shorter than its diff:
```python
import functools
import math

import jax
import jax.numpy as jnp
import numpy as np
from jax import lax
from jax.experimental import pallas as pl
from jax.experimental.pallas import tpu as pltpu
from jax.sharding import PartitionSpec as P

EPSILON = 1e-05
HIGHEST = lax.Precision.HIGHEST
F32 = jnp.float32
BF16 = jnp.bfloat16

WIDTH = 256
TOTAL = 32768
SEQ = 128
CHUNK = 256
LOCAL = 64
HIDDEN = 64
BANDS = 16
CLIPS = 16
SEND_ROWS = 16
BACK_ROWS = 8


def halves(table):
    high = table.astype(BF16)
    low = (table - high.astype(np.float32)).astype(BF16)
    return high, low


def tables():
    k1 = np.arange(SEQ)[:, None] + 0.25
    s = np.arange(SEQ)[None, :]
    u = np.arange(CHUNK)[None, :]
    first = 2.0 * np.pi * k1 * s / SEQ
    analysis = np.concatenate([np.cos(first), -np.sin(first)], 0).astype(np.float32)
    synthesis = (np.concatenate([np.cos(first), -np.sin(first)], 0).T / TOTAL).astype(np.float32)
    twist = 2.0 * np.pi * k1 * u / TOTAL
    k2 = np.arange(CHUNK)
    second = 2.0 * np.pi * ((k2[:, None] * k2[None, :]) % CHUNK) / CHUNK
    inner = np.concatenate([np.cos(second), np.sin(second)], 1).astype(np.float32)
    return (
        *halves(analysis),
        *halves(synthesis),
        *halves(inner),
        np.cos(twist).astype(np.float32),
        np.sin(twist).astype(np.float32),
    )


def dot(a, b, dims=((1,), (0,)), precision=None):
    return lax.dot_general(a, b, (dims, ((), ())), precision=precision, preferred_element_type=F32)


def split(x):
    high = x.astype(BF16)
    return high, (x - high.astype(F32)).astype(BF16)


def clip_bounds(clip_len, clip_order):
    starts, lengths = [], []
    start = jnp.int32(0)
    for p in range(CLIPS):
        length = clip_len[clip_order[p]]
        starts.append(start)
        lengths.append(length)
        start = start + length
    return starts, lengths


def front_kernel(
    rank, clip_len, clip_order, full, in_proj, out_proj, filt_in, filt_out, decay,
    send, gate_out, grad_out, hidden_out, window_out, scratch,
):
    inputs = jnp.concatenate([full[128 * j : 128 * j + 64, :] for j in range(4)], 0)
    cotangent = jnp.concatenate([full[128 * j + 64 : 128 * j + 128, :] for j in range(4)], 0)
    raw = dot(in_proj[...], inputs)
    out_grad = dot(out_proj[...], cotangent, ((0,), (0,)))
    gate_two = raw[2 * LOCAL :, :]
    gate_out[...] = gate_two
    grad_out[...] = out_grad

    offset = rank[0] * CHUNK
    starts, lengths = clip_bounds(clip_len, clip_order)
    time = offset + lax.broadcasted_iota(jnp.int32, (SEQ, CHUNK), 1)
    place = lax.broadcasted_iota(jnp.int32, (SEQ, CHUNK), 0)
    member = jnp.zeros((SEQ, CHUNK), F32)
    for p in range(CLIPS):
        inside = (time >= starts[p]) & (time < starts[p] + lengths[p]) & (place == p)
        member = jnp.where(inside, 1.0, member)
    wide = inputs.astype(F32)
    squares = jnp.sum(wide * wide, 0, keepdims=True)
    power = dot(jnp.broadcast_to(squares, (8, CHUNK)), member, ((1,), (1,)), HIGHEST)[:1, :]
    high, low = split(power)
    mid = low.astype(F32)
    low = power - high.astype(F32) - mid
    high = high.astype(F32)

    step = offset + lax.broadcasted_iota(jnp.int32, (BANDS, CHUNK), 1)
    band = 1 + lax.broadcasted_iota(jnp.int32, (BANDS, CHUNK), 0)
    phases = ((step * band) & (TOTAL - 1)).astype(F32) * (2.0 * math.pi / TOTAL)
    ramp = (offset + lax.broadcasted_iota(jnp.int32, (8, CHUNK), 1)).astype(F32) * (1.0 / TOTAL)
    first_row = lax.broadcasted_iota(jnp.int32, (8, HIDDEN), 0) == 0
    ramp_weight = jnp.where(first_row, filt_in[:8, :], 0.0)
    first = ((0,), (0,))
    hidden = jnp.sin(
        dot(ramp_weight, ramp, first, HIGHEST)
        + dot(filt_in[1 : 1 + BANDS, :], jnp.cos(phases), first, HIGHEST)
        + dot(filt_in[1 + BANDS : 1 + 2 * BANDS, :], jnp.sin(phases), first, HIGHEST)
    )
    hidden_out[...] = hidden
    rows = lax.broadcasted_iota(jnp.int32, (LOCAL, LOCAL), 0)
    columns = lax.broadcasted_iota(jnp.int32, (LOCAL, LOCAL), 1)
    shapes = []
    for i in range(2):
        spread = jnp.broadcast_to(decay[i : i + 1, :], (LOCAL, LOCAL))
        rate = jnp.sum(jnp.where(rows == columns, spread, 0.0), 1, keepdims=True)
        window = jnp.exp(-rate * ramp[:1, :]) * TOTAL ** (-0.5)
        window_out[i * LOCAL : (i + 1) * LOCAL, :] = window
        weights = filt_out[i * LOCAL : (i + 1) * LOCAL, :]
        shapes.append(dot(weights, hidden, precision=HIGHEST) * window)

    arrays = [raw[:LOCAL, :], raw[LOCAL : 2 * LOCAL, :], gate_two * out_grad, *shapes]
    for at, values in enumerate(arrays):
        scratch[pl.ds(2 * at, LOCAL, stride=SEND_ROWS), :] = values[:, :128]
        scratch[pl.ds(2 * at + 1, LOCAL, stride=SEND_ROWS), :] = values[:, 128:]
    for at, values in enumerate([high, mid, low]):
        scratch[pl.ds(10 + at, LOCAL, stride=SEND_ROWS), :] = jnp.broadcast_to(values, (LOCAL, 128))
    for at in range(13, SEND_ROWS):
        scratch[pl.ds(at, LOCAL, stride=SEND_ROWS), :] = jnp.zeros((LOCAL, 128), F32)
    packed = scratch[...].astype(BF16)
    send[: LOCAL * SEND_ROWS, :] = packed
    send[LOCAL * SEND_ROWS :, :] = packed


def series_kernel(
    rank, clip_len, clip_order, skip_gain, received,
    analysis_high, analysis_low, synthesis_high, synthesis_low, inner_high, inner_low,
    twist_cos, twist_sin, back, scratch, packed,
):
    role = rank[0] // LOCAL
    channel = rank[0] % LOCAL
    forward = role == 0
    skip_one = skip_gain[0, channel]
    skip_two = skip_gain[1, channel]
    scratch[...] = received[...].astype(F32)

    def plane(row):
        return scratch[pl.ds(row, SEQ, stride=SEND_ROWS), :]

    def signal(at):
        return jnp.concatenate([plane(2 * at), plane(2 * at + 1)], 1)

    power = jnp.sum(plane(10) + (plane(11) + plane(12)), 0, keepdims=True)
    starts, lengths = clip_bounds(clip_len, clip_order)
    time = lax.broadcasted_iota(jnp.int32, (SEQ, CHUNK), 0) * CHUNK + lax.broadcasted_iota(
        jnp.int32, (SEQ, CHUNK), 1
    )
    lane = lax.broadcasted_iota(jnp.int32, (1, 128), 1)
    counts = jnp.ones((1, 128), F32)
    for p in range(CLIPS):
        counts = jnp.where(lane == p, lengths[p].astype(F32), counts)
    inverse_rms = lax.rsqrt(power / (WIDTH * counts) + EPSILON)
    scale = jnp.zeros((SEQ, CHUNK), F32)
    for p in range(CLIPS):
        scale = jnp.where(time >= starts[p], inverse_rms[:, p : p + 1], scale)

    cosines = twist_cos[...]
    sines = twist_sin[...]

    def turn(values, count):
        high, low = split(values)
        product = (
            dot(high, inner_high[...]) + dot(low, inner_high[...]) + dot(high, inner_low[...])
        )
        pieces = []
        for at in range(count):
            real = product[256 * at : 256 * at + 128, :]
            imag = product[256 * at + 128 : 256 * at + 256, :]
            pieces.append((real[:, :256], real[:, 256:], imag[:, :256], imag[:, 256:]))
        return pieces

    def to_spectrum(signals):
        stacked = jnp.concatenate(signals, 1)
        high, low = split(stacked)
        rows = (
            dot(analysis_high[...], high)
            + dot(analysis_high[...], low)
            + dot(analysis_low[...], high)
        )
        twisted = []
        for at in range(len(signals)):
            real = rows[:128, 256 * at : 256 * at + 256]
            imag = rows[128:, 256 * at : 256 * at + 256]
            twisted.append(cosines * real + sines * imag)
            twisted.append(cosines * imag - sines * real)
        pieces = turn(jnp.concatenate(twisted, 0), len(signals))
        return [(rc + is_, ic - rs) for rc, rs, ic, is_ in pieces]

    def to_signal(spectra):
        stacked = jnp.concatenate([part for pair in spectra for part in pair], 0)
        columns = []
        for rc, rs, ic, is_ in turn(stacked, len(spectra)):
            real = rc - is_
            imag = ic + rs
            columns.append(
                jnp.concatenate([cosines * real - sines * imag, cosines * imag + sines * real], 0)
            )
        high, low = split(jnp.concatenate(columns, 1))
        rows = (
            dot(synthesis_high[...], high)
            + dot(synthesis_high[...], low)
            + dot(synthesis_low[...], high)
        )
        return [rows[:, 256 * at : 256 * at + 256] for at in range(len(spectra))]

    def times(a, b, sign):
        return (a[0] * b[0] - sign * (a[1] * b[1]), a[1] * b[0] + sign * (a[0] * b[1]))

    def choose(a, b):
        return jnp.where(forward, a, b)

    def choose_spectrum(a, b):
        return tuple(choose(x, y) for x, y in zip(a, b))

    value = signal(0) * scale
    gate_one = signal(1) * scale
    scaled_two = signal(2) * scale
    value_spec, second_spec, filter_one, filter_two = to_spectrum(
        [value, scaled_two, signal(3), signal(4)]
    )
    carry_one, level_grad = to_signal(
        [times(value_spec, filter_one, 1.0), times(second_spec, filter_two, -1.0)]
    )
    carry_one = carry_one + skip_one * value
    level_grad = level_grad + skip_two * scaled_two
    level_one = gate_one * carry_one
    scaled_one = gate_one * level_grad
    level_spec, first_spec = to_spectrum([level_one, scaled_one])
    sign = choose(jnp.float32(1.0), jnp.float32(-1.0))
    chain, shape_grad = to_signal(
        [
            times(
                choose_spectrum(level_spec, first_spec),
                choose_spectrum(filter_two, filter_one),
                sign,
            ),
            times(
                choose_spectrum(second_spec, first_spec),
                choose_spectrum(level_spec, value_spec),
                -1.0,
            ),
        ]
    )
    source = choose(level_one, scaled_one)
    chain = scale * (chain + choose(skip_two, skip_one) * source)
    gate_grad = scale * (level_grad * carry_one)
    partner = choose(scaled_two, value)
    skip_grad = jnp.sum(jnp.sum(source * partner, 0, keepdims=True), 1, keepdims=True)
    high, low = split(skip_grad)
    mid = low.astype(F32)
    low = skip_grad - high.astype(F32) - mid
    high = high.astype(F32)
    skip_row = jnp.where(
        lane == 0, high, jnp.where(lane == 1, mid, jnp.where(lane == 2, low, 0.0))
    )
    for at, values in enumerate([chain, shape_grad, gate_grad]):
        packed[pl.ds(2 * at, SEQ, stride=BACK_ROWS), :] = values[:, :128]
        packed[pl.ds(2 * at + 1, SEQ, stride=BACK_ROWS), :] = values[:, 128:]
    packed[pl.ds(6, SEQ, stride=BACK_ROWS), :] = jnp.broadcast_to(skip_row, (SEQ, 128))
    packed[pl.ds(7, SEQ, stride=BACK_ROWS), :] = jnp.zeros((SEQ, 128), F32)
    back[...] = packed[...].astype(BF16)


def back_kernel(
    received, full, in_proj, out_proj, gate_in, grad_in, hidden, window,
    partial, weights, skip_out, scratch,
):
    scratch[...] = received[...].astype(F32)

    def plane(role, row):
        return scratch[pl.ds(role * LOCAL * BACK_ROWS + row, LOCAL, stride=BACK_ROWS), :]

    def signal(role, at):
        return jnp.concatenate([plane(role, 2 * at), plane(role, 2 * at + 1)], 1)

    carry = signal(0, 0)
    gated = (gate_in[...] * carry).astype(BF16)
    scaled_grad = jnp.concatenate(
        [signal(1, 0).astype(BF16), signal(1, 2).astype(BF16), (grad_in[...] * carry).astype(BF16)],
        0,
    )
    inputs = jnp.concatenate([full[128 * j : 128 * j + 64, :] for j in range(4)], 0)
    cotangent = jnp.concatenate([full[128 * j + 64 : 128 * j + 128, :] for j in range(4)], 0)
    mixed = dot(out_proj[...], gated).astype(BF16)
    grad_inputs = dot(in_proj[...], scaled_grad, ((0,), (0,))).astype(BF16)
    for j in range(4):
        partial[128 * j : 128 * j + 64, :] = mixed[64 * j : 64 * j + 64, :]
        partial[128 * j + 64 : 128 * j + 128, :] = grad_inputs[64 * j : 64 * j + 64, :]
    last = ((1,), (1,))
    in_weight = dot(scaled_grad, inputs, last)
    empty = jnp.zeros((LOCAL, CHUNK), BF16)
    out_weight = dot(cotangent, jnp.concatenate([gated, empty], 0), last)
    shape_grads = jnp.concatenate([signal(1, 1), signal(0, 1)], 0) * window[...]
    padded = jnp.concatenate([hidden[...], jnp.zeros((LOCAL, CHUNK), F32)], 0)
    filter_grad = dot(shape_grads, padded, last, HIGHEST)
    for at in range(24):
        for half in range(2):
            weights[2 * at + half] = in_weight[
                8 * at : 8 * at + 8, 128 * half : 128 * half + 128
            ].astype(BF16)
    for at in range(32):
        weights[48 + at] = out_weight[8 * at : 8 * at + 8, :].astype(BF16)
    for at in range(16):
        weights[80 + at] = filter_grad[8 * at : 8 * at + 8, :].astype(BF16)
    for at in range(96, 128):
        weights[at] = jnp.zeros((8, 128), BF16)
    lane = lax.broadcasted_iota(jnp.int32, (8, 128), 1)
    pick = jnp.where(lane < 3, 1.0, 0.0).astype(BF16)
    for role in range(2):
        total = dot(pick, plane(role, 6).astype(BF16), last)[:1, :]
        skip_out[1 - role : 2 - role, :] = total * TOTAL ** (-0.5)


def sum_kernel(received, spread):
    total = jnp.sum(received[...].astype(F32), 0, keepdims=True) * TOTAL ** (-0.5)
    spread[...] = jnp.broadcast_to(total, (SEQ, 8, 128)).astype(BF16)


def last_kernel(received, in_weight, out_weight, filter_grad):
    for at in range(24):
        for half in range(2):
            in_weight[8 * at : 8 * at + 8, 128 * half : 128 * half + 128] = received[
                2 * at + half
            ].astype(F32)
    for at in range(32):
        out_weight[8 * at : 8 * at + 8, :] = received[48 + at].astype(F32)[:, :LOCAL]
    for at in range(16):
        filter_grad[8 * at : 8 * at + 8, :] = received[80 + at].astype(F32)[:, :HIDDEN]


def call(kernel, name, outs, scalars, arrays, scratch=()):
    def vmem():
        return pl.BlockSpec(memory_space=pltpu.VMEM)

    return pl.pallas_call(
        kernel,
        name=name,
        out_shape=[jax.ShapeDtypeStruct(shape, kind) for shape, kind in outs],
        in_specs=[pl.BlockSpec(memory_space=pltpu.SMEM)] * scalars + [vmem() for _ in range(arrays)],
        out_specs=[vmem() for _ in outs],
        scratch_shapes=[pltpu.VMEM(shape, F32) for shape in scratch],
        compiler_params=pltpu.CompilerParams(vmem_limit_bytes=32 * 1024 * 1024),
    )


def front():
    return call(
        front_kernel,
        "project",
        [
            ((SEQ * SEND_ROWS, 128), BF16),
            ((LOCAL, CHUNK), F32),
            ((LOCAL, CHUNK), F32),
            ((HIDDEN, CHUNK), F32),
            ((2 * LOCAL, CHUNK), F32),
        ],
        3,
        6,
        [(LOCAL * SEND_ROWS, 128)],
    )


def series():
    return call(
        series_kernel,
        "convolve",
        [((SEQ * BACK_ROWS, 128), BF16)],
        4,
        9,
        [(SEQ * SEND_ROWS, 128), (SEQ * BACK_ROWS, 128)],
    )


def rear():
    return call(
        back_kernel,
        "weigh",
        [((4 * 128, CHUNK), BF16), ((SEQ, 8, 128), BF16), ((2, LOCAL), F32)],
        0,
        8,
        [(SEQ * BACK_ROWS, 128)],
    )


def total():
    return call(sum_kernel, "add_up", [((SEQ, 8, 128), BF16)], 0, 1)


def finish():
    return call(
        last_kernel,
        "unpack",
        [((3 * LOCAL, WIDTH), F32), ((WIDTH, LOCAL), F32), ((2 * LOCAL, HIDDEN), F32)],
        0,
        1,
    )


def swap(values):
    return lax.all_to_all(values, "seq", split_axis=0, concat_axis=0, tiled=True)


def shards(
    inputs,
    clip_len,
    clip_order,
    in_proj,
    out_proj,
    filt_in,
    filt_out,
    decay_rate,
    skip_gain,
    cotangent,
):
    rank = lax.axis_index("seq").astype(jnp.int32).reshape(1)
    in_rows = in_proj.reshape(3 * LOCAL, WIDTH)
    full = lax.all_gather(jnp.concatenate([inputs, cotangent], 0), "ch", axis=0, tiled=True)
    send, gate_two, out_grad, hidden, window = front()(
        rank, clip_len, clip_order, full, in_rows, out_proj, filt_in,
        filt_out.reshape(2 * LOCAL, HIDDEN), decay_rate,
    )
    received = swap(send.reshape(SEQ, SEND_ROWS, 128)).reshape(SEQ * SEND_ROWS, 128)
    (back,) = series()(
        rank, clip_len, clip_order, skip_gain, received, *[jnp.asarray(x) for x in tables()]
    )
    returned = swap(back.reshape(SEQ, BACK_ROWS, 128)).reshape(SEQ * BACK_ROWS, 128)
    partial, weights, grad_skip = rear()(
        returned, full, in_rows, out_proj, gate_two, out_grad, hidden, window
    )
    rows = lax.psum_scatter(partial, "ch", scatter_dimension=0, tiled=True)
    (spread,) = total()(swap(weights))
    in_weight, out_weight, filter_grad = finish()(swap(spread))
    return (
        rows[:64],
        rows[64:],
        in_weight.reshape(3, LOCAL, WIDTH),
        out_weight,
        filter_grad.reshape(2, LOCAL, HIDDEN),
        grad_skip,
    )


def solution(mesh):
    return jax.shard_map(
        shards,
        mesh=mesh,
        in_specs=(
            P("ch", "seq"),
            P(),
            P(),
            P(None, "ch", None),
            P(None, "ch"),
            P(),
            P(None, "ch", None),
            P(None, "ch"),
            P(None, "ch"),
            P("ch", "seq"),
        ),
        out_specs=(
            P("ch", "seq"),
            P("ch", "seq"),
            P(None, "ch", None),
            P(None, "ch"),
            P(None, "ch", None),
            P(None, "ch"),
        ),
        check_vma=False,
    )
```

time: 2050 us -> 152 us (0.07)
  the two profiles are of different devices: /device:TPU:32 before, /device:TPU:1 now
where the time goes in v1:
time: 152 us; the launch traced here: 151 us
  blocking collectives  66.5 us (44%)
  waiting for transfers between devices  40.8 us (27%)
  between operations  14.3 us (9%)
  starting transfers between devices  13.7 us (9%)
  Pallas kernels  11.6 us (8%)
  local copies, waits for them, and re-layouts  4.34 us (3%)
    all_to_all x2, blocking collectives, swap(): lax.all_to_all(values, 'seq', split_axis=0, concat_axis=0, tiled=True)  50 us
    reduce_scatter x1, waiting for transfers between devices, shards(): rows = lax.psum_scatter(partial, 'ch', scatter_dimension=0, tiled=True)  28.9 us
    all_gather x1, blocking collectives, shards(): lax.all_gather(jnp.concatenate([inputs, cotangent], 0), 'ch', axis=0, til...  16.5 us
    all_to_all x2, starting transfers between devices, swap(): lax.all_to_all(values, 'seq', split_axis=0, concat_axis=0, tiled=True)  13.7 us
    all_to_all x2, waiting for transfers between devices, swap(): lax.all_to_all(values, 'seq', split_axis=0, concat_axis=0, tiled=True)  11.3 us
    pallas_call x1, Pallas kernels, shards(): series()  7.1 us
  transfers between devices with their start and end apart: 3, of which 2 were waited for; matrix products, arithmetic and copies ran while one was open for 1% of the time, Pallas kernels for 1%

profile of v1, /device:TPU:1, one launch (start us, length us, event | category | flops | bytes accessed | tf_op | source)
XLA Modules:
  0.0 151.3 jit_solution(11697556784283086565)
XLA Ops:
  7.2 0.9 copy.24.out_proj
  8.2 16.5 %all_gather.3.full = bf16[512,256]{1,0:T(8,128)(2,1)S(1)} all-gather(bf16[128,256]{1,0:T(8,128)(2,1)S(1)} %pad_maximum_fusion), channel_id=1, replica_groups=mesh['seq'=128,'ch'=4] {'ch'}, dimensions={0}, use_global_device_ids=true | all-gather | bytes 327680 | tf_op jit(solution)/shard_map/all_gather | solution.py:432
  24.7 0.6 copy-done.11
  25.4 0.0 copy-done.12
  25.4 1.8 %project.1 = (bf16[2048,128]{1,0:T(8,128)(2,1)S(1)}, f32[64,256]{1,0:T(8,128)S(1)}, f32[64,256]{1,0:T(8,128)S(1)}, f32[64,256]{1,0:T(8,128)S(1)}, f32[128,256]{1,0:T(8,128)S(1)}) custom-call(s32[1]{0:T(128)} %bitcast.rank, s32[16]{0:T(128)S(1)} %copy-done.11, s32[16]{0:T(128)S(1)} %copy-done.12, bf16[512,256]{1,0:T(8,128)(2,1)S(1)} %all_gather.3.full, ...), custom_call_target="tpu_custom_call" | custom-call | tf_op jit(solution)/shard_map/project/pallas_call | solution.py:433
  27.2 0.0 copy-start.1
  27.2 0.0 copy-start.3
  27.2 0.0 copy-start.4
  27.2 0.0 copy-start.6
  27.3 31.3 %all_to_all.20 = bf16[128,16,128]{2,1,0:T(8,128)(2,1)S(1)} all-to-all(bf16[128,16,128]{2,1,0:T(8,128)(2,1)S(1)} %bitcast.12), channel_id=1, replica_groups=mesh['seq'=128,'ch'=4] {'seq'}, dimensions={0} | all-to-all | bytes 1048576 | tf_op jit(solution)/shard_map/all_to_all | solution.py:415
  58.6 0.6 copy-done.13
  59.2 7.1 %convolve.1 = bf16[1024,128]{1,0:T(8,128)(2,1)S(1)} custom-call(s32[1]{0:T(128)} %bitcast.rank, s32[16]{0:T(128)S(1)} %copy-done.11, s32[16]{0:T(128)S(1)} %copy-done.12, f32[2,64]{1,0:T(2,128)S(1)} %copy-done.13, bf16[2048,128]{1,0:T(8,128)(2,1)S(1)} %bitcast.9, bf16[256,128]{1,0:T(8,128)(2,1)S(1)} %copy-done.9, bf16[256,128]{1,0:T(8,128)(2,1)S(1)} %copy-done.8, ...), custom_call_target="tpu_custom_call" | custom-call | tf_op jit(solution)/shard_map/convolve/pallas_call | solution.py:438
  66.3 18.7 %all_to_all.21 = bf16[128,8,128]{2,1,0:T(8,128)(2,1)S(1)} all-to-all(bf16[128,8,128]{2,1,0:T(8,128)(2,1)S(1)} %bitcast.10), channel_id=1, replica_groups=mesh['seq'=128,'ch'=4] {'seq'}, dimensions={0} | all-to-all | bytes 524288 | tf_op jit(solution)/shard_map/all_to_all | solution.py:415
  85.0 1.1 weigh.1
  86.2 7.5 %all-to-all-start.2 = ((bf16[128,8,128]{2,1,0:T(8,128)(2,1)}), bf16[128,8,128]{2,1,0:T(8,128)(2,1)S(1)}, u32[]{:S(2)}, u32[]{:S(2)}) async-start(bf16[128,8,128]{2,1,0:T(8,128)(2,1)} %get-tuple-element.23), calls=%async_computation.3 | async-start | bytes 524288 | tf_op jit(solution)/shard_map/all_to_all | solution.py:415
  93.7 0.0 reduce-scatter.2.cloned.1.call-start
  93.8 0.7 reduce-scatter.2.cloned.1.call-update
  94.5 11.3 %all-to-all-done.2.received = bf16[128,8,128]{2,1,0:T(8,128)(2,1)S(1)} async-done(((bf16[128,8,128]{2,1,0:T(8,128)(2,1)}), bf16[128,8,128]{2,1,0:T(8,128)(2,1)S(1)}, u32[]{:S(2)}, u32[]{:S(2)}) %all-to-all-start.2) | async-done | bytes 262176 | tf_op jit(solution)/shard_map/all_to_all | solution.py:415
  105.7 0.9 add_up.1
  106.6 6.1 %all-to-all-start.3 = ((bf16[128,8,128]{2,1,0:T(8,128)(2,1)}), bf16[128,8,128]{2,1,0:T(8,128)(2,1)S(1)}, u32[]{:S(2)}, u32[]{:S(2)}) async-start(bf16[128,8,128]{2,1,0:T(8,128)(2,1)} %add_up.1), calls=%async_computation.4 | async-start | bytes 524288 | tf_op jit(solution)/shard_map/all_to_all | solution.py:415
  112.8 28.9 %reduce-scatter.2.cloned.1.call-done = bf16[128,256]{1,0:T(8,128)(2,1)} async-done(((bf16[512,256]{1,0:T(8,128)(2,1)}), bf16[128,256]{1,0:T(8,128)(2,1)}) %reduce-scatter.2.cloned.1.call-update) | async-done | bytes 65552 | tf_op jit(solution)/shard_map/reduce_scatter | solution.py:445
  141.6 1.4 fusion
  143.0 0.7 unpack.1
  143.7 0.7 copy.26
  (29 shorter events, 0.1 us)
Async XLA Ops:
  7.2 0.9 copy-start.15
  7.2 0.9 copy-start.16
  8.1 16.6 %copy-start = (bf16[3,64,256]{2,1,0:T(8,128)(2,1)S(1)}, bf16[3,64,256]{2,1,0:T(8,128)(2,1)}, u32[]{:S(2)}) copy-start(bf16[3,64,256]{2,1,0:T(8,128)(2,1)} %param.21) | copy-start | bytes 294916
  8.1 16.6 %copy-start.5 = (f32[2,64,64]{2,1,0:T(8,128)S(1)}, f32[2,64,64]{2,1,0:T(8,128)}, u32[]{:S(2)}) copy-start(f32[2,64,64]{2,1,0:T(8,128)} %param.24) | copy-start | bytes 98308
  8.1 16.6 %copy-start.10 = (f32[33,64]{1,0:T(8,128)S(1)}, f32[33,64]{1,0:T(8,128)}, u32[]{:S(2)}) copy-start(f32[33,64]{1,0:T(8,128)} %filt_in.1) | copy-start | bytes 25348
  8.1 16.6 %copy-start.14 = (f32[2,64]{1,0:T(2,128)S(1)}, f32[2,64]{1,0:T(2,128)}, u32[]{:S(2)}) copy-start(f32[2,64]{1,0:T(2,128)} %decay.1) | copy-start | bytes 1540
  24.7 0.7 copy-start.11
  24.7 0.7 copy-start.12
  27.2 31.4 %copy-start.1 = (bf16[256,512]{1,0:T(8,128)(2,1)S(1)}, bf16[256,512]{1,0:T(8,128)(2,1)}, u32[]{:S(2)}) copy-start(bf16[256,512]{1,0:T(8,128)(2,1)} %constant.27.clone.inner_low) | copy-start | bytes 786436
  27.2 31.4 %copy-start.2 = (bf16[256,512]{1,0:T(8,128)(2,1)S(1)}, bf16[256,512]{1,0:T(8,128)(2,1)}, u32[]{:S(2)}) copy-start(bf16[256,512]{1,0:T(8,128)(2,1)} %constant.26.clone.inner_high) | copy-start | bytes 786436
  27.2 31.3 %copy-start.3 = (f32[128,256]{1,0:T(8,128)S(1)}, f32[128,256]{1,0:T(8,128)}, u32[]{:S(2)}) copy-start(f32[128,256]{1,0:T(8,128)} %constant.29.clone.twist_sin) | copy-start | bytes 393220
  27.2 31.3 %copy-start.4 = (f32[128,256]{1,0:T(8,128)S(1)}, f32[128,256]{1,0:T(8,128)}, u32[]{:S(2)}) copy-start(f32[128,256]{1,0:T(8,128)} %constant.28.clone.twist_cos) | copy-start | bytes 393220
  27.2 31.3 %copy-start.6 = (bf16[128,256]{1,0:T(8,128)(2,1)S(1)}, bf16[128,256]{1,0:T(8,128)(2,1)}, u32[]{:S(2)}) copy-start(bf16[128,256]{1,0:T(8,128)(2,1)} %constant.25.clone.synthesis_low) | copy-start | bytes 196612
  27.3 31.3 %copy-start.7 = (bf16[128,256]{1,0:T(8,128)(2,1)S(1)}, bf16[128,256]{1,0:T(8,128)(2,1)}, u32[]{:S(2)}) copy-start(bf16[128,256]{1,0:T(8,128)(2,1)} %constant.24.clone.synthesis_high) | copy-start | bytes 196612
  27.3 31.3 %copy-start.8 = (bf16[256,128]{1,0:T(8,128)(2,1)S(1)}, bf16[256,128]{1,0:T(8,128)(2,1)}, u32[]{:S(2)}) copy-start(bf16[256,128]{1,0:T(8,128)(2,1)} %constant.23.clone.analysis_low) | copy-start | bytes 196612
  27.3 31.3 %copy-start.9 = (bf16[256,128]{1,0:T(8,128)(2,1)S(1)}, bf16[256,128]{1,0:T(8,128)(2,1)}, u32[]{:S(2)}) copy-start(bf16[256,128]{1,0:T(8,128)(2,1)} %constant.22.clone.analysis_high) | copy-start | bytes 196612
  58.6 0.7 copy-start.13
  86.2 19.6 %all-to-all-start.2 = ((bf16[128,8,128]{2,1,0:T(8,128)(2,1)}), bf16[128,8,128]{2,1,0:T(8,128)(2,1)S(1)}, u32[]{:S(2)}, u32[]{:S(2)}) async-start(bf16[128,8,128]{2,1,0:T(8,128)(2,1)} %get-tuple-element.23), calls=%async_computation.3 | async-start | bytes 524288 | tf_op jit(solution)/shard_map/all_to_all | solution.py:415
  93.7 47.9 %reduce-scatter.2.cloned.1.call-start = ((), (), s32[]{:S(2)}) async-start(), calls=%async_computation.5 | async-start | bytes 327680 | tf_op jit(solution)/shard_map/reduce_scatter | solution.py:445
  106.6 36.4 %all-to-all-start.3 = ((bf16[128,8,128]{2,1,0:T(8,128)(2,1)}), bf16[128,8,128]{2,1,0:T(8,128)(2,1)S(1)}, u32[]{:S(2)}, u32[]{:S(2)}) async-start(bf16[128,8,128]{2,1,0:T(8,128)(2,1)} %add_up.1), calls=%async_computation.4 | async-start | bytes 524288 | tf_op jit(solution)/shard_map/all_to_all | solution.py:415
Sparse Core Ops, SparseCore 0:
  97.6 44.0 reduce-scatter.1

commit v2 on v1

v2 whole, which is shorter than its diff:
```python
import functools
import math

import jax
import jax.numpy as jnp
import numpy as np
from jax import lax
from jax.experimental import pallas as pl
from jax.experimental.pallas import tpu as pltpu
from jax.sharding import PartitionSpec as P

EPSILON = 1e-05
HIGHEST = lax.Precision.HIGHEST
F32 = jnp.float32
BF16 = jnp.bfloat16

WIDTH = 256
TOTAL = 32768
SEQ = 128
CHUNK = 256
LOCAL = 64
HIDDEN = 64
BANDS = 16
CLIPS = 16
SHAPE_ROWS = 4
SEND_ROWS = 8
BACK_ROWS = 8


def halves(table):
    high = table.astype(BF16)
    low = (table - high.astype(np.float32)).astype(BF16)
    return high, low


def tables():
    k1 = np.arange(SEQ)[:, None] + 0.25
    s = np.arange(SEQ)[None, :]
    u = np.arange(CHUNK)[None, :]
    first = 2.0 * np.pi * k1 * s / SEQ
    analysis = np.concatenate([np.cos(first), -np.sin(first)], 0).astype(np.float32)
    synthesis = (np.concatenate([np.cos(first), -np.sin(first)], 0).T / TOTAL).astype(np.float32)
    twist = 2.0 * np.pi * k1 * u / TOTAL
    k2 = np.arange(CHUNK)
    second = 2.0 * np.pi * ((k2[:, None] * k2[None, :]) % CHUNK) / CHUNK
    inner = np.concatenate([np.cos(second), np.sin(second)], 1).astype(np.float32)
    return (
        *halves(analysis),
        *halves(synthesis),
        *halves(inner),
        np.cos(twist).astype(np.float32),
        np.sin(twist).astype(np.float32),
    )


def dot(a, b, dims=((1,), (0,)), precision=None):
    return lax.dot_general(a, b, (dims, ((), ())), precision=precision, preferred_element_type=F32)


def split(x):
    high = x.astype(BF16)
    return high, (x - high.astype(F32)).astype(BF16)


def clip_bounds(clip_len, clip_order):
    starts, lengths = [], []
    start = jnp.int32(0)
    for p in range(CLIPS):
        length = clip_len[clip_order[p]]
        starts.append(start)
        lengths.append(length)
        start = start + length
    return starts, lengths


def shape_kernel(rank, filt_in, filt_out, decay, send, hidden_out, window_out, scratch):
    offset = rank[0] * CHUNK
    step = offset + lax.broadcasted_iota(jnp.int32, (BANDS, CHUNK), 1)
    band = 1 + lax.broadcasted_iota(jnp.int32, (BANDS, CHUNK), 0)
    phases = ((step * band) & (TOTAL - 1)).astype(F32) * (2.0 * math.pi / TOTAL)
    ramp = (offset + lax.broadcasted_iota(jnp.int32, (8, CHUNK), 1)).astype(F32) * (1.0 / TOTAL)
    first_row = lax.broadcasted_iota(jnp.int32, (8, HIDDEN), 0) == 0
    ramp_weight = jnp.where(first_row, filt_in[:8, :], 0.0)
    first = ((0,), (0,))
    hidden = jnp.sin(
        dot(ramp_weight, ramp, first, HIGHEST)
        + dot(filt_in[1 : 1 + BANDS, :], jnp.cos(phases), first, HIGHEST)
        + dot(filt_in[1 + BANDS : 1 + 2 * BANDS, :], jnp.sin(phases), first, HIGHEST)
    )
    hidden_out[...] = hidden
    rows = lax.broadcasted_iota(jnp.int32, (LOCAL, LOCAL), 0)
    columns = lax.broadcasted_iota(jnp.int32, (LOCAL, LOCAL), 1)
    for i in range(2):
        spread = jnp.broadcast_to(decay[i : i + 1, :], (LOCAL, LOCAL))
        rate = jnp.sum(jnp.where(rows == columns, spread, 0.0), 1, keepdims=True)
        window = jnp.exp(-rate * ramp[:1, :]) * TOTAL ** (-0.5)
        window_out[i * LOCAL : (i + 1) * LOCAL, :] = window
        weights = filt_out[i * LOCAL : (i + 1) * LOCAL, :]
        shape = dot(weights, hidden, precision=HIGHEST) * window
        scratch[pl.ds(2 * i, LOCAL, stride=SHAPE_ROWS), :] = shape[:, :128]
        scratch[pl.ds(2 * i + 1, LOCAL, stride=SHAPE_ROWS), :] = shape[:, 128:]
    packed = scratch[...].astype(BF16)
    send[: LOCAL * SHAPE_ROWS, :] = packed
    send[LOCAL * SHAPE_ROWS :, :] = packed


def front_kernel(
    rank, clip_len, clip_order, full, in_proj, out_proj, send, gate_out, grad_out, scratch
):
    inputs = jnp.concatenate([full[128 * j : 128 * j + 64, :] for j in range(4)], 0)
    cotangent = jnp.concatenate([full[128 * j + 64 : 128 * j + 128, :] for j in range(4)], 0)
    raw = dot(in_proj[...], inputs)
    out_grad = dot(out_proj[...], cotangent)
    gate_two = raw[2 * LOCAL :, :]
    gate_out[...] = gate_two
    grad_out[...] = out_grad

    offset = rank[0] * CHUNK
    starts, lengths = clip_bounds(clip_len, clip_order)
    time = offset + lax.broadcasted_iota(jnp.int32, (SEQ, CHUNK), 1)
    place = lax.broadcasted_iota(jnp.int32, (SEQ, CHUNK), 0)
    member = jnp.zeros((SEQ, CHUNK), F32)
    for p in range(CLIPS):
        inside = (time >= starts[p]) & (time < starts[p] + lengths[p]) & (place == p)
        member = jnp.where(inside, 1.0, member)
    wide = inputs.astype(F32)
    squares = jnp.sum(wide * wide, 0, keepdims=True)
    power = dot(jnp.broadcast_to(squares, (8, CHUNK)), member, ((1,), (1,)), HIGHEST)[:1, :]
    high, low = split(power)

    arrays = [raw[:LOCAL, :], raw[LOCAL : 2 * LOCAL, :], gate_two * out_grad]
    for at, values in enumerate(arrays):
        scratch[pl.ds(2 * at, LOCAL, stride=SEND_ROWS), :] = values[:, :128]
        scratch[pl.ds(2 * at + 1, LOCAL, stride=SEND_ROWS), :] = values[:, 128:]
    for at, values in enumerate([high, low]):
        scratch[pl.ds(6 + at, LOCAL, stride=SEND_ROWS), :] = jnp.broadcast_to(
            values.astype(F32), (LOCAL, 128)
        )
    packed = scratch[...].astype(BF16)
    send[: LOCAL * SEND_ROWS, :] = packed
    send[LOCAL * SEND_ROWS :, :] = packed


def turn(values, count, inner_high, inner_low):
    high, low = split(values)
    product = dot(high, inner_high[...]) + dot(low, inner_high[...]) + dot(high, inner_low[...])
    pieces = []
    for at in range(count):
        real = product[256 * at : 256 * at + 128, :]
        imag = product[256 * at + 128 : 256 * at + 256, :]
        pieces.append((real[:, :256], real[:, 256:], imag[:, :256], imag[:, 256:]))
    return pieces


def to_spectrum(signals, cosines, sines, analysis_high, analysis_low, inner_high, inner_low):
    high, low = split(jnp.concatenate(signals, 1))
    rows = (
        dot(analysis_high[...], high)
        + dot(analysis_high[...], low)
        + dot(analysis_low[...], high)
    )
    twisted = []
    for at in range(len(signals)):
        real = rows[:128, 256 * at : 256 * at + 256]
        imag = rows[128:, 256 * at : 256 * at + 256]
        twisted.append(cosines * real + sines * imag)
        twisted.append(cosines * imag - sines * real)
    pieces = turn(jnp.concatenate(twisted, 0), len(signals), inner_high, inner_low)
    return [(rc + is_, ic - rs) for rc, rs, ic, is_ in pieces]


def to_signal(spectra, cosines, sines, synthesis_high, synthesis_low, inner_high, inner_low):
    stacked = jnp.concatenate([part for pair in spectra for part in pair], 0)
    columns = []
    for rc, rs, ic, is_ in turn(stacked, len(spectra), inner_high, inner_low):
        real = rc - is_
        imag = ic + rs
        columns.append(
            jnp.concatenate([cosines * real - sines * imag, cosines * imag + sines * real], 0)
        )
    high, low = split(jnp.concatenate(columns, 1))
    rows = (
        dot(synthesis_high[...], high)
        + dot(synthesis_high[...], low)
        + dot(synthesis_low[...], high)
    )
    return [rows[:, 256 * at : 256 * at + 256] for at in range(len(spectra))]


def filter_kernel(
    received, analysis_high, analysis_low, inner_high, inner_low, twist_cos, twist_sin,
    spectra, scratch,
):
    scratch[...] = received[...].astype(F32)

    def signal(at):
        return jnp.concatenate(
            [scratch[pl.ds(2 * at + half, SEQ, stride=SHAPE_ROWS), :] for half in range(2)], 1
        )

    filters = to_spectrum(
        [signal(0), signal(1)],
        twist_cos[...], twist_sin[...], analysis_high, analysis_low, inner_high, inner_low,
    )
    for at, (real, imag) in enumerate(filters):
        spectra[256 * at : 256 * at + 128, :] = real
        spectra[256 * at + 128 : 256 * at + 256, :] = imag


def series_kernel(
    rank, clip_len, clip_order, skip_gain, received, spectra,
    analysis_high, analysis_low, synthesis_high, synthesis_low, inner_high, inner_low,
    twist_cos, twist_sin, back, scratch, packed,
):
    role = rank[0] // LOCAL
    channel = rank[0] % LOCAL
    forward = role == 0
    skip_one = skip_gain[0, channel]
    skip_two = skip_gain[1, channel]
    scratch[...] = received[...].astype(F32)

    def plane(row):
        return scratch[pl.ds(row, SEQ, stride=SEND_ROWS), :]

    def signal(at):
        return jnp.concatenate([plane(2 * at), plane(2 * at + 1)], 1)

    power = jnp.sum(plane(6) + plane(7), 0, keepdims=True)
    starts, lengths = clip_bounds(clip_len, clip_order)
    time = lax.broadcasted_iota(jnp.int32, (SEQ, CHUNK), 0) * CHUNK + lax.broadcasted_iota(
        jnp.int32, (SEQ, CHUNK), 1
    )
    lane = lax.broadcasted_iota(jnp.int32, (1, 128), 1)
    counts = jnp.ones((1, 128), F32)
    for p in range(CLIPS):
        counts = jnp.where(lane == p, lengths[p].astype(F32), counts)
    inverse_rms = lax.rsqrt(power / (WIDTH * counts) + EPSILON)
    scale = jnp.zeros((SEQ, CHUNK), F32)
    for p in range(CLIPS):
        scale = jnp.where(time >= starts[p], inverse_rms[:, p : p + 1], scale)

    cosines = twist_cos[...]
    sines = twist_sin[...]

    def analyse(signals):
        return to_spectrum(
            signals, cosines, sines, analysis_high, analysis_low, inner_high, inner_low
        )

    def synthesise(parts):
        return to_signal(
            parts, cosines, sines, synthesis_high, synthesis_low, inner_high, inner_low
        )

    def times(a, b, sign):
        return (a[0] * b[0] - sign * (a[1] * b[1]), a[1] * b[0] + sign * (a[0] * b[1]))

    def choose(a, b):
        return jnp.where(forward, a, b)

    def choose_spectrum(a, b):
        return tuple(choose(x, y) for x, y in zip(a, b))

    value = signal(0) * scale
    gate_one = signal(1) * scale
    scaled_two = signal(2) * scale
    filter_one, filter_two = [
        (spectra[256 * at : 256 * at + 128, :], spectra[256 * at + 128 : 256 * at + 256, :])
        for at in range(2)
    ]
    value_spec, second_spec = analyse([value, scaled_two])
    carry_one, level_grad = synthesise(
        [times(value_spec, filter_one, 1.0), times(second_spec, filter_two, -1.0)]
    )
    carry_one = carry_one + skip_one * value
    level_grad = level_grad + skip_two * scaled_two
    level_one = gate_one * carry_one
    scaled_one = gate_one * level_grad
    level_spec, first_spec = analyse([level_one, scaled_one])
    sign = choose(jnp.float32(1.0), jnp.float32(-1.0))
    chain, shape_grad = synthesise(
        [
            times(
                choose_spectrum(level_spec, first_spec),
                choose_spectrum(filter_two, filter_one),
                sign,
            ),
            times(
                choose_spectrum(second_spec, first_spec),
                choose_spectrum(level_spec, value_spec),
                -1.0,
            ),
        ]
    )
    source = choose(level_one, scaled_one)
    chain = scale * (chain + choose(skip_two, skip_one) * source)
    gate_grad = scale * (level_grad * carry_one)
    partner = choose(scaled_two, value)
    skip_grad = jnp.sum(jnp.sum(source * partner, 0, keepdims=True), 1, keepdims=True)
    high, low = split(skip_grad)
    mid = low.astype(F32)
    low = skip_grad - high.astype(F32) - mid
    high = high.astype(F32)
    skip_row = jnp.where(
        lane == 0, high, jnp.where(lane == 1, mid, jnp.where(lane == 2, low, 0.0))
    )
    for at, values in enumerate([chain, shape_grad, gate_grad]):
        packed[pl.ds(2 * at, SEQ, stride=BACK_ROWS), :] = values[:, :128]
        packed[pl.ds(2 * at + 1, SEQ, stride=BACK_ROWS), :] = values[:, 128:]
    packed[pl.ds(6, SEQ, stride=BACK_ROWS), :] = jnp.broadcast_to(skip_row, (SEQ, 128))
    packed[pl.ds(7, SEQ, stride=BACK_ROWS), :] = jnp.zeros((SEQ, 128), F32)
    back[...] = packed[...].astype(BF16)


def back_kernel(
    place, received, full, in_proj, out_proj, gate_in, grad_in, hidden, window,
    given, kept, weights, skip_out, scratch,
):
    scratch[...] = received[...].astype(F32)

    def plane(role, row):
        return scratch[pl.ds(role * LOCAL * BACK_ROWS + row, LOCAL, stride=BACK_ROWS), :]

    def signal(role, at):
        return jnp.concatenate([plane(role, 2 * at), plane(role, 2 * at + 1)], 1)

    carry = signal(0, 0)
    gated = (gate_in[...] * carry).astype(BF16)
    scaled_grad = jnp.concatenate(
        [signal(1, 0).astype(BF16), signal(1, 2).astype(BF16), (grad_in[...] * carry).astype(BF16)],
        0,
    )
    inputs = jnp.concatenate([full[128 * j : 128 * j + 64, :] for j in range(4)], 0)
    cotangent = jnp.concatenate([full[128 * j + 64 : 128 * j + 128, :] for j in range(4)], 0)
    first = ((0,), (0,))
    last = ((1,), (1,))
    mixed = dot(out_proj[...], gated, first)
    grad_inputs = dot(in_proj[...], scaled_grad, first)
    even = place[0] % 2 == 0
    for at in range(2):
        for to, values in enumerate([mixed, grad_inputs]):
            low = values[128 * at : 128 * at + 64, :]
            high = values[128 * at + 64 : 128 * at + 128, :]
            rows = slice(128 * at + 64 * to, 128 * at + 64 * to + 64)
            given[rows, :] = jnp.where(even, high, low).astype(BF16)
            kept[rows, :] = jnp.where(even, low, high)
    in_weight = dot(scaled_grad, inputs, last)
    out_weight = dot(gated, cotangent, last)
    shape_grads = jnp.concatenate([signal(1, 1), signal(0, 1)], 0) * window[...]
    padded = jnp.concatenate([hidden[...], jnp.zeros((LOCAL, CHUNK), F32)], 0)
    filter_grad = dot(shape_grads, padded, last, HIGHEST)
    for at in range(32):
        source, row = (in_weight, at) if at < 24 else (out_weight, at - 24)
        for half in range(2):
            weights[2 * at + half] = source[
                8 * row : 8 * row + 8, 128 * half : 128 * half + 128
            ].astype(BF16)
    for at in range(16):
        weights[64 + at] = filter_grad[8 * at : 8 * at + 8, :].astype(BF16)
    for at in range(80, 128):
        weights[at] = jnp.zeros((8, 128), BF16)
    lane = lax.broadcasted_iota(jnp.int32, (8, 128), 1)
    pick = jnp.where(lane < 3, 1.0, 0.0).astype(BF16)
    for role in range(2):
        total = dot(pick, plane(role, 6).astype(BF16), last)[:1, :]
        skip_out[1 - role : 2 - role, :] = total * TOTAL ** (-0.5)


def core_kernel(place, received, kept, given, left):
    total = kept[...] + received[...].astype(F32)
    near = place[0] < 2
    given[...] = jnp.where(near, total[128:, :], total[:128, :]).astype(BF16)
    left[...] = jnp.where(near, total[:128, :], total[128:, :])


def chip_kernel(received, left, mixed, grad_inputs):
    total = (left[...] + received[...].astype(F32)).astype(BF16)
    mixed[...] = total[:64, :]
    grad_inputs[...] = total[64:, :]


def sum_kernel(received, spread):
    total = jnp.sum(received[...].astype(F32), 0, keepdims=True) * TOTAL ** (-0.5)
    spread[...] = jnp.broadcast_to(total, (SEQ, 8, 128)).astype(BF16)


def last_kernel(received, in_weight, out_weight, filter_grad):
    for at in range(32):
        target, row = (in_weight, at) if at < 24 else (out_weight, at - 24)
        for half in range(2):
            target[8 * row : 8 * row + 8, 128 * half : 128 * half + 128] = received[
                2 * at + half
            ].astype(F32)
    for at in range(16):
        filter_grad[8 * at : 8 * at + 8, :] = received[64 + at].astype(F32)[:, :HIDDEN]


def call(kernel, name, outs, scalars, arrays, scratch=()):
    def vmem():
        return pl.BlockSpec(memory_space=pltpu.VMEM)

    return pl.pallas_call(
        kernel,
        name=name,
        out_shape=[jax.ShapeDtypeStruct(shape, kind) for shape, kind in outs],
        in_specs=[pl.BlockSpec(memory_space=pltpu.SMEM)] * scalars + [vmem() for _ in range(arrays)],
        out_specs=[vmem() for _ in outs],
        scratch_shapes=[pltpu.VMEM(shape, F32) for shape in scratch],
        compiler_params=pltpu.CompilerParams(vmem_limit_bytes=32 * 1024 * 1024),
    )


def shaping():
    return call(
        shape_kernel,
        "shape",
        [
            ((SEQ * SHAPE_ROWS, 128), BF16),
            ((HIDDEN, CHUNK), F32),
            ((2 * LOCAL, CHUNK), F32),
        ],
        1,
        3,
        [(LOCAL * SHAPE_ROWS, 128)],
    )


def front():
    return call(
        front_kernel,
        "project",
        [((SEQ * SEND_ROWS, 128), BF16), ((LOCAL, CHUNK), F32), ((LOCAL, CHUNK), F32)],
        3,
        3,
        [(LOCAL * SEND_ROWS, 128)],
    )


def filters():
    return call(
        filter_kernel, "filters", [((512, CHUNK), F32)], 0, 7, [(SEQ * SHAPE_ROWS, 128)]
    )


def series():
    return call(
        series_kernel,
        "convolve",
        [((SEQ * BACK_ROWS, 128), BF16)],
        4,
        10,
        [(SEQ * SEND_ROWS, 128), (SEQ * BACK_ROWS, 128)],
    )


def rear():
    return call(
        back_kernel,
        "weigh",
        [
            ((256, CHUNK), BF16),
            ((256, CHUNK), F32),
            ((SEQ, 8, 128), BF16),
            ((2, LOCAL), F32),
        ],
        1,
        8,
        [(SEQ * BACK_ROWS, 128)],
    )


def core_sum():
    return call(core_kernel, "add_core", [((128, CHUNK), BF16), ((128, CHUNK), F32)], 1, 2)


def chip_sum():
    return call(chip_kernel, "add_chip", [((64, CHUNK), BF16), ((64, CHUNK), BF16)], 0, 2)


def total():
    return call(sum_kernel, "add_up", [((SEQ, 8, 128), BF16)], 0, 1)


def finish():
    return call(
        last_kernel,
        "unpack",
        [((3 * LOCAL, WIDTH), F32), ((LOCAL, WIDTH), F32), ((2 * LOCAL, HIDDEN), F32)],
        0,
        1,
    )


def swap(values):
    return lax.all_to_all(values, "seq", split_axis=0, concat_axis=0, tiled=True)


def shards(
    inputs,
    clip_len,
    clip_order,
    in_proj,
    out_proj,
    filt_in,
    filt_out,
    decay_rate,
    skip_gain,
    cotangent,
):
    rank = lax.axis_index("seq").astype(jnp.int32).reshape(1)
    place = lax.axis_index("ch").astype(jnp.int32).reshape(1)
    in_rows = in_proj.reshape(3 * LOCAL, WIDTH)
    out_rows = out_proj.T
    analysis_high, analysis_low, *rest = [jnp.asarray(x) for x in tables()]
    synthesis_high, synthesis_low, inner_high, inner_low, twist_cos, twist_sin = rest
    shapes, hidden, window = shaping()(
        rank, filt_in, filt_out.reshape(2 * LOCAL, HIDDEN), decay_rate
    )
    shapes = swap(shapes.reshape(SEQ, SHAPE_ROWS, 128)).reshape(SEQ * SHAPE_ROWS, 128)
    full = lax.all_gather(jnp.concatenate([inputs, cotangent], 0), "ch", axis=0, tiled=True)
    send, gate_two, out_grad = front()(rank, clip_len, clip_order, full, in_rows, out_rows)
    received = swap(send.reshape(SEQ, SEND_ROWS, 128)).reshape(SEQ * SEND_ROWS, 128)
    (spectra,) = filters()(
        shapes, analysis_high, analysis_low, inner_high, inner_low, twist_cos, twist_sin
    )
    (back,) = series()(
        rank, clip_len, clip_order, skip_gain, received, spectra,
        analysis_high, analysis_low, *rest,
    )
    returned = swap(back.reshape(SEQ, BACK_ROWS, 128)).reshape(SEQ * BACK_ROWS, 128)
    given, kept, weights, grad_skip = rear()(
        place, returned, full, in_rows, out_rows, gate_two, out_grad, hidden, window
    )
    over_cores = lax.ppermute(given, "ch", [(0, 1), (1, 0), (2, 3), (3, 2)])
    given, left = core_sum()(place, over_cores, kept)
    over_chips = lax.ppermute(given, "ch", [(0, 2), (2, 0), (1, 3), (3, 1)])
    mixed, grad_inputs = chip_sum()(over_chips, left)
    (spread,) = total()(swap(weights))
    in_weight, out_weight, filter_grad = finish()(swap(spread))
    return (
        mixed,
        grad_inputs,
        in_weight.reshape(3, LOCAL, WIDTH),
        out_weight.T,
        filter_grad.reshape(2, LOCAL, HIDDEN),
        grad_skip,
    )


def solution(mesh):
    return jax.shard_map(
        shards,
        mesh=mesh,
        in_specs=(
            P("ch", "seq"),
            P(),
            P(),
            P(None, "ch", None),
            P(None, "ch"),
            P(),
            P(None, "ch", None),
            P(None, "ch"),
            P(None, "ch"),
            P("ch", "seq"),
        ),
        out_specs=(
            P("ch", "seq"),
            P("ch", "seq"),
            P(None, "ch", None),
            P(None, "ch"),
            P(None, "ch", None),
            P(None, "ch"),
        ),
        check_vma=False,
    )
```

time: 152 us -> 134 us (0.88)
  starting transfers between devices: 13.7 us -> 55.8 us
  blocking collectives: 66.5 us -> 31.7 us
  between operations: 14.3 us -> 0.85 us
  waiting for transfers between devices: 40.8 us -> 27.8 us
  Pallas kernels: 11.6 us -> 13.7 us
    all_to_all x2 -> x1, blocking collectives: 50 us -> 18.9 us  [swap(): lax.all_to_all(values, 'seq', split_axis=0, concat_axis=0, tiled=True)]
    all_to_all x2 -> x4, starting transfers between devices: 13.7 us -> 43.6 us  [swap(): lax.all_to_all(values, 'seq', split_axis=0, concat_axis=0, tiled=True)]
    reduce_scatter x1 -> x0, waiting for transfers between devices: 28.9 us -> none  [shards(): rows = lax.psum_scatter(partial, 'ch', scatter_dimension=0, tiled=True)]
    all_to_all x2 -> x4, waiting for transfers between devices: 11.3 us -> 24.2 us  [swap(): lax.all_to_all(values, 'seq', split_axis=0, concat_axis=0, tiled=True)]
    ppermute x0 -> x2, starting transfers between devices: none -> 12.2 us  [the longest x1 6.59 us: shards(): over_chips = lax.ppermute(given, 'ch', [(0, 2), (2, 0), (1, 3), (3, 1)])]
    all_gather x1, blocking collectives: 16.5 us -> 12.8 us  [shards(): lax.all_gather(jnp.concatenate([inputs, cotangent], 0), 'ch', axis=0, til...]
    ppermute x0 -> x2, waiting for transfers between devices: none -> 3.67 us  [the longest x1 2.7 us: shards(): over_chips = lax.ppermute(given, 'ch', [(0, 2), (2, 0), (1, 3), (3, 1)])]
    pallas_call x1 -> x5, Pallas kernels: 1.81 us -> 4.75 us  [the longest x1 1.67 us: shards(): shaping()(rank, filt_in, filt_out.reshape(2 * LOCAL, HIDDEN), decay_rate)]
  transfers between devices with their start and end apart: 3 -> 6, of which waited for: 2 -> 4; matrix products, arithmetic and copies ran while one was open for 1% -> 0% of each run, Pallas kernels for 1% -> 2%
where the time goes in v2:
time: 134 us; the launch traced here: 133 us
  starting transfers between devices  55.8 us (42%)
  blocking collectives  31.7 us (24%)
  waiting for transfers between devices  27.8 us (21%)
  Pallas kernels  13.7 us (10%)
  local copies, waits for them, and re-layouts  2.96 us (2%)
    all_to_all x4, starting transfers between devices, swap(): lax.all_to_all(values, 'seq', split_axis=0, concat_axis=0, tiled=True)  43.6 us
    all_to_all x4, waiting for transfers between devices, swap(): lax.all_to_all(values, 'seq', split_axis=0, concat_axis=0, tiled=True)  24.2 us
    all_to_all x1, blocking collectives, swap(): lax.all_to_all(values, 'seq', split_axis=0, concat_axis=0, tiled=True)  18.9 us
    all_gather x1, blocking collectives, shards(): lax.all_gather(jnp.concatenate([inputs, cotangent], 0), 'ch', axis=0, til...  12.8 us
    ppermute x1, starting transfers between devices, shards(): over_chips = lax.ppermute(given, 'ch', [(0, 2), (2, 0), (1, 3), (3, 1)])  6.59 us
    pallas_call x1, Pallas kernels, shards(): series()  6.41 us
    ppermute x1, starting transfers between devices, shards(): over_cores = lax.ppermute(given, 'ch', [(0, 1), (1, 0), (2, 3), (3, 2)])  5.65 us
    unnamed x36, local copies, waits for them, and re-layouts  2.96 us
  transfers between devices with their start and end apart: 6, of which 4 were waited for; matrix products, arithmetic and copies ran while one was open for 0% of the time, Pallas kernels for 2%

profile of v2, /device:TPU:1, one launch (start us, length us, event | category | flops | bytes accessed | tf_op | source)
XLA Modules:
  0.0 132.9 jit_solution(17507415118365917774)
XLA Ops:
  0.6 0.7 copy-done.14
  1.3 0.8 copy-done.10
  2.2 0.7 copy-done.11
  2.9 1.7 %shape.1 = (bf16[512,128]{1,0:T(8,128)(2,1)}, f32[64,256]{1,0:T(8,128)S(1)}, f32[128,256]{1,0:T(8,128)S(1)}) custom-call(s32[1]{0:T(128)} %bitcast.1.rank, f32[33,64]{1,0:T(8,128)S(1)} %copy-done.11, f32[128,64]{1,0:T(8,128)S(1)} %bitcast.21, f32[2,64]{1,0:T(2,128)S(1)} %copy-done.14), custom_call_target="tpu_custom_call" | custom-call | tf_op jit(solution)/shard_map/shape/pallas_call | solution.py:516
  4.6 17.9 %all-to-all-start.1 = ((bf16[128,4,128]{2,1,0:T(4,128)(2,1)}), bf16[128,4,128]{2,1,0:T(4,128)(2,1)S(1)}, u32[]{:S(2)}, u32[]{:S(2)}) async-start(bf16[128,4,128]{2,1,0:T(4,128)(2,1)} %bitcast.7), calls=%async_computation.1 | async-start | bytes 262144 | tf_op jit(solution)/shard_map/all_to_all | solution.py:495
  22.5 12.8 %all_gather.3.full = bf16[512,256]{1,0:T(8,128)(2,1)S(1)} all-gather(bf16[128,256]{1,0:T(8,128)(2,1)S(1)} %pad_maximum_fusion), channel_id=1, replica_groups=mesh['seq'=128,'ch'=4] {'ch'}, dimensions={0}, use_global_device_ids=true | all-gather | bytes 327680 | tf_op jit(solution)/shard_map/all_gather | solution.py:520
  35.3 0.6 copy-done.12
  36.0 1.5 %project.1 = (bf16[1024,128]{1,0:T(8,128)(2,1)}, f32[64,256]{1,0:T(8,128)S(1)}, f32[64,256]{1,0:T(8,128)S(1)}) custom-call(s32[1]{0:T(128)} %bitcast.1.rank, s32[16]{0:T(128)S(1)} %copy-done.12, s32[16]{0:T(128)S(1)} %copy-done.13, bf16[512,256]{1,0:T(8,128)(2,1)S(1)} %all_gather.3.full, bf16[192,256]{1,0:T(8,128)(2,1)S(1)} %bitcast.17, ...), custom_call_target="tpu_custom_call" | custom-call | tf_op jit(solution)/shard_map/project/pallas_call | solution.py:521
  37.5 13.1 %all-to-all-start = ((bf16[128,8,128]{2,1,0:T(8,128)(2,1)}), bf16[128,8,128]{2,1,0:T(8,128)(2,1)S(1)}, u32[]{:S(2)}, u32[]{:S(2)}) async-start(bf16[128,8,128]{2,1,0:T(8,128)(2,1)} %bitcast.4), calls=%async_computation | async-start | bytes 524288 | tf_op jit(solution)/shard_map/all_to_all | solution.py:495
  50.7 0.9 filters.1.spectra
  51.7 12.3 %all-to-all-done = bf16[128,8,128]{2,1,0:T(8,128)(2,1)S(1)} async-done(((bf16[128,8,128]{2,1,0:T(8,128)(2,1)}), bf16[128,8,128]{2,1,0:T(8,128)(2,1)S(1)}, u32[]{:S(2)}, u32[]{:S(2)}) %all-to-all-start) | async-done | bytes 262176 | tf_op jit(solution)/shard_map/all_to_all | solution.py:495
  64.0 6.4 %convolve.1 = bf16[1024,128]{1,0:T(8,128)(2,1)} custom-call(s32[1]{0:T(128)} %bitcast.1.rank, s32[16]{0:T(128)S(1)} %copy-done.12, s32[16]{0:T(128)S(1)} %copy-done.13, f32[2,64]{1,0:T(2,128)S(1)} %copy-done.15, bf16[1024,128]{1,0:T(8,128)(2,1)S(1)} %bitcast.15, f32[512,256]{1,0:T(8,128)S(1)} %filters.1.spectra, bf16[256,128]{1,0:T(8,128)(2,1)S(1)} %copy-done.5, ...), custom_call_target="tpu_custom_call" | custom-call | tf_op jit(solution)/shard_map/convolve/pallas_call | solution.py:526
  70.4 6.4 %all-to-all-start.2 = ((bf16[128,8,128]{2,1,0:T(8,128)(2,1)}), bf16[128,8,128]{2,1,0:T(8,128)(2,1)S(1)}, u32[]{:S(2)}, u32[]{:S(2)}) async-start(bf16[128,8,128]{2,1,0:T(8,128)(2,1)} %bitcast.9), calls=%async_computation.2 | async-start | bytes 524288 | tf_op jit(solution)/shard_map/all_to_all | solution.py:495
  76.8 11.8 %all-to-all-done.2 = bf16[128,8,128]{2,1,0:T(8,128)(2,1)S(1)} async-done(((bf16[128,8,128]{2,1,0:T(8,128)(2,1)}), bf16[128,8,128]{2,1,0:T(8,128)(2,1)S(1)}, u32[]{:S(2)}, u32[]{:S(2)}) %all-to-all-start.2) | async-done | bytes 262176 | tf_op jit(solution)/shard_map/all_to_all | solution.py:495
  88.6 1.0 weigh.1
  89.6 18.9 %all_to_all.25.received = bf16[128,8,128]{2,1,0:T(8,128)(2,1)S(1)} all-to-all(bf16[128,8,128]{2,1,0:T(8,128)(2,1)S(1)} %get-tuple-element.35), channel_id=1, replica_groups=mesh['seq'=128,'ch'=4] {'seq'}, dimensions={0} | all-to-all | bytes 524288 | tf_op jit(solution)/shard_map/all_to_all | solution.py:495
  108.6 0.8 add_up.1
  109.4 6.2 %all-to-all-start.4 = ((bf16[128,8,128]{2,1,0:T(8,128)(2,1)}), bf16[128,8,128]{2,1,0:T(8,128)(2,1)S(1)}, u32[]{:S(2)}, u32[]{:S(2)}) async-start(bf16[128,8,128]{2,1,0:T(8,128)(2,1)} %add_up.1), calls=%async_computation.4 | async-start | bytes 524288 | tf_op jit(solution)/shard_map/all_to_all | solution.py:495
  115.6 5.6 %collective-permute-start = (bf16[256,256]{1,0:T(8,128)(2,1)S(1)}, bf16[256,256]{1,0:T(8,128)(2,1)S(1)}, u32[]{:S(2)}, u32[]{:S(2)}) collective-permute-start(bf16[256,256]{1,0:T(8,128)(2,1)S(1)} %get-tuple-element.29), channel_id=1, source_target_pairs={{0,1},{1,0},{2,3},{3,2},{4,5},{5,4},{6,7},{7,6},{8,9},{9,8},{10,11... | collective-permute-start | bytes 393224 | tf_op jit(solution)/shard_map/ppermute | solution.py:534
  121.2 1.0 collective-permute-done.received
  122.2 6.6 %collective-permute-start.1 = (bf16[128,256]{1,0:T(8,128)(2,1)S(1)}, bf16[128,256]{1,0:T(8,128)(2,1)S(1)}, u32[]{:S(2)}, u32[]{:S(2)}) collective-permute-start(bf16[128,256]{1,0:T(8,128)(2,1)S(1)} %get-tuple-element.31), channel_id=1, source_target_pairs={{0,2},{2,0},{1,3},{3,1},{4,6},{6,4},{5,7},{7,5},{8,10},{10,8},{9,1... | collective-permute-start | bytes 196616 | tf_op jit(solution)/shard_map/ppermute | solution.py:536
  128.8 2.7 %collective-permute-done.1.received = bf16[128,256]{1,0:T(8,128)(2,1)S(1)} collective-permute-done((bf16[128,256]{1,0:T(8,128)(2,1)S(1)}, bf16[128,256]{1,0:T(8,128)(2,1)S(1)}, u32[]{:S(2)}, u32[]{:S(2)}) %collective-permute-start.1) | collective-permute-done | bytes 65568 | tf_op jit(solution)/shard_map/ppermute | solution.py:536
  131.5 0.6 add_chip.1
  132.2 0.7 unpack.1
  (36 shorter events, 0.1 us)
Async XLA Ops:
  0.6 0.7 copy-start.14
  1.3 0.8 copy-start.10
  2.2 0.7 copy-start.11
  4.6 17.9 %copy-start.16 = (bf16[64,256]{1,0:T(8,128)(2,1)S(1)}, bf16[64,256]{1,0:T(8,128)(2,1)}, u32[]{:S(2)}) copy-start(bf16[64,256]{1,0:T(8,128)(2,1)} %param.27) | copy-start | bytes 98308
  4.6 17.9 %copy-start.17 = (bf16[64,256]{1,0:T(8,128)(2,1)S(1)}, bf16[64,256]{1,0:T(8,128)(2,1)}, u32[]{:S(2)}) copy-start(bf16[64,256]{1,0:T(8,128)(2,1)} %param.18) | copy-start | bytes 98308
  4.6 32.9 %all-to-all-start.1 = ((bf16[128,4,128]{2,1,0:T(4,128)(2,1)}), bf16[128,4,128]{2,1,0:T(4,128)(2,1)S(1)}, u32[]{:S(2)}, u32[]{:S(2)}) async-start(bf16[128,4,128]{2,1,0:T(4,128)(2,1)} %bitcast.7), calls=%async_computation.1 | async-start | bytes 262144 | tf_op jit(solution)/shard_map/all_to_all | solution.py:495
  22.5 12.8 %copy-start.4 = (bf16[3,64,256]{2,1,0:T(8,128)(2,1)S(1)}, bf16[3,64,256]{2,1,0:T(8,128)(2,1)}, u32[]{:S(2)}) copy-start(bf16[3,64,256]{2,1,0:T(8,128)(2,1)} %param.21) | copy-start | bytes 294916
  22.5 12.8 %copy-start.7 = (bf16[256,64]{0,1:T(8,128)(2,1)S(1)}, bf16[256,64]{0,1:T(8,128)(2,1)}, u32[]{:S(2)}) copy-start(bf16[256,64]{0,1:T(8,128)(2,1)} %param.22) | copy-start | bytes 98308
  35.3 0.7 copy-start.12
  35.3 0.7 copy-start.13
  36.0 14.6 %copy-start.2 = (f32[128,256]{1,0:T(8,128)S(1)}, f32[128,256]{1,0:T(8,128)}, u32[]{:S(2)}) copy-start(f32[128,256]{1,0:T(8,128)} %constant.31.clone.twist_cos) | copy-start | bytes 393220
  36.0 14.6 %copy-start.3 = (f32[128,256]{1,0:T(8,128)S(1)}, f32[128,256]{1,0:T(8,128)}, u32[]{:S(2)}) copy-start(f32[128,256]{1,0:T(8,128)} %constant.32.clone.twist_sin) | copy-start | bytes 393220
  36.0 14.6 %copy-start.5 = (bf16[256,128]{1,0:T(8,128)(2,1)S(1)}, bf16[256,128]{1,0:T(8,128)(2,1)}, u32[]{:S(2)}) copy-start(bf16[256,128]{1,0:T(8,128)(2,1)} %constant.25.clone.analysis_high) | copy-start | bytes 196612
  36.0 14.6 %copy-start.6 = (bf16[256,128]{1,0:T(8,128)(2,1)S(1)}, bf16[256,128]{1,0:T(8,128)(2,1)}, u32[]{:S(2)}) copy-start(bf16[256,128]{1,0:T(8,128)(2,1)} %constant.26.clone.analysis_low) | copy-start | bytes 196612
  37.5 13.2 %copy-start = (bf16[256,512]{1,0:T(8,128)(2,1)S(1)}, bf16[256,512]{1,0:T(8,128)(2,1)}, u32[]{:S(2)}) copy-start(bf16[256,512]{1,0:T(8,128)(2,1)} %constant.29.clone.inner_high) | copy-start | bytes 786436
  37.5 13.2 %copy-start.1 = (bf16[256,512]{1,0:T(8,128)(2,1)S(1)}, bf16[256,512]{1,0:T(8,128)(2,1)}, u32[]{:S(2)}) copy-start(bf16[256,512]{1,0:T(8,128)(2,1)} %constant.30.clone.inner_low) | copy-start | bytes 786436
  37.5 26.5 %all-to-all-start = ((bf16[128,8,128]{2,1,0:T(8,128)(2,1)}), bf16[128,8,128]{2,1,0:T(8,128)(2,1)S(1)}, u32[]{:S(2)}, u32[]{:S(2)}) async-start(bf16[128,8,128]{2,1,0:T(8,128)(2,1)} %bitcast.4), calls=%async_computation | async-start | bytes 524288 | tf_op jit(solution)/shard_map/all_to_all | solution.py:495
  50.7 13.3 %copy-start.8 = (bf16[128,256]{1,0:T(8,128)(2,1)S(1)}, bf16[128,256]{1,0:T(8,128)(2,1)}, u32[]{:S(2)}) copy-start(bf16[128,256]{1,0:T(8,128)(2,1)} %constant.27.clone.synthesis_high) | copy-start | bytes 196612
  50.7 13.3 %copy-start.9 = (bf16[128,256]{1,0:T(8,128)(2,1)S(1)}, bf16[128,256]{1,0:T(8,128)(2,1)}, u32[]{:S(2)}) copy-start(bf16[128,256]{1,0:T(8,128)(2,1)} %constant.28.clone.synthesis_low) | copy-start | bytes 196612
  51.6 12.4 %copy-start.15 = (f32[2,64]{1,0:T(2,128)S(1)}, f32[2,64]{1,0:T(2,128)}, u32[]{:S(2)}) copy-start(f32[2,64]{1,0:T(2,128)} %skip_gain.1) | copy-start | bytes 1540
  70.4 18.2 %all-to-all-start.2 = ((bf16[128,8,128]{2,1,0:T(8,128)(2,1)}), bf16[128,8,128]{2,1,0:T(8,128)(2,1)S(1)}, u32[]{:S(2)}, u32[]{:S(2)}) async-start(bf16[128,8,128]{2,1,0:T(8,128)(2,1)} %bitcast.9), calls=%async_computation.2 | async-start | bytes 524288 | tf_op jit(solution)/shard_map/all_to_all | solution.py:495
  109.4 22.8 %all-to-all-start.4 = ((bf16[128,8,128]{2,1,0:T(8,128)(2,1)}), bf16[128,8,128]{2,1,0:T(8,128)(2,1)S(1)}, u32[]{:S(2)}, u32[]{:S(2)}) async-start(bf16[128,8,128]{2,1,0:T(8,128)(2,1)} %add_up.1), calls=%async_computation.4 | async-start | bytes 524288 | tf_op jit(solution)/shard_map/all_to_all | solution.py:495
  115.6 6.6 %collective-permute-start = (bf16[256,256]{1,0:T(8,128)(2,1)S(1)}, bf16[256,256]{1,0:T(8,128)(2,1)S(1)}, u32[]{:S(2)}, u32[]{:S(2)}) collective-permute-start(bf16[256,256]{1,0:T(8,128)(2,1)S(1)} %get-tuple-element.29), channel_id=1, source_target_pairs={{0,1},{1,0},{2,3},{3,2},{4,5},{5,4},{6,7},{7,6},{8,9},{9,8},{10,11... | collective-permute-start | bytes 393224 | tf_op jit(solution)/shard_map/ppermute | solution.py:534
  122.2 9.3 %collective-permute-start.1 = (bf16[128,256]{1,0:T(8,128)(2,1)S(1)}, bf16[128,256]{1,0:T(8,128)(2,1)S(1)}, u32[]{:S(2)}, u32[]{:S(2)}) collective-permute-start(bf16[128,256]{1,0:T(8,128)(2,1)S(1)} %get-tuple-element.31), channel_id=1, source_target_pairs={{0,2},{2,0},{1,3},{3,1},{4,6},{6,4},{5,7},{7,5},{8,10},{10,8},{9,1... | collective-permute-start | bytes 196616 | tf_op jit(solution)/shard_map/ppermute | solution.py:536

commit v3 on v2

--- a/solution.py
+++ b/solution.py
@@ -22,8 +22,7 @@
 HIDDEN = 64
 BANDS = 16
 CLIPS = 16
-SHAPE_ROWS = 4
-SEND_ROWS = 8
+SEND_ROWS = 12
 BACK_ROWS = 8
 
 
@@ -73,40 +72,11 @@
     return starts, lengths
 
 
-def shape_kernel(rank, filt_in, filt_out, decay, send, hidden_out, window_out, scratch):
-    offset = rank[0] * CHUNK
-    step = offset + lax.broadcasted_iota(jnp.int32, (BANDS, CHUNK), 1)
-    band = 1 + lax.broadcasted_iota(jnp.int32, (BANDS, CHUNK), 0)
-    phases = ((step * band) & (TOTAL - 1)).astype(F32) * (2.0 * math.pi / TOTAL)
-    ramp = (offset + lax.broadcasted_iota(jnp.int32, (8, CHUNK), 1)).astype(F32) * (1.0 / TOTAL)
-    first_row = lax.broadcasted_iota(jnp.int32, (8, HIDDEN), 0) == 0
-    ramp_weight = jnp.where(first_row, filt_in[:8, :], 0.0)
+def front_kernel(
+    rank, clip_len, clip_order, full, in_proj, out_proj, filt_in, filt_out, decay,
+    send, gate_out, grad_out, hidden_out, window_out, scratch,
+):
     first = ((0,), (0,))
-    hidden = jnp.sin(
-        dot(ramp_weight, ramp, first, HIGHEST)
-        + dot(filt_in[1 : 1 + BANDS, :], jnp.cos(phases), first, HIGHEST)
-        + dot(filt_in[1 + BANDS : 1 + 2 * BANDS, :], jnp.sin(phases), first, HIGHEST)
-    )
-    hidden_out[...] = hidden
-    rows = lax.broadcasted_iota(jnp.int32, (LOCAL, LOCAL), 0)
-    columns = lax.broadcasted_iota(jnp.int32, (LOCAL, LOCAL), 1)
-    for i in range(2):
-        spread = jnp.broadcast_to(decay[i : i + 1, :], (LOCAL, LOCAL))
-        rate = jnp.sum(jnp.where(rows == columns, spread, 0.0), 1, keepdims=True)
-        window = jnp.exp(-rate * ramp[:1, :]) * TOTAL ** (-0.5)
-        window_out[i * LOCAL : (i + 1) * LOCAL, :] = window
-        weights = filt_out[i * LOCAL : (i + 1) * LOCAL, :]
-        shape = dot(weights, hidden, precision=HIGHEST) * window
-        scratch[pl.ds(2 * i, LOCAL, stride=SHAPE_ROWS), :] = shape[:, :128]
-        scratch[pl.ds(2 * i + 1, LOCAL, stride=SHAPE_ROWS), :] = shape[:, 128:]
-    packed = scratch[...].astype(BF16)
-    send[: LOCAL * SHAPE_ROWS, :] = packed
-    send[LOCAL * SHAPE_ROWS :, :] = packed
-
-
-def front_kernel(
-    rank, clip_len, clip_order, full, in_proj, out_proj, send, gate_out, grad_out, scratch
-):
     inputs = jnp.concatenate([full[128 * j : 128 * j + 64, :] for j in range(4)], 0)
     cotangent = jnp.concatenate([full[128 * j + 64 : 128 * j + 128, :] for j in range(4)], 0)
     raw = dot(in_proj[...], inputs)
@@ -128,12 +98,35 @@
     power = dot(jnp.broadcast_to(squares, (8, CHUNK)), member, ((1,), (1,)), HIGHEST)[:1, :]
     high, low = split(power)
 
-    arrays = [raw[:LOCAL, :], raw[LOCAL : 2 * LOCAL, :], gate_two * out_grad]
+    step = offset + lax.broadcasted_iota(jnp.int32, (BANDS, CHUNK), 1)
+    band = 1 + lax.broadcasted_iota(jnp.int32, (BANDS, CHUNK), 0)
+    phases = ((step * band) & (TOTAL - 1)).astype(F32) * (2.0 * math.pi / TOTAL)
+    ramp = (offset + lax.broadcasted_iota(jnp.int32, (8, CHUNK), 1)).astype(F32) * (1.0 / TOTAL)
+    first_row = lax.broadcasted_iota(jnp.int32, (8, HIDDEN), 0) == 0
+    ramp_weight = jnp.where(first_row, filt_in[:8, :], 0.0)
+    hidden = jnp.sin(
+        dot(ramp_weight, ramp, first, HIGHEST)
+        + dot(filt_in[1 : 1 + BANDS, :], jnp.cos(phases), first, HIGHEST)
+        + dot(filt_in[1 + BANDS : 1 + 2 * BANDS, :], jnp.sin(phases), first, HIGHEST)
+    )
+    hidden_out[...] = hidden
+    rows = lax.broadcasted_iota(jnp.int32, (LOCAL, LOCAL), 0)
+    columns = lax.broadcasted_iota(jnp.int32, (LOCAL, LOCAL), 1)
+    shapes = []
+    for i in range(2):
+        spread = jnp.broadcast_to(decay[i : i + 1, :], (LOCAL, LOCAL))
+        rate = jnp.sum(jnp.where(rows == columns, spread, 0.0), 1, keepdims=True)
+        window = jnp.exp(-rate * ramp[:1, :]) * TOTAL ** (-0.5)
+        window_out[i * LOCAL : (i + 1) * LOCAL, :] = window
+        weights = filt_out[i * LOCAL : (i + 1) * LOCAL, :]
+        shapes.append(dot(weights, hidden, precision=HIGHEST) * window)
+
+    arrays = [raw[:LOCAL, :], raw[LOCAL : 2 * LOCAL, :], gate_two * out_grad, *shapes]
     for at, values in enumerate(arrays):
         scratch[pl.ds(2 * at, LOCAL, stride=SEND_ROWS), :] = values[:, :128]
         scratch[pl.ds(2 * at + 1, LOCAL, stride=SEND_ROWS), :] = values[:, 128:]
     for at, values in enumerate([high, low]):
-        scratch[pl.ds(6 + at, LOCAL, stride=SEND_ROWS), :] = jnp.broadcast_to(
+        scratch[pl.ds(10 + at, LOCAL, stride=SEND_ROWS), :] = jnp.broadcast_to(
             values.astype(F32), (LOCAL, 128)
         )
     packed = scratch[...].astype(BF16)
@@ -187,28 +180,8 @@
     return [rows[:, 256 * at : 256 * at + 256] for at in range(len(spectra))]
 
 
-def filter_kernel(
-    received, analysis_high, analysis_low, inner_high, inner_low, twist_cos, twist_sin,
-    spectra, scratch,
-):
-    scratch[...] = received[...].astype(F32)
-
-    def signal(at):
-        return jnp.concatenate(
-            [scratch[pl.ds(2 * at + half, SEQ, stride=SHAPE_ROWS), :] for half in range(2)], 1
-        )
-
-    filters = to_spectrum(
-        [signal(0), signal(1)],
-        twist_cos[...], twist_sin[...], analysis_high, analysis_low, inner_high, inner_low,
-    )
-    for at, (real, imag) in enumerate(filters):
-        spectra[256 * at : 256 * at + 128, :] = real
-        spectra[256 * at + 128 : 256 * at + 256, :] = imag
-
-
 def series_kernel(
-    rank, clip_len, clip_order, skip_gain, received, spectra,
+    rank, clip_len, clip_order, skip_gain, received,
     analysis_high, analysis_low, synthesis_high, synthesis_low, inner_high, inner_low,
     twist_cos, twist_sin, back, scratch, packed,
 ):
@@ -225,7 +198,7 @@
     def signal(at):
         return jnp.concatenate([plane(2 * at), plane(2 * at + 1)], 1)
 
-    power = jnp.sum(plane(6) + plane(7), 0, keepdims=True)
+    power = jnp.sum(plane(10) + plane(11), 0, keepdims=True)
     starts, lengths = clip_bounds(clip_len, clip_order)
     time = lax.broadcasted_iota(jnp.int32, (SEQ, CHUNK), 0) * CHUNK + lax.broadcasted_iota(
         jnp.int32, (SEQ, CHUNK), 1
@@ -264,11 +237,9 @@
     value = signal(0) * scale
     gate_one = signal(1) * scale
     scaled_two = signal(2) * scale
-    filter_one, filter_two = [
-        (spectra[256 * at : 256 * at + 128, :], spectra[256 * at + 128 : 256 * at + 256, :])
-        for at in range(2)
-    ]
-    value_spec, second_spec = analyse([value, scaled_two])
+    value_spec, second_spec, filter_one, filter_two = analyse(
+        [value, scaled_two, signal(3), signal(4)]
+    )
     carry_one, level_grad = synthesise(
         [times(value_spec, filter_one, 1.0), times(second_spec, filter_two, -1.0)]
     )
@@ -410,35 +381,20 @@
     )
 
 
-def shaping():
-    return call(
-        shape_kernel,
-        "shape",
-        [
-            ((SEQ * SHAPE_ROWS, 128), BF16),
-            ((HIDDEN, CHUNK), F32),
-            ((2 * LOCAL, CHUNK), F32),
-        ],
-        1,
-        3,
-        [(LOCAL * SHAPE_ROWS, 128)],
-    )
-
-
 def front():
     return call(
         front_kernel,
         "project",
-        [((SEQ * SEND_ROWS, 128), BF16), ((LOCAL, CHUNK), F32), ((LOCAL, CHUNK), F32)],
+        [
+            ((SEQ * SEND_ROWS, 128), BF16),
+            ((LOCAL, CHUNK), F32),
+            ((LOCAL, CHUNK), F32),
+            ((HIDDEN, CHUNK), F32),
+            ((2 * LOCAL, CHUNK), F32),
+        ],
         3,
-        3,
+        6,
         [(LOCAL * SEND_ROWS, 128)],
-    )
-
-
-def filters():
-    return call(
-        filter_kernel, "filters", [((512, CHUNK), F32)], 0, 7, [(SEQ * SHAPE_ROWS, 128)]
     )
 
 
@@ -448,7 +404,7 @@
         "convolve",
         [((SEQ * BACK_ROWS, 128), BF16)],
         4,
-        10,
+        9,
         [(SEQ * SEND_ROWS, 128), (SEQ * BACK_ROWS, 128)],
     )
 
@@ -511,21 +467,14 @@
     place = lax.axis_index("ch").astype(jnp.int32).reshape(1)
     in_rows = in_proj.reshape(3 * LOCAL, WIDTH)
     out_rows = out_proj.T
-    analysis_high, analysis_low, *rest = [jnp.asarray(x) for x in tables()]
-    synthesis_high, synthesis_low, inner_high, inner_low, twist_cos, twist_sin = rest
-    shapes, hidden, window = shaping()(
-        rank, filt_in, filt_out.reshape(2 * LOCAL, HIDDEN), decay_rate
-    )
-    shapes = swap(shapes.reshape(SEQ, SHAPE_ROWS, 128)).reshape(SEQ * SHAPE_ROWS, 128)
     full = lax.all_gather(jnp.concatenate([inputs, cotangent], 0), "ch", axis=0, tiled=True)
-    send, gate_two, out_grad = front()(rank, clip_len, clip_order, full, in_rows, out_rows)
-    received = swap(send.reshape(SEQ, SEND_ROWS, 128)).reshape(SEQ * SEND_ROWS, 128)
-    (spectra,) = filters()(
-        shapes, analysis_high, analysis_low, inner_high, inner_low, twist_cos, twist_sin
-    )
+    send, gate_two, out_grad, hidden, window = front()(
+        rank, clip_len, clip_order, full, in_rows, out_rows, filt_in,
+        filt_out.reshape(2 * LOCAL, HIDDEN), decay_rate,
+    )
+    received = swap(send.reshape(SEQ * SEND_ROWS // 4, 4, 128)).reshape(SEQ * SEND_ROWS, 128)
     (back,) = series()(
-        rank, clip_len, clip_order, skip_gain, received, spectra,
-        analysis_high, analysis_low, *rest,
+        rank, clip_len, clip_order, skip_gain, received, *[jnp.asarray(x) for x in tables()]
     )
     returned = swap(back.reshape(SEQ, BACK_ROWS, 128)).reshape(SEQ * BACK_ROWS, 128)
     given, kept, weights, grad_skip = rear()(
@@ -533,9 +482,10 @@
     )
     over_cores = lax.ppermute(given, "ch", [(0, 1), (1, 0), (2, 3), (3, 2)])
     given, left = core_sum()(place, over_cores, kept)
+    (spread,) = total()(swap(weights))
+    spread, given = lax.optimization_barrier((spread, given))
     over_chips = lax.ppermute(given, "ch", [(0, 2), (2, 0), (1, 3), (3, 1)])
     mixed, grad_inputs = chip_sum()(over_chips, left)
-    (spread,) = total()(swap(weights))
     in_weight, out_weight, filter_grad = finish()(swap(spread))
     return (
         mixed,

time: 134 us -> 120 us (0.90)
  the two profiles are of different devices: /device:TPU:1 before, /device:TPU:8 now
where the time goes in v3:
time: 120 us; the launch traced here: 119 us
  blocking collectives  45.5 us (38%)
  waiting for transfers between devices  30.4 us (25%)
  starting transfers between devices  27.7 us (23%)
  Pallas kernels  12.8 us (11%)
  local copies, waits for them, and re-layouts  1.34 us (1%)
    all_to_all x1, blocking collectives, swap(): lax.all_to_all(values, 'seq', split_axis=0, concat_axis=0, tiled=True)  32 us
    all_to_all x3, waiting for transfers between devices, swap(): lax.all_to_all(values, 'seq', split_axis=0, concat_axis=0, tiled=True)  25.2 us
    all_to_all x3, starting transfers between devices, swap(): lax.all_to_all(values, 'seq', split_axis=0, concat_axis=0, tiled=True)  18.8 us
    all_gather x1, blocking collectives, shards(): lax.all_gather(jnp.concatenate([inputs, cotangent], 0), 'ch', axis=0, til...  13.5 us
    pallas_call x1, Pallas kernels, shards(): series()  7.71 us
    ppermute x1, starting transfers between devices, shards(): over_chips = lax.ppermute(given, 'ch', [(0, 2), (2, 0), (1, 3), (3, 1)])  6.98 us
    ppermute x1, waiting for transfers between devices, shards(): over_chips = lax.ppermute(given, 'ch', [(0, 2), (2, 0), (1, 3), (3, 1)])  3.92 us
  transfers between devices with their start and end apart: 5, of which 5 were waited for; matrix products, arithmetic and copies ran while one was open for 0% of the time, Pallas kernels for 1%

profile of v3, /device:TPU:8, one launch (start us, length us, event | category | flops | bytes accessed | tf_op | source)
XLA Modules:
  0.0 119.3 jit_solution(10517924622313770001)
XLA Ops:
  0.6 0.8 pad_maximum_fusion
  1.4 13.5 %all_gather.3.full = bf16[512,256]{1,0:T(8,128)(2,1)S(1)} all-gather(bf16[128,256]{1,0:T(8,128)(2,1)S(1)} %pad_maximum_fusion), channel_id=1, replica_groups=mesh['seq'=128,'ch'=4] {'ch'}, dimensions={0}, use_global_device_ids=true | all-gather | bytes 327680 | tf_op jit(solution)/shard_map/all_gather | solution.py:470
  15.0 0.6 copy-done.14
  15.6 0.0 copy-done.13
  15.6 0.0 copy-start.8
  15.7 0.0 copy-start.9
  15.7 1.7 %project.1 = (bf16[1536,128]{1,0:T(8,128)(2,1)S(1)}, f32[64,256]{1,0:T(8,128)S(1)}, f32[64,256]{1,0:T(8,128)S(1)}, f32[64,256]{1,0:T(8,128)S(1)}, f32[128,256]{1,0:T(8,128)S(1)}) custom-call(s32[1]{0:T(128)} %bitcast.1.rank, s32[16]{0:T(128)S(1)} %copy-done.12, s32[16]{0:T(128)S(1)} %copy-done.13, bf16[512,256]{1,0:T(8,128)(2,1)S(1)} %all_gather.3.full, ...), custom_call_target="tpu_custom_call" | custom-call | tf_op jit(solution)/shard_map/project/pallas_call | solution.py:471
  17.4 32.0 %all_to_all.20 = bf16[384,4,128]{2,1,0:T(4,128)(2,1)S(1)} all-to-all(bf16[384,4,128]{2,1,0:T(4,128)(2,1)S(1)} %bitcast.14), channel_id=1, replica_groups=mesh['seq'=128,'ch'=4] {'seq'}, dimensions={0} | all-to-all | bytes 786432 | tf_op jit(solution)/shard_map/all_to_all | solution.py:451
  49.5 0.6 copy-done.15
  50.1 7.7 %convolve.1 = bf16[1024,128]{1,0:T(8,128)(2,1)} custom-call(s32[1]{0:T(128)} %bitcast.1.rank, s32[16]{0:T(128)S(1)} %copy-done.12, s32[16]{0:T(128)S(1)} %copy-done.13, f32[2,64]{1,0:T(2,128)S(1)} %copy-done.15, bf16[1536,128]{1,0:T(8,128)(2,1)S(1)} %bitcast.12, bf16[256,128]{1,0:T(8,128)(2,1)S(1)} %copy-done.9, bf16[256,128]{1,0:T(8,128)(2,1)S(1)} %copy-done.8, ...), custom_call_target="tpu_custom_call" | custom-call | tf_op jit(solution)/shard_map/convolve/pallas_call | solution.py:476
  57.8 6.4 %all-to-all-start.1 = ((bf16[128,8,128]{2,1,0:T(8,128)(2,1)}), bf16[128,8,128]{2,1,0:T(8,128)(2,1)S(1)}, u32[]{:S(2)}, u32[]{:S(2)}) async-start(bf16[128,8,128]{2,1,0:T(8,128)(2,1)} %bitcast.7), calls=%async_computation.1 | async-start | bytes 524288 | tf_op jit(solution)/shard_map/all_to_all | solution.py:451
  64.2 13.7 %all-to-all-done.1 = bf16[128,8,128]{2,1,0:T(8,128)(2,1)S(1)} async-done(((bf16[128,8,128]{2,1,0:T(8,128)(2,1)}), bf16[128,8,128]{2,1,0:T(8,128)(2,1)S(1)}, u32[]{:S(2)}, u32[]{:S(2)}) %all-to-all-start.1) | async-done | bytes 262176 | tf_op jit(solution)/shard_map/all_to_all | solution.py:451
  77.8 1.1 weigh.1
  79.0 6.2 %all-to-all-start.2 = ((bf16[128,8,128]{2,1,0:T(8,128)(2,1)}), bf16[128,8,128]{2,1,0:T(8,128)(2,1)S(1)}, u32[]{:S(2)}, u32[]{:S(2)}) async-start(bf16[128,8,128]{2,1,0:T(8,128)(2,1)} %get-tuple-element.29), calls=%async_computation.2 | async-start | bytes 524288 | tf_op jit(solution)/shard_map/all_to_all | solution.py:451
  85.2 1.9 %collective-permute-start = (bf16[256,256]{1,0:T(8,128)(2,1)S(1)}, bf16[256,256]{1,0:T(8,128)(2,1)S(1)}, u32[]{:S(2)}, u32[]{:S(2)}) collective-permute-start(bf16[256,256]{1,0:T(8,128)(2,1)S(1)} %get-tuple-element.30), channel_id=1, source_target_pairs={{0,1},{1,0},{2,3},{3,2},{4,5},{5,4},{6,7},{7,6},{8,9},{9,8},{10,11... | collective-permute-start | bytes 393224 | tf_op jit(solution)/shard_map/ppermute | solution.py:483
  87.1 1.3 %collective-permute-done.received = bf16[256,256]{1,0:T(8,128)(2,1)S(1)} collective-permute-done((bf16[256,256]{1,0:T(8,128)(2,1)S(1)}, bf16[256,256]{1,0:T(8,128)(2,1)S(1)}, u32[]{:S(2)}, u32[]{:S(2)}) %collective-permute-start) | collective-permute-done | bytes 131104 | tf_op jit(solution)/shard_map/ppermute | solution.py:483
  88.5 9.9 %all-to-all-done.2.received = bf16[128,8,128]{2,1,0:T(8,128)(2,1)S(1)} async-done(((bf16[128,8,128]{2,1,0:T(8,128)(2,1)}), bf16[128,8,128]{2,1,0:T(8,128)(2,1)S(1)}, u32[]{:S(2)}, u32[]{:S(2)}) %all-to-all-start.2) | async-done | bytes 262176 | tf_op jit(solution)/shard_map/all_to_all | solution.py:451
  98.4 0.9 add_up.1
  99.2 6.2 %all-to-all-start.3 = ((bf16[128,8,128]{2,1,0:T(8,128)(2,1)}), bf16[128,8,128]{2,1,0:T(8,128)(2,1)S(1)}, u32[]{:S(2)}, u32[]{:S(2)}) async-start(bf16[128,8,128]{2,1,0:T(8,128)(2,1)} %add_up.1), calls=%async_computation.3 | async-start | bytes 524288 | tf_op jit(solution)/shard_map/all_to_all | solution.py:451
  105.4 7.0 %collective-permute-start.1 = (bf16[128,256]{1,0:T(8,128)(2,1)S(1)}, bf16[128,256]{1,0:T(8,128)(2,1)S(1)}, u32[]{:S(2)}, u32[]{:S(2)}) collective-permute-start(bf16[128,256]{1,0:T(8,128)(2,1)S(1)} %get-tuple-element.33), channel_id=1, source_target_pairs={{0,2},{2,0},{1,3},{3,1},{4,6},{6,4},{5,7},{7,5},{8,10},{10,8},{9,1... | collective-permute-start | bytes 196616 | tf_op jit(solution)/shard_map/ppermute | solution.py:487
  112.4 3.9 %collective-permute-done.1.received = bf16[128,256]{1,0:T(8,128)(2,1)S(1)} collective-permute-done((bf16[128,256]{1,0:T(8,128)(2,1)S(1)}, bf16[128,256]{1,0:T(8,128)(2,1)S(1)}, u32[]{:S(2)}, u32[]{:S(2)}) %collective-permute-start.1) | collective-permute-done | bytes 65568 | tf_op jit(solution)/shard_map/ppermute | solution.py:487
  116.3 0.6 add_chip.1
  117.0 1.7 %all-to-all-done.3.received = bf16[128,8,128]{2,1,0:T(8,128)(2,1)S(1)} async-done(((bf16[128,8,128]{2,1,0:T(8,128)(2,1)}), bf16[128,8,128]{2,1,0:T(8,128)(2,1)S(1)}, u32[]{:S(2)}, u32[]{:S(2)}) %all-to-all-start.3) | async-done | bytes 262176 | tf_op jit(solution)/shard_map/all_to_all | solution.py:451
  118.6 0.7 unpack.1
  (28 shorter events, 0.1 us)
Async XLA Ops:
  1.4 13.5 %copy-start = (bf16[3,64,256]{2,1,0:T(8,128)(2,1)S(1)}, bf16[3,64,256]{2,1,0:T(8,128)(2,1)}, u32[]{:S(2)}) copy-start(bf16[3,64,256]{2,1,0:T(8,128)(2,1)} %param.21) | copy-start | bytes 294916
  1.4 13.5 %copy-start.5 = (bf16[256,64]{0,1:T(8,128)(2,1)S(1)}, bf16[256,64]{0,1:T(8,128)(2,1)}, u32[]{:S(2)}) copy-start(bf16[256,64]{0,1:T(8,128)(2,1)} %param.22) | copy-start | bytes 98308
  1.4 13.5 %copy-start.10 = (f32[2,64,64]{2,1,0:T(8,128)S(1)}, f32[2,64,64]{2,1,0:T(8,128)}, u32[]{:S(2)}) copy-start(f32[2,64,64]{2,1,0:T(8,128)} %param.24) | copy-start | bytes 98308
  1.4 13.5 %copy-start.11 = (f32[33,64]{1,0:T(8,128)S(1)}, f32[33,64]{1,0:T(8,128)}, u32[]{:S(2)}) copy-start(f32[33,64]{1,0:T(8,128)} %filt_in.1) | copy-start | bytes 25348
  14.9 0.7 copy-start.14
  14.9 0.7 copy-start.12
  14.9 0.7 copy-start.13
  15.6 33.8 %copy-start.6 = (bf16[128,256]{1,0:T(8,128)(2,1)S(1)}, bf16[128,256]{1,0:T(8,128)(2,1)}, u32[]{:S(2)}) copy-start(bf16[128,256]{1,0:T(8,128)(2,1)} %constant.28.clone.synthesis_low) | copy-start | bytes 196612
  15.6 33.8 %copy-start.7 = (bf16[128,256]{1,0:T(8,128)(2,1)S(1)}, bf16[128,256]{1,0:T(8,128)(2,1)}, u32[]{:S(2)}) copy-start(bf16[128,256]{1,0:T(8,128)(2,1)} %constant.27.clone.synthesis_high) | copy-start | bytes 196612
  15.6 33.8 %copy-start.8 = (bf16[256,128]{1,0:T(8,128)(2,1)S(1)}, bf16[256,128]{1,0:T(8,128)(2,1)}, u32[]{:S(2)}) copy-start(bf16[256,128]{1,0:T(8,128)(2,1)} %constant.26.clone.analysis_low) | copy-start | bytes 196612
  15.7 33.8 %copy-start.9 = (bf16[256,128]{1,0:T(8,128)(2,1)S(1)}, bf16[256,128]{1,0:T(8,128)(2,1)}, u32[]{:S(2)}) copy-start(bf16[256,128]{1,0:T(8,128)(2,1)} %constant.25.clone.analysis_high) | copy-start | bytes 196612
  17.3 32.1 %copy-start.1 = (bf16[256,512]{1,0:T(8,128)(2,1)S(1)}, bf16[256,512]{1,0:T(8,128)(2,1)}, u32[]{:S(2)}) copy-start(bf16[256,512]{1,0:T(8,128)(2,1)} %constant.30.clone.inner_low) | copy-start | bytes 786436
  17.4 32.1 %copy-start.2 = (bf16[256,512]{1,0:T(8,128)(2,1)S(1)}, bf16[256,512]{1,0:T(8,128)(2,1)}, u32[]{:S(2)}) copy-start(bf16[256,512]{1,0:T(8,128)(2,1)} %constant.29.clone.inner_high) | copy-start | bytes 786436
  17.4 32.1 %copy-start.3 = (f32[128,256]{1,0:T(8,128)S(1)}, f32[128,256]{1,0:T(8,128)}, u32[]{:S(2)}) copy-start(f32[128,256]{1,0:T(8,128)} %constant.32.clone.twist_sin) | copy-start | bytes 393220
  17.4 32.1 %copy-start.4 = (f32[128,256]{1,0:T(8,128)S(1)}, f32[128,256]{1,0:T(8,128)}, u32[]{:S(2)}) copy-start(f32[128,256]{1,0:T(8,128)} %constant.31.clone.twist_cos) | copy-start | bytes 393220
  49.4 0.7 copy-start.15
  57.8 20.0 %all-to-all-start.1 = ((bf16[128,8,128]{2,1,0:T(8,128)(2,1)}), bf16[128,8,128]{2,1,0:T(8,128)(2,1)S(1)}, u32[]{:S(2)}, u32[]{:S(2)}) async-start(bf16[128,8,128]{2,1,0:T(8,128)(2,1)} %bitcast.7), calls=%async_computation.1 | async-start | bytes 524288 | tf_op jit(solution)/shard_map/all_to_all | solution.py:451
  79.0 19.4 %all-to-all-start.2 = ((bf16[128,8,128]{2,1,0:T(8,128)(2,1)}), bf16[128,8,128]{2,1,0:T(8,128)(2,1)S(1)}, u32[]{:S(2)}, u32[]{:S(2)}) async-start(bf16[128,8,128]{2,1,0:T(8,128)(2,1)} %get-tuple-element.29), calls=%async_computation.2 | async-start | bytes 524288 | tf_op jit(solution)/shard_map/all_to_all | solution.py:451
  85.2 3.2 %collective-permute-start = (bf16[256,256]{1,0:T(8,128)(2,1)S(1)}, bf16[256,256]{1,0:T(8,128)(2,1)S(1)}, u32[]{:S(2)}, u32[]{:S(2)}) collective-permute-start(bf16[256,256]{1,0:T(8,128)(2,1)S(1)} %get-tuple-element.30), channel_id=1, source_target_pairs={{0,1},{1,0},{2,3},{3,2},{4,5},{5,4},{6,7},{7,6},{8,9},{9,8},{10,11... | collective-permute-start | bytes 393224 | tf_op jit(solution)/shard_map/ppermute | solution.py:483
  99.2 19.4 %all-to-all-start.3 = ((bf16[128,8,128]{2,1,0:T(8,128)(2,1)}), bf16[128,8,128]{2,1,0:T(8,128)(2,1)S(1)}, u32[]{:S(2)}, u32[]{:S(2)}) async-start(bf16[128,8,128]{2,1,0:T(8,128)(2,1)} %add_up.1), calls=%async_computation.3 | async-start | bytes 524288 | tf_op jit(solution)/shard_map/all_to_all | solution.py:451
  105.4 10.9 %collective-permute-start.1 = (bf16[128,256]{1,0:T(8,128)(2,1)S(1)}, bf16[128,256]{1,0:T(8,128)(2,1)S(1)}, u32[]{:S(2)}, u32[]{:S(2)}) collective-permute-start(bf16[128,256]{1,0:T(8,128)(2,1)S(1)} %get-tuple-element.33), channel_id=1, source_target_pairs={{0,2},{2,0},{1,3},{3,1},{4,6},{6,4},{5,7},{7,5},{8,10},{10,8},{9,1... | collective-permute-start | bytes 196616 | tf_op jit(solution)/shard_map/ppermute | solution.py:487

commit v4 on v3

--- a/solution.py
+++ b/solution.py
@@ -23,13 +23,7 @@
 BANDS = 16
 CLIPS = 16
 SEND_ROWS = 12
-BACK_ROWS = 8
-
-
-def halves(table):
-    high = table.astype(BF16)
-    low = (table - high.astype(np.float32)).astype(BF16)
-    return high, low
+BACK_ROWS = 6
 
 
 def tables():
@@ -44,9 +38,9 @@
     second = 2.0 * np.pi * ((k2[:, None] * k2[None, :]) % CHUNK) / CHUNK
     inner = np.concatenate([np.cos(second), np.sin(second)], 1).astype(np.float32)
     return (
-        *halves(analysis),
-        *halves(synthesis),
-        *halves(inner),
+        analysis.astype(BF16),
+        synthesis.astype(BF16),
+        inner.astype(BF16),
         np.cos(twist).astype(np.float32),
         np.sin(twist).astype(np.float32),
     )
@@ -134,9 +128,8 @@
     send[LOCAL * SEND_ROWS :, :] = packed
 
 
-def turn(values, count, inner_high, inner_low):
-    high, low = split(values)
-    product = dot(high, inner_high[...]) + dot(low, inner_high[...]) + dot(high, inner_low[...])
+def turn(values, count, inner):
+    product = dot(values.astype(BF16), inner[...])
     pieces = []
     for at in range(count):
         real = product[256 * at : 256 * at + 128, :]
@@ -145,45 +138,34 @@
     return pieces
 
 
-def to_spectrum(signals, cosines, sines, analysis_high, analysis_low, inner_high, inner_low):
-    high, low = split(jnp.concatenate(signals, 1))
-    rows = (
-        dot(analysis_high[...], high)
-        + dot(analysis_high[...], low)
-        + dot(analysis_low[...], high)
-    )
+def to_spectrum(signals, cosines, sines, analysis, inner):
+    rows = dot(analysis[...], jnp.concatenate(signals, 1).astype(BF16))
     twisted = []
     for at in range(len(signals)):
         real = rows[:128, 256 * at : 256 * at + 256]
         imag = rows[128:, 256 * at : 256 * at + 256]
         twisted.append(cosines * real + sines * imag)
         twisted.append(cosines * imag - sines * real)
-    pieces = turn(jnp.concatenate(twisted, 0), len(signals), inner_high, inner_low)
+    pieces = turn(jnp.concatenate(twisted, 0), len(signals), inner)
     return [(rc + is_, ic - rs) for rc, rs, ic, is_ in pieces]
 
 
-def to_signal(spectra, cosines, sines, synthesis_high, synthesis_low, inner_high, inner_low):
+def to_signal(spectra, cosines, sines, synthesis, inner):
     stacked = jnp.concatenate([part for pair in spectra for part in pair], 0)
     columns = []
-    for rc, rs, ic, is_ in turn(stacked, len(spectra), inner_high, inner_low):
+    for rc, rs, ic, is_ in turn(stacked, len(spectra), inner):
         real = rc - is_
         imag = ic + rs
         columns.append(
             jnp.concatenate([cosines * real - sines * imag, cosines * imag + sines * real], 0)
         )
-    high, low = split(jnp.concatenate(columns, 1))
-    rows = (
-        dot(synthesis_high[...], high)
-        + dot(synthesis_high[...], low)
-        + dot(synthesis_low[...], high)
-    )
+    rows = dot(synthesis[...], jnp.concatenate(columns, 1).astype(BF16))
     return [rows[:, 256 * at : 256 * at + 256] for at in range(len(spectra))]
 
 
 def series_kernel(
     rank, clip_len, clip_order, skip_gain, received,
-    analysis_high, analysis_low, synthesis_high, synthesis_low, inner_high, inner_low,
-    twist_cos, twist_sin, back, scratch, packed,
+    analysis, synthesis, inner, twist_cos, twist_sin, back, scratch, packed,
 ):
     role = rank[0] // LOCAL
     channel = rank[0] % LOCAL
@@ -216,14 +198,10 @@
     sines = twist_sin[...]
 
     def analyse(signals):
-        return to_spectrum(
-            signals, cosines, sines, analysis_high, analysis_low, inner_high, inner_low
-        )
+        return to_spectrum(signals, cosines, sines, analysis, inner)
 
     def synthesise(parts):
-        return to_signal(
-            parts, cosines, sines, synthesis_high, synthesis_low, inner_high, inner_low
-        )
+        return to_signal(parts, cosines, sines, synthesis, inner)
 
     def times(a, b, sign):
         return (a[0] * b[0] - sign * (a[1] * b[1]), a[1] * b[0] + sign * (a[0] * b[1]))
@@ -275,17 +253,17 @@
     skip_row = jnp.where(
         lane == 0, high, jnp.where(lane == 1, mid, jnp.where(lane == 2, low, 0.0))
     )
-    for at, values in enumerate([chain, shape_grad, gate_grad]):
+    for at, values in enumerate([chain, shape_grad]):
         packed[pl.ds(2 * at, SEQ, stride=BACK_ROWS), :] = values[:, :128]
         packed[pl.ds(2 * at + 1, SEQ, stride=BACK_ROWS), :] = values[:, 128:]
-    packed[pl.ds(6, SEQ, stride=BACK_ROWS), :] = jnp.broadcast_to(skip_row, (SEQ, 128))
-    packed[pl.ds(7, SEQ, stride=BACK_ROWS), :] = jnp.zeros((SEQ, 128), F32)
+    packed[pl.ds(4, SEQ, stride=BACK_ROWS), :] = choose(gate_grad[:, :128], gate_grad[:, 128:])
+    packed[pl.ds(5, SEQ, stride=BACK_ROWS), :] = jnp.broadcast_to(skip_row, (SEQ, 128))
     back[...] = packed[...].astype(BF16)
 
 
 def back_kernel(
     place, received, full, in_proj, out_proj, gate_in, grad_in, hidden, window,
-    given, kept, weights, skip_out, scratch,
+    given, kept, weights, skip_out, scratch, packed,
 ):
     scratch[...] = received[...].astype(F32)
 
@@ -298,7 +276,11 @@
     carry = signal(0, 0)
     gated = (gate_in[...] * carry).astype(BF16)
     scaled_grad = jnp.concatenate(
-        [signal(1, 0).astype(BF16), signal(1, 2).astype(BF16), (grad_in[...] * carry).astype(BF16)],
+        [
+            signal(1, 0).astype(BF16),
+            jnp.concatenate([plane(0, 4), plane(1, 4)], 1).astype(BF16),
+            (grad_in[...] * carry).astype(BF16),
+        ],
         0,
     )
     inputs = jnp.concatenate([full[128 * j : 128 * j + 64, :] for j in range(4)], 0)
@@ -320,20 +302,21 @@
     shape_grads = jnp.concatenate([signal(1, 1), signal(0, 1)], 0) * window[...]
     padded = jnp.concatenate([hidden[...], jnp.zeros((LOCAL, CHUNK), F32)], 0)
     filter_grad = dot(shape_grads, padded, last, HIGHEST)
-    for at in range(32):
-        source, row = (in_weight, at) if at < 24 else (out_weight, at - 24)
-        for half in range(2):
-            weights[2 * at + half] = source[
-                8 * row : 8 * row + 8, 128 * half : 128 * half + 128
-            ].astype(BF16)
-    for at in range(16):
-        weights[64 + at] = filter_grad[8 * at : 8 * at + 8, :].astype(BF16)
-    for at in range(80, 128):
-        weights[at] = jnp.zeros((8, 128), BF16)
+    rows = [
+        in_weight[:128, :128],
+        jnp.concatenate([in_weight[128:, :128], in_weight[:64, 128:]], 0),
+        in_weight[64:, 128:],
+        jnp.concatenate([out_weight[:, :128], out_weight[:, 128:]], 0),
+        filter_grad,
+        jnp.zeros((SEQ, 128), F32),
+    ]
+    for at, values in enumerate(rows):
+        packed[pl.ds(at, SEQ, stride=BACK_ROWS), :] = values
+    weights[...] = packed[...].astype(BF16)
     lane = lax.broadcasted_iota(jnp.int32, (8, 128), 1)
     pick = jnp.where(lane < 3, 1.0, 0.0).astype(BF16)
     for role in range(2):
-        total = dot(pick, plane(role, 6).astype(BF16), last)[:1, :]
+        total = dot(pick, plane(role, 5).astype(BF16), last)[:1, :]
         skip_out[1 - role : 2 - role, :] = total * TOTAL ** (-0.5)
 
 
@@ -351,19 +334,24 @@
 
 
 def sum_kernel(received, spread):
-    total = jnp.sum(received[...].astype(F32), 0, keepdims=True) * TOTAL ** (-0.5)
-    spread[...] = jnp.broadcast_to(total, (SEQ, 8, 128)).astype(BF16)
-
-
-def last_kernel(received, in_weight, out_weight, filter_grad):
-    for at in range(32):
-        target, row = (in_weight, at) if at < 24 else (out_weight, at - 24)
-        for half in range(2):
-            target[8 * row : 8 * row + 8, 128 * half : 128 * half + 128] = received[
-                2 * at + half
-            ].astype(F32)
-    for at in range(16):
-        filter_grad[8 * at : 8 * at + 8, :] = received[64 + at].astype(F32)[:, :HIDDEN]
+    four = 4 * BACK_ROWS
+    parts = jnp.sum(received[...].astype(F32).reshape(SEQ // 4, four, 128), 0)
+    total = sum(parts[BACK_ROWS * at : BACK_ROWS * at + BACK_ROWS, :] for at in range(4))
+    total = jnp.concatenate([total * TOTAL ** (-0.5)] * 4, 0)
+    total = jnp.broadcast_to(total[None], (SEQ // 4, four, 128)).reshape(SEQ * BACK_ROWS, 128)
+    spread[...] = total.astype(BF16)
+
+
+def last_kernel(received, in_weight, out_weight, filter_grad, scratch):
+    scratch[...] = received[...].astype(F32)
+    rows = [scratch[pl.ds(at, SEQ, stride=BACK_ROWS), :] for at in range(5)]
+    in_weight[:128, :128] = rows[0]
+    in_weight[128:, :128] = rows[1][:64, :]
+    in_weight[:64, 128:] = rows[1][64:, :]
+    in_weight[64:, 128:] = rows[2]
+    out_weight[:, :128] = rows[3][:64, :]
+    out_weight[:, 128:] = rows[3][64:, :]
+    filter_grad[...] = rows[4][:, :HIDDEN]
 
 
 def call(kernel, name, outs, scalars, arrays, scratch=()):
@@ -404,7 +392,7 @@
         "convolve",
         [((SEQ * BACK_ROWS, 128), BF16)],
         4,
-        9,
+        6,
         [(SEQ * SEND_ROWS, 128), (SEQ * BACK_ROWS, 128)],
     )
 
@@ -416,12 +404,12 @@
         [
             ((256, CHUNK), BF16),
             ((256, CHUNK), F32),
-            ((SEQ, 8, 128), BF16),
+            ((SEQ * BACK_ROWS, 128), BF16),
             ((2, LOCAL), F32),
         ],
         1,
         8,
-        [(SEQ * BACK_ROWS, 128)],
+        [(SEQ * BACK_ROWS, 128), (SEQ * BACK_ROWS, 128)],
     )
 
 
@@ -434,7 +422,7 @@
 
 
 def total():
-    return call(sum_kernel, "add_up", [((SEQ, 8, 128), BF16)], 0, 1)
+    return call(sum_kernel, "add_up", [((SEQ * BACK_ROWS, 128), BF16)], 0, 1)
 
 
 def finish():
@@ -444,11 +432,14 @@
         [((3 * LOCAL, WIDTH), F32), ((LOCAL, WIDTH), F32), ((2 * LOCAL, HIDDEN), F32)],
         0,
         1,
-    )
-
-
-def swap(values):
-    return lax.all_to_all(values, "seq", split_axis=0, concat_axis=0, tiled=True)
+        [(SEQ * BACK_ROWS, 128)],
+    )
+
+
+def swap(values, group):
+    tiles = values.reshape(values.shape[0] // group, group, 128)
+    tiles = lax.all_to_all(tiles, "seq", split_axis=0, concat_axis=0, tiled=True)
+    return tiles.reshape(values.shape)
 
 
 def shards(
@@ -465,6 +456,7 @@
 ):
     rank = lax.axis_index("seq").astype(jnp.int32).reshape(1)
     place = lax.axis_index("ch").astype(jnp.int32).reshape(1)
+    rank, place = lax.optimization_barrier((rank, place))
     in_rows = in_proj.reshape(3 * LOCAL, WIDTH)
     out_rows = out_proj.T
     full = lax.all_gather(jnp.concatenate([inputs, cotangent], 0), "ch", axis=0, tiled=True)
@@ -472,21 +464,21 @@
         rank, clip_len, clip_order, full, in_rows, out_rows, filt_in,
         filt_out.reshape(2 * LOCAL, HIDDEN), decay_rate,
     )
-    received = swap(send.reshape(SEQ * SEND_ROWS // 4, 4, 128)).reshape(SEQ * SEND_ROWS, 128)
+    received = swap(send, 4)
     (back,) = series()(
         rank, clip_len, clip_order, skip_gain, received, *[jnp.asarray(x) for x in tables()]
     )
-    returned = swap(back.reshape(SEQ, BACK_ROWS, 128)).reshape(SEQ * BACK_ROWS, 128)
+    returned = swap(back, 2)
     given, kept, weights, grad_skip = rear()(
         place, returned, full, in_rows, out_rows, gate_two, out_grad, hidden, window
     )
     over_cores = lax.ppermute(given, "ch", [(0, 1), (1, 0), (2, 3), (3, 2)])
     given, left = core_sum()(place, over_cores, kept)
-    (spread,) = total()(swap(weights))
+    (spread,) = total()(swap(weights, 2))
     spread, given = lax.optimization_barrier((spread, given))
     over_chips = lax.ppermute(given, "ch", [(0, 2), (2, 0), (1, 3), (3, 1)])
     mixed, grad_inputs = chip_sum()(over_chips, left)
-    in_weight, out_weight, filter_grad = finish()(swap(spread))
+    in_weight, out_weight, filter_grad = finish()(swap(spread, 2))
     return (
         mixed,
         grad_inputs,

time: 120 us -> 113 us (0.942)
  blocking collectives: 45.5 us -> 64 us
  waiting for transfers between devices: 30.4 us -> 15.6 us
  starting transfers between devices: 27.7 us -> 21.3 us
  Pallas kernels: 12.8 us -> 8.23 us
    all_to_all x1 -> x2, blocking collectives: 32 us -> 50.5 us  [swap(): lax.all_to_all(tiles, 'seq', split_axis=0, concat_axis=0, tiled=True)]
    all_to_all x3 -> x2, waiting for transfers between devices: 25.2 us -> 10.6 us  [swap(): lax.all_to_all(tiles, 'seq', split_axis=0, concat_axis=0, tiled=True)]
    all_to_all x3 -> x2, starting transfers between devices: 18.8 us -> 12.5 us  [swap(): lax.all_to_all(tiles, 'seq', split_axis=0, concat_axis=0, tiled=True)]
    pallas_call x1, Pallas kernels: 7.71 us -> 3.28 us  [shards(): series()]
  transfers between devices with their start and end apart: 5 -> 4, of which waited for: 5 -> 4; matrix products, arithmetic and copies ran while one was open for 0% -> 0% of each run, Pallas kernels for 1% -> 1%
where the time goes in v4:
time: 113 us; the launch traced here: 112 us
  blocking collectives  64 us (57%)
  starting transfers between devices  21.3 us (19%)
  waiting for transfers between devices  15.6 us (14%)
  Pallas kernels  8.23 us (7%)
  local copies, waits for them, and re-layouts  1.34 us (1%)
    all_to_all x2, blocking collectives, swap(): lax.all_to_all(tiles, 'seq', split_axis=0, concat_axis=0, tiled=True)  50.5 us
    all_gather x1, blocking collectives, shards(): lax.all_gather(jnp.concatenate([inputs, cotangent], 0), 'ch', axis=0, til...  13.5 us
    all_to_all x2, starting transfers between devices, swap(): lax.all_to_all(tiles, 'seq', split_axis=0, concat_axis=0, tiled=True)  12.5 us
    all_to_all x2, waiting for transfers between devices, swap(): lax.all_to_all(tiles, 'seq', split_axis=0, concat_axis=0, tiled=True)  10.6 us
    ppermute x1, starting transfers between devices, shards(): over_chips = lax.ppermute(given, 'ch', [(0, 2), (2, 0), (1, 3), (3, 1)])  6.92 us
    ppermute x1, waiting for transfers between devices, shards(): over_chips = lax.ppermute(given, 'ch', [(0, 2), (2, 0), (1, 3), (3, 1)])  3.65 us
    pallas_call x1, Pallas kernels, shards(): series()  3.28 us
  transfers between devices with their start and end apart: 4, of which 4 were waited for; matrix products, arithmetic and copies ran while one was open for 0% of the time, Pallas kernels for 1%

profile of v4, /device:TPU:8, one launch (start us, length us, event | category | flops | bytes accessed | tf_op | source)
XLA Modules:
  0.0 112.1 jit_solution(1119177112555136540)
XLA Ops:
  0.6 0.8 pad_maximum_fusion
  1.5 13.5 %all_gather.3.full = bf16[512,256]{1,0:T(8,128)(2,1)S(1)} all-gather(bf16[128,256]{1,0:T(8,128)(2,1)S(1)} %pad_maximum_fusion), channel_id=1, replica_groups=mesh['seq'=128,'ch'=4] {'ch'}, dimensions={0}, use_global_device_ids=true | all-gather | bytes 327680 | tf_op jit(solution)/shard_map/all_gather | solution.py:462
  15.0 0.6 copy-done.9
  15.6 0.0 copy-done.10
  15.6 1.7 %project.1 = (bf16[1536,128]{1,0:T(8,128)(2,1)S(1)}, f32[64,256]{1,0:T(8,128)S(1)}, f32[64,256]{1,0:T(8,128)S(1)}, f32[64,256]{1,0:T(8,128)S(1)}, f32[128,256]{1,0:T(8,128)S(1)}) custom-call(s32[1]{0:T(128)} %bitcast.rank, s32[16]{0:T(128)S(1)} %copy-done.9, s32[16]{0:T(128)S(1)} %copy-done.10, bf16[512,256]{1,0:T(8,128)(2,1)S(1)} %all_gather.3.full, ...), custom_call_target="tpu_custom_call" | custom-call | tf_op jit(solution)/shard_map/project/pallas_call | solution.py:463
  17.3 0.0 copy-start.1
  17.3 0.0 copy-start.3
  17.3 0.0 copy-start.5
  17.4 32.0 %all_to_all.20 = bf16[384,4,128]{2,1,0:T(4,128)(2,1)S(1)} all-to-all(bf16[384,4,128]{2,1,0:T(4,128)(2,1)S(1)} %bitcast.21), channel_id=1, replica_groups=mesh['seq'=128,'ch'=4] {'seq'}, dimensions={0} | all-to-all | bytes 786432 | tf_op jit(solution)/shard_map/all_to_all | solution.py:441
  49.4 0.6 copy-done.12
  50.1 3.3 %convolve.1 = bf16[768,128]{1,0:T(8,128)(2,1)S(1)} custom-call(s32[1]{0:T(128)} %bitcast.rank, s32[16]{0:T(128)S(1)} %copy-done.9, s32[16]{0:T(128)S(1)} %copy-done.10, f32[2,64]{1,0:T(2,128)S(1)} %copy-done.12, bf16[1536,128]{1,0:T(8,128)(2,1)S(1)} %bitcast.16, bf16[256,128]{1,0:T(8,128)(2,1)S(1)} %copy-done.6, bf16[128,256]{1,0:T(8,128)(2,1)S(1)} %copy-done.5, ...), custom_call_target="tpu_custom_call" | custom-call | tf_op jit(solution)/shard_map/convolve/pallas_call | solution.py:468
  53.3 18.5 %all_to_all.21 = bf16[384,2,128]{2,1,0:T(2,128)(2,1)S(1)} all-to-all(bf16[384,2,128]{2,1,0:T(2,128)(2,1)S(1)} %bitcast.17), channel_id=1, replica_groups=mesh['seq'=128,'ch'=4] {'seq'}, dimensions={0} | all-to-all | bytes 393216 | tf_op jit(solution)/shard_map/all_to_all | solution.py:441
  71.9 1.1 weigh.1
  73.0 6.2 %all-to-all-start.2 = ((bf16[384,2,128]{2,1,0:T(2,128)(2,1)}), bf16[384,2,128]{2,1,0:T(2,128)(2,1)S(1)}, u32[]{:S(2)}, u32[]{:S(2)}) async-start(bf16[384,2,128]{2,1,0:T(2,128)(2,1)} %bitcast.9), calls=%async_computation.2 | async-start | bytes 393216 | tf_op jit(solution)/shard_map/all_to_all | solution.py:441
  79.2 1.9 %collective-permute-start = (bf16[256,256]{1,0:T(8,128)(2,1)S(1)}, bf16[256,256]{1,0:T(8,128)(2,1)S(1)}, u32[]{:S(2)}, u32[]{:S(2)}) collective-permute-start(bf16[256,256]{1,0:T(8,128)(2,1)S(1)} %get-tuple-element.34), channel_id=1, source_target_pairs={{0,1},{1,0},{2,3},{3,2},{4,5},{5,4},{6,7},{7,6},{8,9},{9,8},{10,11... | collective-permute-start | bytes 393224 | tf_op jit(solution)/shard_map/ppermute | solution.py:475
  81.1 1.3 %collective-permute-done.received = bf16[256,256]{1,0:T(8,128)(2,1)S(1)} collective-permute-done((bf16[256,256]{1,0:T(8,128)(2,1)S(1)}, bf16[256,256]{1,0:T(8,128)(2,1)S(1)}, u32[]{:S(2)}, u32[]{:S(2)}) %collective-permute-start) | collective-permute-done | bytes 131104 | tf_op jit(solution)/shard_map/ppermute | solution.py:475
  82.5 9.3 %all-to-all-done.2 = bf16[384,2,128]{2,1,0:T(2,128)(2,1)S(1)} async-done(((bf16[384,2,128]{2,1,0:T(2,128)(2,1)}), bf16[384,2,128]{2,1,0:T(2,128)(2,1)S(1)}, u32[]{:S(2)}, u32[]{:S(2)}) %all-to-all-start.2) | async-done | bytes 196640 | tf_op jit(solution)/shard_map/all_to_all | solution.py:441
  91.8 0.7 add_up.1
  92.5 6.3 %all-to-all-start.3 = ((bf16[384,2,128]{2,1,0:T(2,128)(2,1)}), bf16[384,2,128]{2,1,0:T(2,128)(2,1)S(1)}, u32[]{:S(2)}, u32[]{:S(2)}) async-start(bf16[384,2,128]{2,1,0:T(2,128)(2,1)} %bitcast.11), calls=%async_computation.3 | async-start | bytes 393216 | tf_op jit(solution)/shard_map/all_to_all | solution.py:441
  98.8 6.9 %collective-permute-start.1 = (bf16[128,256]{1,0:T(8,128)(2,1)S(1)}, bf16[128,256]{1,0:T(8,128)(2,1)S(1)}, u32[]{:S(2)}, u32[]{:S(2)}) collective-permute-start(bf16[128,256]{1,0:T(8,128)(2,1)S(1)} %get-tuple-element.37), channel_id=1, source_target_pairs={{0,2},{2,0},{1,3},{3,1},{4,6},{6,4},{5,7},{7,5},{8,10},{10,8},{9,1... | collective-permute-start | bytes 196616 | tf_op jit(solution)/shard_map/ppermute | solution.py:479
  105.7 3.7 %collective-permute-done.1.received = bf16[128,256]{1,0:T(8,128)(2,1)S(1)} collective-permute-done((bf16[128,256]{1,0:T(8,128)(2,1)S(1)}, bf16[128,256]{1,0:T(8,128)(2,1)S(1)}, u32[]{:S(2)}, u32[]{:S(2)}) %collective-permute-start.1) | collective-permute-done | bytes 65568 | tf_op jit(solution)/shard_map/ppermute | solution.py:479
  109.4 0.6 add_chip.1
  110.0 1.3 %all-to-all-done.3 = bf16[384,2,128]{2,1,0:T(2,128)(2,1)S(1)} async-done(((bf16[384,2,128]{2,1,0:T(2,128)(2,1)}), bf16[384,2,128]{2,1,0:T(2,128)(2,1)S(1)}, u32[]{:S(2)}, u32[]{:S(2)}) %all-to-all-start.3) | async-done | bytes 196640 | tf_op jit(solution)/shard_map/all_to_all | solution.py:441
  111.4 0.8 unpack.1
  (21 shorter events, 0.1 us)
Async XLA Ops:
  1.4 13.5 %copy-start = (bf16[3,64,256]{2,1,0:T(8,128)(2,1)S(1)}, bf16[3,64,256]{2,1,0:T(8,128)(2,1)}, u32[]{:S(2)}) copy-start(bf16[3,64,256]{2,1,0:T(8,128)(2,1)} %param.18) | copy-start | bytes 294916
  1.4 13.5 %copy-start.4 = (bf16[256,64]{0,1:T(8,128)(2,1)S(1)}, bf16[256,64]{0,1:T(8,128)(2,1)}, u32[]{:S(2)}) copy-start(bf16[256,64]{0,1:T(8,128)(2,1)} %param.19) | copy-start | bytes 98308
  1.4 13.5 %copy-start.7 = (f32[2,64,64]{2,1,0:T(8,128)S(1)}, f32[2,64,64]{2,1,0:T(8,128)}, u32[]{:S(2)}) copy-start(f32[2,64,64]{2,1,0:T(8,128)} %param.21) | copy-start | bytes 98308
  1.4 13.5 %copy-start.8 = (f32[33,64]{1,0:T(8,128)S(1)}, f32[33,64]{1,0:T(8,128)}, u32[]{:S(2)}) copy-start(f32[33,64]{1,0:T(8,128)} %filt_in.1) | copy-start | bytes 25348
  1.4 13.5 %copy-start.11 = (f32[2,64]{1,0:T(2,128)S(1)}, f32[2,64]{1,0:T(2,128)}, u32[]{:S(2)}) copy-start(f32[2,64]{1,0:T(2,128)} %decay.1) | copy-start | bytes 1540
  15.0 0.7 copy-start.9
  15.0 0.7 copy-start.10
  17.3 32.1 %copy-start.1 = (bf16[256,512]{1,0:T(8,128)(2,1)S(1)}, bf16[256,512]{1,0:T(8,128)(2,1)}, u32[]{:S(2)}) copy-start(bf16[256,512]{1,0:T(8,128)(2,1)} %constant.21.clone.inner) | copy-start | bytes 786436
  17.3 32.1 %copy-start.2 = (f32[128,256]{1,0:T(8,128)S(1)}, f32[128,256]{1,0:T(8,128)}, u32[]{:S(2)}) copy-start(f32[128,256]{1,0:T(8,128)} %constant.23.clone.twist_sin) | copy-start | bytes 393220
  17.3 32.1 %copy-start.3 = (f32[128,256]{1,0:T(8,128)S(1)}, f32[128,256]{1,0:T(8,128)}, u32[]{:S(2)}) copy-start(f32[128,256]{1,0:T(8,128)} %constant.22.clone.twist_cos) | copy-start | bytes 393220
  17.3 32.1 %copy-start.5 = (bf16[128,256]{1,0:T(8,128)(2,1)S(1)}, bf16[128,256]{1,0:T(8,128)(2,1)}, u32[]{:S(2)}) copy-start(bf16[128,256]{1,0:T(8,128)(2,1)} %constant.20.clone.synthesis) | copy-start | bytes 196612
  17.4 32.1 %copy-start.6 = (bf16[256,128]{1,0:T(8,128)(2,1)S(1)}, bf16[256,128]{1,0:T(8,128)(2,1)}, u32[]{:S(2)}) copy-start(bf16[256,128]{1,0:T(8,128)(2,1)} %constant.19.clone.analysis) | copy-start | bytes 196612
  49.4 0.7 copy-start.12
  73.0 18.8 %all-to-all-start.2 = ((bf16[384,2,128]{2,1,0:T(2,128)(2,1)}), bf16[384,2,128]{2,1,0:T(2,128)(2,1)S(1)}, u32[]{:S(2)}, u32[]{:S(2)}) async-start(bf16[384,2,128]{2,1,0:T(2,128)(2,1)} %bitcast.9), calls=%async_computation.2 | async-start | bytes 393216 | tf_op jit(solution)/shard_map/all_to_all | solution.py:441
  79.2 3.2 %collective-permute-start = (bf16[256,256]{1,0:T(8,128)(2,1)S(1)}, bf16[256,256]{1,0:T(8,128)(2,1)S(1)}, u32[]{:S(2)}, u32[]{:S(2)}) collective-permute-start(bf16[256,256]{1,0:T(8,128)(2,1)S(1)} %get-tuple-element.34), channel_id=1, source_target_pairs={{0,1},{1,0},{2,3},{3,2},{4,5},{5,4},{6,7},{7,6},{8,9},{9,8},{10,11... | collective-permute-start | bytes 393224 | tf_op jit(solution)/shard_map/ppermute | solution.py:475
  92.5 18.8 %all-to-all-start.3 = ((bf16[384,2,128]{2,1,0:T(2,128)(2,1)}), bf16[384,2,128]{2,1,0:T(2,128)(2,1)S(1)}, u32[]{:S(2)}, u32[]{:S(2)}) async-start(bf16[384,2,128]{2,1,0:T(2,128)(2,1)} %bitcast.11), calls=%async_computation.3 | async-start | bytes 393216 | tf_op jit(solution)/shard_map/all_to_all | solution.py:441
  98.8 10.6 %collective-permute-start.1 = (bf16[128,256]{1,0:T(8,128)(2,1)S(1)}, bf16[128,256]{1,0:T(8,128)(2,1)S(1)}, u32[]{:S(2)}, u32[]{:S(2)}) collective-permute-start(bf16[128,256]{1,0:T(8,128)(2,1)S(1)} %get-tuple-element.37), channel_id=1, source_target_pairs={{0,2},{2,0},{1,3},{3,1},{4,6},{6,4},{5,7},{7,5},{8,10},{10,8},{9,1... | collective-permute-start | bytes 196616 | tf_op jit(solution)/shard_map/ppermute | solution.py:479

commit v5 on v4

v5 whole, which is shorter than its diff:
```python
import functools
import math

import jax
import jax.numpy as jnp
import numpy as np
from jax import lax
from jax.experimental import pallas as pl
from jax.experimental.pallas import tpu as pltpu
from jax.sharding import PartitionSpec as P

EPSILON = 1e-05
HIGHEST = lax.Precision.HIGHEST
F32 = jnp.float32
BF16 = jnp.bfloat16

WIDTH = 256
TOTAL = 32768
SEQ = 128
CHUNK = 256
LOCAL = 64
HIDDEN = 64
BANDS = 16
CLIPS = 16
SEND_ROWS = 12
BACK_ROWS = 12
PART_ROWS = 10
PARTS = 64


def tables():
    k1 = np.arange(SEQ)[:, None] + 0.25
    s = np.arange(SEQ)[None, :]
    u = np.arange(CHUNK)[None, :]
    first = 2.0 * np.pi * k1 * s / SEQ
    analysis = np.concatenate([np.cos(first), -np.sin(first)], 0).astype(np.float32)
    synthesis = (np.concatenate([np.cos(first), -np.sin(first)], 0).T / TOTAL).astype(np.float32)
    twist = 2.0 * np.pi * k1 * u / TOTAL
    k2 = np.arange(CHUNK)
    second = 2.0 * np.pi * ((k2[:, None] * k2[None, :]) % CHUNK) / CHUNK
    inner = np.concatenate([np.cos(second), np.sin(second)], 1).astype(np.float32)
    return (
        analysis.astype(BF16),
        synthesis.astype(BF16),
        inner.astype(BF16),
        np.cos(twist).astype(np.float32),
        np.sin(twist).astype(np.float32),
    )


def dot(a, b, dims=((1,), (0,)), precision=None):
    return lax.dot_general(a, b, (dims, ((), ())), precision=precision, preferred_element_type=F32)


def split(x):
    high = x.astype(BF16)
    return high, (x - high.astype(F32)).astype(BF16)


def to_column(row, count):
    shape = (count, count)
    rows = lax.broadcasted_iota(jnp.int32, shape, 0)
    columns = lax.broadcasted_iota(jnp.int32, shape, 1)
    spread = jnp.broadcast_to(row, shape)
    return jnp.sum(jnp.where(rows == columns, spread, jnp.zeros_like(spread)), 1, keepdims=True)


def clip_bounds(clip_len, clip_order):
    shape = (CLIPS, CLIPS)
    rows = lax.broadcasted_iota(jnp.int32, shape, 0)
    columns = lax.broadcasted_iota(jnp.int32, shape, 1)
    sizes = to_column(clip_len.astype(F32), CLIPS)
    lengths = jnp.sum(jnp.where(rows == clip_order, sizes, 0.0), 0, keepdims=True)
    starts = jnp.sum(
        jnp.where(rows < columns, to_column(lengths, CLIPS), 0.0), 0, keepdims=True
    )
    return starts, lengths


def front_kernel(
    rank, clip_len, clip_order, skip_gain, full, in_proj, out_proj, filt_in, filt_out, decay,
    send, gate_out, grad_out, hidden_out, window_out, notes, scratch,
):
    first = ((0,), (0,))
    inputs = jnp.concatenate([full[128 * j : 128 * j + 64, :] for j in range(4)], 0)
    cotangent = jnp.concatenate([full[128 * j + 64 : 128 * j + 128, :] for j in range(4)], 0)
    raw = dot(in_proj[...], inputs)
    out_grad = dot(out_proj[...], cotangent)
    gate_two = raw[2 * LOCAL :, :]
    gate_out[...] = gate_two
    grad_out[...] = out_grad

    offset = rank[0] * CHUNK
    starts, lengths = clip_bounds(clip_len[...], clip_order[...])
    begin = to_column(starts, CLIPS)
    end = begin + to_column(lengths, CLIPS)
    time = (offset + lax.broadcasted_iota(jnp.int32, (CLIPS, CHUNK), 1)).astype(F32)
    member = jnp.where((time >= begin) & (time < end), 1.0, 0.0)
    member = jnp.concatenate([member, jnp.zeros((128 - CLIPS, CHUNK), F32)], 0)
    wide = inputs.astype(F32)
    squares = jnp.sum(wide * wide, 0, keepdims=True)
    power = dot(jnp.broadcast_to(squares, (8, CHUNK)), member, ((1,), (1,)), HIGHEST)[:1, :]
    high, low = split(power)

    step = offset + lax.broadcasted_iota(jnp.int32, (BANDS, CHUNK), 1)
    band = 1 + lax.broadcasted_iota(jnp.int32, (BANDS, CHUNK), 0)
    phases = ((step * band) & (TOTAL - 1)).astype(F32) * (2.0 * math.pi / TOTAL)
    ramp = (offset + lax.broadcasted_iota(jnp.int32, (8, CHUNK), 1)).astype(F32) * (1.0 / TOTAL)
    first_row = lax.broadcasted_iota(jnp.int32, (8, HIDDEN), 0) == 0
    ramp_weight = jnp.where(first_row, filt_in[:8, :], 0.0)
    hidden = jnp.sin(
        dot(ramp_weight, ramp, first, HIGHEST)
        + dot(filt_in[1 : 1 + BANDS, :], jnp.cos(phases), first, HIGHEST)
        + dot(filt_in[1 + BANDS : 1 + 2 * BANDS, :], jnp.sin(phases), first, HIGHEST)
    )
    hidden_out[...] = hidden
    rows = lax.broadcasted_iota(jnp.int32, (LOCAL, LOCAL), 0)
    columns = lax.broadcasted_iota(jnp.int32, (LOCAL, LOCAL), 1)
    shapes = []
    for i in range(2):
        spread = jnp.broadcast_to(decay[i : i + 1, :], (LOCAL, LOCAL))
        rate = jnp.sum(jnp.where(rows == columns, spread, 0.0), 1, keepdims=True)
        window = jnp.exp(-rate * ramp[:1, :]) * TOTAL ** (-0.5)
        window_out[i * LOCAL : (i + 1) * LOCAL, :] = window
        weights = filt_out[i * LOCAL : (i + 1) * LOCAL, :]
        shapes.append(dot(weights, hidden, precision=HIGHEST) * window)

    channel = lax.broadcasted_iota(jnp.int32, (1, LOCAL), 1) == rank[0] % LOCAL
    skips = jnp.sum(jnp.where(channel, skip_gain[...], 0.0), 1, keepdims=True)
    empty = jnp.zeros((1, 128 - CLIPS), F32)
    backward = jnp.full((1, 128), rank[0] // LOCAL, jnp.int32).astype(F32)
    rows = [
        jnp.concatenate([starts, empty], 1),
        jnp.concatenate([lengths, empty], 1),
        jnp.broadcast_to(skips[:1, :], (1, 128)),
        jnp.broadcast_to(skips[1:, :], (1, 128)),
        backward,
        jnp.zeros((3, 128), F32),
    ]
    notes[...] = jnp.concatenate(rows, 0)

    arrays = [raw[:LOCAL, :], raw[LOCAL : 2 * LOCAL, :], gate_two * out_grad, *shapes]
    for at, values in enumerate(arrays):
        scratch[pl.ds(2 * at, LOCAL, stride=SEND_ROWS), :] = values[:, :128]
        scratch[pl.ds(2 * at + 1, LOCAL, stride=SEND_ROWS), :] = values[:, 128:]
    for at, values in enumerate([high, low]):
        scratch[pl.ds(10 + at, LOCAL, stride=SEND_ROWS), :] = jnp.broadcast_to(
            values.astype(F32), (LOCAL, 128)
        )
    packed = scratch[...].astype(BF16)
    send[: LOCAL * SEND_ROWS, :] = packed
    send[LOCAL * SEND_ROWS :, :] = packed


def turn(values, count, inner):
    product = dot(values.astype(BF16), inner[...])
    pieces = []
    for at in range(count):
        real = product[256 * at : 256 * at + 128, :]
        imag = product[256 * at + 128 : 256 * at + 256, :]
        pieces.append((real[:, :256], real[:, 256:], imag[:, :256], imag[:, 256:]))
    return pieces


def to_spectrum(signals, cosines, sines, analysis, inner):
    rows = dot(analysis[...], jnp.concatenate(signals, 1).astype(BF16))
    twisted = []
    for at in range(len(signals)):
        real = rows[:128, 256 * at : 256 * at + 256]
        imag = rows[128:, 256 * at : 256 * at + 256]
        twisted.append(cosines * real + sines * imag)
        twisted.append(cosines * imag - sines * real)
    pieces = turn(jnp.concatenate(twisted, 0), len(signals), inner)
    return [(rc + is_, ic - rs) for rc, rs, ic, is_ in pieces]


def to_signal(spectra, cosines, sines, synthesis, inner):
    stacked = jnp.concatenate([part for pair in spectra for part in pair], 0)
    columns = []
    for rc, rs, ic, is_ in turn(stacked, len(spectra), inner):
        real = rc - is_
        imag = ic + rs
        columns.append(
            jnp.concatenate([cosines * real - sines * imag, cosines * imag + sines * real], 0)
        )
    rows = dot(synthesis, jnp.concatenate(columns, 1).astype(BF16))
    return [rows[:, 256 * at : 256 * at + 256] for at in range(len(spectra))]


def series_kernel(
    notes, received, analysis, synthesis, inner, twist_cos, twist_sin, back, scratch, packed
):
    starts = notes[:1, :]
    counts = jnp.maximum(notes[1:2, :], 1.0)
    skip_one = notes[2:3, :1]
    skip_two = notes[3:4, :1]
    role = notes[4:5, :1]
    scratch[...] = received[...].astype(F32)

    def plane(row):
        return scratch[pl.ds(row, SEQ, stride=SEND_ROWS), :]

    def signal(at):
        return jnp.concatenate([plane(2 * at), plane(2 * at + 1)], 1)

    power = jnp.sum(plane(10) + plane(11), 0, keepdims=True)
    time = lax.broadcasted_iota(jnp.int32, (SEQ, CHUNK), 0) * CHUNK + lax.broadcasted_iota(
        jnp.int32, (SEQ, CHUNK), 1
    )
    time = time.astype(F32)
    lane = lax.broadcasted_iota(jnp.int32, (1, 128), 1)
    inverse_rms = lax.rsqrt(power / (WIDTH * counts) + EPSILON)
    scale = jnp.zeros((SEQ, CHUNK), F32)
    for p in range(CLIPS):
        scale = jnp.where(time >= starts[:, p : p + 1], inverse_rms[:, p : p + 1], scale)

    cosines = twist_cos[...]
    sines = twist_sin[...]

    def analyse(signals):
        return to_spectrum(signals, cosines, sines, analysis, inner)

    def synthesise(parts, table):
        return to_signal(parts, cosines, sines, table, inner)

    def times(a, b, sign):
        return (a[0] * b[0] - sign * (a[1] * b[1]), a[1] * b[0] + sign * (a[0] * b[1]))

    def half(values):
        lower = values[:PARTS, :]
        upper = values[PARTS:, :]
        return jnp.where(jnp.broadcast_to(role, lower.shape) == 0.0, lower, upper)

    value = signal(0) * scale
    gate_one = signal(1) * scale
    scaled_two = signal(2) * scale
    value_spec, second_spec, filter_one, filter_two = analyse(
        [value, scaled_two, signal(3), signal(4)]
    )
    carry_one, level_grad = synthesise(
        [times(value_spec, filter_one, 1.0), times(second_spec, filter_two, -1.0)],
        synthesis[...],
    )
    carry_one = carry_one + skip_one * value
    level_grad = level_grad + skip_two * scaled_two
    level_one = gate_one * carry_one
    scaled_one = gate_one * level_grad
    level_spec, first_spec = analyse([level_one, scaled_one])
    carry_two, shape_two, value_grad, shape_one = synthesise(
        [
            times(level_spec, filter_two, 1.0),
            times(second_spec, level_spec, -1.0),
            times(first_spec, filter_one, -1.0),
            times(first_spec, value_spec, -1.0),
        ],
        half(synthesis[...].astype(F32)).astype(BF16),
    )
    scale_half = half(scale)
    carry_two = scale_half * (carry_two + skip_two * half(level_one))
    value_grad = scale_half * (value_grad + skip_one * half(scaled_one))
    gate_grad = scale_half * half(level_grad * carry_one)

    def total(values):
        return jnp.sum(jnp.sum(values, 0, keepdims=True), 1, keepdims=True)

    skip_row = jnp.zeros((1, 128), F32)
    for at, skip_grad in enumerate([total(scaled_one * value), total(scaled_two * level_one)]):
        high, low = split(skip_grad)
        mid = low.astype(F32)
        low = skip_grad - high.astype(F32) - mid
        for to, part in enumerate([high.astype(F32), mid, low]):
            skip_row = jnp.where(lane == 3 * at + to, part, skip_row)
    for at, values in enumerate([carry_two, shape_two, value_grad, shape_one, gate_grad]):
        packed[pl.ds(2 * at, PARTS, stride=BACK_ROWS), :] = values[:, :128]
        packed[pl.ds(2 * at + 1, PARTS, stride=BACK_ROWS), :] = values[:, 128:]
    packed[pl.ds(10, PARTS, stride=BACK_ROWS), :] = jnp.broadcast_to(skip_row, (PARTS, 128))
    packed[pl.ds(11, PARTS, stride=BACK_ROWS), :] = jnp.zeros((PARTS, 128), F32)
    back[...] = packed[...].astype(BF16)


def back_kernel(
    place, received, full, in_proj, out_proj, gate_in, grad_in, hidden, window,
    given, kept, weights, skip_out, scratch, packed,
):
    scratch[...] = received[...].astype(F32)

    def plane(row):
        return scratch[pl.ds(row, LOCAL, stride=BACK_ROWS), :]

    def signal(at):
        return jnp.concatenate([plane(2 * at), plane(2 * at + 1)], 1)

    carry = signal(0)
    gated = (gate_in[...] * carry).astype(BF16)
    scaled_grad = jnp.concatenate(
        [signal(2).astype(BF16), signal(4).astype(BF16), (grad_in[...] * carry).astype(BF16)], 0
    )
    inputs = jnp.concatenate([full[128 * j : 128 * j + 64, :] for j in range(4)], 0)
    cotangent = jnp.concatenate([full[128 * j + 64 : 128 * j + 128, :] for j in range(4)], 0)
    first = ((0,), (0,))
    last = ((1,), (1,))
    mixed = dot(out_proj[...], gated, first)
    grad_inputs = dot(in_proj[...], scaled_grad, first)
    even = place[0] % 2 == 0
    for at in range(2):
        for to, values in enumerate([mixed, grad_inputs]):
            low = values[128 * at : 128 * at + 64, :]
            high = values[128 * at + 64 : 128 * at + 128, :]
            rows = slice(128 * at + 64 * to, 128 * at + 64 * to + 64)
            given[rows, :] = jnp.where(even, high, low).astype(BF16)
            kept[rows, :] = jnp.where(even, low, high)
    in_weight = dot(scaled_grad, inputs, last)
    out_weight = dot(gated, cotangent, last)
    blank = jnp.zeros((LOCAL, CHUNK), F32)
    shape_one = signal(3) * window[:LOCAL, :]
    shape_two = signal(1) * window[LOCAL:, :]
    filter_grad = dot(
        shape_one, jnp.concatenate([hidden[...], blank], 0), last, HIGHEST
    ) + dot(shape_two, jnp.concatenate([blank, hidden[...]], 0), last, HIGHEST)
    rows = [
        in_weight[64 * at : 64 * at + 64, 128 * half : 128 * half + 128]
        for at in range(3)
        for half in range(2)
    ]
    rows += [out_weight[:, :128], out_weight[:, 128:], filter_grad, jnp.zeros((PARTS, 128), F32)]
    for at, values in enumerate(rows):
        packed[pl.ds(at, PARTS, stride=PART_ROWS), :] = values
    weights[...] = packed[...].astype(BF16)
    lane = lax.broadcasted_iota(jnp.int32, (8, 128), 1)
    order = lax.broadcasted_iota(jnp.int32, (8, 128), 0)
    pick = jnp.where((lane >= 3 * order) & (lane < 3 * order + 3), 1.0, 0.0).astype(BF16)
    skip_out[...] = dot(pick, plane(10).astype(BF16), last)[:2, :] * TOTAL ** (-0.5)


def core_kernel(place, received, kept, given, left):
    total = kept[...] + received[...].astype(F32)
    near = place[0] < 2
    given[...] = jnp.where(near, total[128:, :], total[:128, :]).astype(BF16)
    left[...] = jnp.where(near, total[:128, :], total[128:, :])


def sum_kernel(received, spread):
    four = 4 * PART_ROWS
    parts = jnp.sum(received[...].astype(F32).reshape(PARTS // 4, four, 128), 0)
    total = sum(parts[PART_ROWS * at : PART_ROWS * at + PART_ROWS, :] for at in range(4))
    total = jnp.concatenate([total * TOTAL ** (-0.5)] * 4, 0)
    total = jnp.broadcast_to(total[None], (SEQ // 4, four, 128)).reshape(SEQ * PART_ROWS, 128)
    spread[...] = total.astype(BF16)


def last_kernel(
    received, over_chips, left, mixed, grad_inputs, in_weight, out_weight, filter_grad, scratch
):
    summed = (left[...] + over_chips[...].astype(F32)).astype(BF16)
    mixed[...] = summed[:64, :]
    grad_inputs[...] = summed[64:, :]
    scratch[...] = received[...].astype(F32)

    def block(at):
        first = scratch[pl.ds(at, PARTS, stride=PART_ROWS), :]
        return first + scratch[pl.ds(PARTS * PART_ROWS + at, PARTS, stride=PART_ROWS), :]

    for half in range(2):
        for at in range(3):
            in_weight[64 * at : 64 * at + 64, 128 * half : 128 * half + 128] = block(2 * at + half)
        out_weight[:, 128 * half : 128 * half + 128] = block(6 + half)
    filters = block(8)
    filter_grad[:LOCAL, :] = filters[:, :HIDDEN]
    filter_grad[LOCAL:, :] = filters[:, HIDDEN:]


def call(kernel, name, outs, scalars, arrays, scratch=()):
    def vmem():
        return pl.BlockSpec(memory_space=pltpu.VMEM)

    return pl.pallas_call(
        kernel,
        name=name,
        out_shape=[jax.ShapeDtypeStruct(shape, kind) for shape, kind in outs],
        in_specs=[pl.BlockSpec(memory_space=pltpu.SMEM)] * scalars + [vmem() for _ in range(arrays)],
        out_specs=[vmem() for _ in outs],
        scratch_shapes=[pltpu.VMEM(shape, F32) for shape in scratch],
        compiler_params=pltpu.CompilerParams(vmem_limit_bytes=32 * 1024 * 1024),
    )


def front():
    return call(
        front_kernel,
        "project",
        [
            ((SEQ * SEND_ROWS, 128), BF16),
            ((LOCAL, CHUNK), F32),
            ((LOCAL, CHUNK), F32),
            ((HIDDEN, CHUNK), F32),
            ((2 * LOCAL, CHUNK), F32),
            ((8, 128), F32),
        ],
        1,
        9,
        [(LOCAL * SEND_ROWS, 128)],
    )


def series():
    return call(
        series_kernel,
        "convolve",
        [((PARTS * BACK_ROWS, 128), BF16)],
        0,
        7,
        [(SEQ * SEND_ROWS, 128), (PARTS * BACK_ROWS, 128)],
    )


def rear():
    return call(
        back_kernel,
        "weigh",
        [
            ((256, CHUNK), BF16),
            ((256, CHUNK), F32),
            ((PARTS * PART_ROWS, 128), BF16),
            ((2, LOCAL), F32),
        ],
        1,
        8,
        [(PARTS * BACK_ROWS, 128), (PARTS * PART_ROWS, 128)],
    )


def core_sum():
    return call(core_kernel, "add_core", [((128, CHUNK), BF16), ((128, CHUNK), F32)], 1, 2)


def total():
    return call(sum_kernel, "add_up", [((SEQ * PART_ROWS, 128), BF16)], 0, 1)


def finish():
    return call(
        last_kernel,
        "unpack",
        [
            ((64, CHUNK), BF16),
            ((64, CHUNK), BF16),
            ((3 * LOCAL, WIDTH), F32),
            ((LOCAL, WIDTH), F32),
            ((2 * LOCAL, HIDDEN), F32),
        ],
        0,
        3,
        [(SEQ * PART_ROWS, 128)],
    )


def swap(values, group, among=None):
    tiles = values.reshape(values.shape[0] // group, group, 128)
    tiles = lax.all_to_all(
        tiles, "seq", split_axis=0, concat_axis=0, axis_index_groups=among, tiled=True
    )
    return tiles.reshape(values.shape)


def shards(
    inputs,
    clip_len,
    clip_order,
    in_proj,
    out_proj,
    filt_in,
    filt_out,
    decay_rate,
    skip_gain,
    cotangent,
):
    rank = lax.axis_index("seq").astype(jnp.int32).reshape(1)
    place = lax.axis_index("ch").astype(jnp.int32).reshape(1)
    rank, place = lax.optimization_barrier((rank, place))
    halves = [list(range(at * PARTS, at * PARTS + PARTS)) for at in range(SEQ // PARTS)]
    in_rows = in_proj.reshape(3 * LOCAL, WIDTH)
    out_rows = out_proj.T
    full = lax.all_gather(jnp.concatenate([inputs, cotangent], 0), "ch", axis=0, tiled=True)
    send, gate_two, out_grad, hidden, window, notes = front()(
        rank, clip_len.reshape(1, CLIPS), clip_order.reshape(1, CLIPS), skip_gain, full, in_rows,
        out_rows, filt_in, filt_out.reshape(2 * LOCAL, HIDDEN), decay_rate,
    )
    received = swap(send, 4)
    (back,) = series()(notes, received, *[jnp.asarray(x) for x in tables()])
    returned = swap(back, 4, halves)
    given, kept, weights, grad_skip = rear()(
        place, returned, full, in_rows, out_rows, gate_two, out_grad, hidden, window
    )
    over_cores = lax.ppermute(given, "ch", [(0, 1), (1, 0), (2, 3), (3, 2)])
    given, left = core_sum()(place, over_cores, kept)
    (spread,) = total()(swap(weights, 2, halves))
    spread, given = lax.optimization_barrier((spread, given))
    over_chips = lax.ppermute(given, "ch", [(0, 2), (2, 0), (1, 3), (3, 1)])
    mixed, grad_inputs, in_weight, out_weight, filter_grad = finish()(
        swap(spread, 2), over_chips, left
    )
    return (
        mixed,
        grad_inputs,
        in_weight.reshape(3, LOCAL, WIDTH),
        out_weight.T,
        filter_grad.reshape(2, LOCAL, HIDDEN),
        grad_skip,
    )


def solution(mesh):
    return jax.shard_map(
        shards,
        mesh=mesh,
        in_specs=(
            P("ch", "seq"),
            P(),
            P(),
            P(None, "ch", None),
            P(None, "ch"),
            P(),
            P(None, "ch", None),
            P(None, "ch"),
            P(None, "ch"),
            P("ch", "seq"),
        ),
        out_specs=(
            P("ch", "seq"),
            P("ch", "seq"),
            P(None, "ch", None),
            P(None, "ch"),
            P(None, "ch", None),
            P(None, "ch"),
        ),
        check_vma=False,
    )
```

time: 113 us -> 108 us (0.956)
  blocking collectives: 64 us -> 61.2 us
  Pallas kernels: 8.23 us -> 6.91 us
    all_to_all x2, blocking collectives: 50.5 us -> 47.7 us  [swap(): lax.all_to_all(tiles, 'seq', split_axis=0, concat_axis=0, axis_index_grou...]
    pallas_call x4 -> x3, Pallas kernels: 5.42 us -> 4.45 us  [the longest x1 2.85 us: shards(): back, = series()(notes, received, *[jnp.asarray(x) for x in tables()])]
  transfers between devices with their start and end apart: 4 -> 4, of which waited for: 4 -> 4; matrix products, arithmetic and copies ran while one was open for 0% -> 0% of each run, Pallas kernels for 1% -> 0%
where the time goes in v5:
time: 108 us; the launch traced here: 107 us
  blocking collectives  61.2 us (57%)
  starting transfers between devices  21.8 us (20%)
  waiting for transfers between devices  15.2 us (14%)
  Pallas kernels  6.91 us (6%)
    all_to_all x2, blocking collectives, swap(): lax.all_to_all(tiles, 'seq', split_axis=0, concat_axis=0, axis_index_grou...  47.7 us
    all_gather x1, blocking collectives, shards(): lax.all_gather(jnp.concatenate([inputs, cotangent], 0), 'ch', axis=0, til...  13.5 us
    all_to_all x2, starting transfers between devices, swap(): lax.all_to_all(tiles, 'seq', split_axis=0, concat_axis=0, axis_index_grou...  13 us
    all_to_all x2, waiting for transfers between devices, swap(): lax.all_to_all(tiles, 'seq', split_axis=0, concat_axis=0, axis_index_grou...  9.53 us
    ppermute x1, starting transfers between devices, shards(): over_chips = lax.ppermute(given, 'ch', [(0, 2), (2, 0), (1, 3), (3, 1)])  6.92 us
    ppermute x1, waiting for transfers between devices, shards(): over_chips = lax.ppermute(given, 'ch', [(0, 2), (2, 0), (1, 3), (3, 1)])  4.39 us
    pallas_call x1, Pallas kernels, shards(): back, = series()(notes, received, *[jnp.asarray(x) for x in tables()])  2.85 us
  transfers between devices with their start and end apart: 4, of which 4 were waited for; matrix products, arithmetic and copies ran while one was open for 0% of the time, Pallas kernels for 0%

profile of v5, /device:TPU:8, one launch (start us, length us, event | category | flops | bytes accessed | tf_op | source)
XLA Modules:
  0.0 107.4 jit_solution(4438801280020524458)
XLA Ops:
  0.6 0.8 pad_maximum_fusion
  1.4 13.5 %all_gather.3.full = bf16[512,256]{1,0:T(8,128)(2,1)S(1)} all-gather(bf16[128,256]{1,0:T(8,128)(2,1)S(1)} %pad_maximum_fusion), channel_id=1, replica_groups=mesh['seq'=128,'ch'=4] {'ch'}, dimensions={0}, use_global_device_ids=true | all-gather | bytes 327680 | tf_op jit(solution)/shard_map/all_gather | solution.py:483
  15.0 0.6 copy-done.10
  15.6 0.0 copy-done.9
  15.7 1.3 %project.1 = (bf16[1536,128]{1,0:T(8,128)(2,1)S(1)}, f32[64,256]{1,0:T(8,128)S(1)}, f32[64,256]{1,0:T(8,128)S(1)}, f32[64,256]{1,0:T(8,128)S(1)}, f32[128,256]{1,0:T(8,128)S(1)}, /*index=5*/f32[8,128]{1,0:T(8,128)S(1)}) custom-call(s32[1]{0:T(128)} %bitcast.rank, s32[1,16]{1,0:T(1,128)S(1)} %bitcast.29, s32[1,16]{1,0:T(1,128)S(1)} %bitcast.30, ...), custom_call_target="tpu_custom_call" | custom-call | tf_op jit(solution)/shard_map/project/pallas_call | solution.py:484
  16.9 0.0 copy-start.1
  16.9 0.0 copy-start.2
  16.9 0.0 copy-start.3
  17.0 0.0 copy-start.5
  17.0 0.0 copy-start.6
  17.0 32.0 %all_to_all.20 = bf16[384,4,128]{2,1,0:T(4,128)(2,1)S(1)} all-to-all(bf16[384,4,128]{2,1,0:T(4,128)(2,1)S(1)} %bitcast.23), channel_id=1, replica_groups=mesh['seq'=128,'ch'=4] {'seq'}, dimensions={0} | all-to-all | bytes 786432 | tf_op jit(solution)/shard_map/all_to_all | solution.py:459
  49.0 2.9 %convolve.1 = bf16[768,128]{1,0:T(8,128)(2,1)S(1)} custom-call(f32[8,128]{1,0:T(8,128)S(1)} %get-tuple-element.29.notes, bf16[1536,128]{1,0:T(8,128)(2,1)S(1)} %bitcast.18, bf16[256,128]{1,0:T(8,128)(2,1)S(1)} %copy-done.6, bf16[128,256]{1,0:T(8,128)(2,1)S(1)} %copy-done.5, bf16[256,512]{1,0:T(8,128)(2,1)S(1)} %copy-done.1, f32[128,256]{1,0:T(8,128)S(1)} %copy-done.3, ...), custom_call_target="tpu_custom_call" | custom-call | tf_op jit(solution)/shard_map/convolve/pallas_call | solution.py:489
  51.9 15.7 %all_to_all.21 = bf16[192,4,128]{2,1,0:T(4,128)(2,1)S(1)} all-to-all(bf16[192,4,128]{2,1,0:T(4,128)(2,1)S(1)} %bitcast.20), channel_id=1, replica_groups={{0,4,8,12,16,20,24,28,32,36,40,44,48,52,56,60,64,68,72,76,80,84,88,92,9..., dimensions={0} | all-to-all | bytes 393216 | tf_op jit(solution)/shard_map/all_to_all | solution.py:459
  67.6 1.2 %weigh.1 = (bf16[256,256]{1,0:T(8,128)(2,1)S(1)}, f32[256,256]{1,0:T(8,128)S(1)}, bf16[640,128]{1,0:T(8,128)(2,1)}, f32[2,64]{1,0:T(2,128)}) custom-call(s32[1]{0:T(128)} %bitcast.1.place, bf16[768,128]{1,0:T(8,128)(2,1)S(1)} %bitcast.21, bf16[512,256]{1,0:T(8,128)(2,1)S(1)} %all_gather.3.full, bf16[192,256]{1,0:T(8,128)(2,1)S(1)} %bitcast.25, ...), custom_call_target="tpu_custom_call" | custom-call | tf_op jit(solution)/shard_map/weigh/pallas_call | solution.py:491
  68.7 5.2 %all-to-all-start.2 = ((bf16[320,2,128]{2,1,0:T(2,128)(2,1)}), bf16[320,2,128]{2,1,0:T(2,128)(2,1)S(1)}, u32[]{:S(2)}, u32[]{:S(2)}) async-start(bf16[320,2,128]{2,1,0:T(2,128)(2,1)} %bitcast.11), calls=%async_computation.2 | async-start | bytes 327680 | tf_op jit(solution)/shard_map/all_to_all | solution.py:459
  73.9 1.9 %collective-permute-start = (bf16[256,256]{1,0:T(8,128)(2,1)S(1)}, bf16[256,256]{1,0:T(8,128)(2,1)S(1)}, u32[]{:S(2)}, u32[]{:S(2)}) collective-permute-start(bf16[256,256]{1,0:T(8,128)(2,1)S(1)} %get-tuple-element.36), channel_id=1, source_target_pairs={{0,1},{1,0},{2,3},{3,2},{4,5},{5,4},{6,7},{7,6},{8,9},{9,8},{10,11... | collective-permute-start | bytes 393224 | tf_op jit(solution)/shard_map/ppermute | solution.py:494
  75.8 1.3 %collective-permute-done.received = bf16[256,256]{1,0:T(8,128)(2,1)S(1)} collective-permute-done((bf16[256,256]{1,0:T(8,128)(2,1)S(1)}, bf16[256,256]{1,0:T(8,128)(2,1)S(1)}, u32[]{:S(2)}, u32[]{:S(2)}) %collective-permute-start) | collective-permute-done | bytes 131104 | tf_op jit(solution)/shard_map/ppermute | solution.py:494
  77.2 7.0 %all-to-all-done.2 = bf16[320,2,128]{2,1,0:T(2,128)(2,1)S(1)} async-done(((bf16[320,2,128]{2,1,0:T(2,128)(2,1)}), bf16[320,2,128]{2,1,0:T(2,128)(2,1)S(1)}, u32[]{:S(2)}, u32[]{:S(2)}) %all-to-all-start.2) | async-done | bytes 163872 | tf_op jit(solution)/shard_map/all_to_all | solution.py:459
  84.2 0.8 add_up.1
  85.0 7.8 %all-to-all-start.3 = ((bf16[640,2,128]{2,1,0:T(2,128)(2,1)}), bf16[640,2,128]{2,1,0:T(2,128)(2,1)S(1)}, u32[]{:S(2)}, u32[]{:S(2)}) async-start(bf16[640,2,128]{2,1,0:T(2,128)(2,1)} %bitcast.13), calls=%async_computation.3 | async-start | bytes 655360 | tf_op jit(solution)/shard_map/all_to_all | solution.py:459
  92.8 6.9 %collective-permute-start.1 = (bf16[128,256]{1,0:T(8,128)(2,1)S(1)}, bf16[128,256]{1,0:T(8,128)(2,1)S(1)}, u32[]{:S(2)}, u32[]{:S(2)}) collective-permute-start(bf16[128,256]{1,0:T(8,128)(2,1)S(1)} %get-tuple-element.40), channel_id=1, source_target_pairs={{0,2},{2,0},{1,3},{3,1},{4,6},{6,4},{5,7},{7,5},{8,10},{10,8},{9,1... | collective-permute-start | bytes 196616 | tf_op jit(solution)/shard_map/ppermute | solution.py:498
  99.7 4.4 %collective-permute-done.1.over_chips = bf16[128,256]{1,0:T(8,128)(2,1)S(1)} collective-permute-done((bf16[128,256]{1,0:T(8,128)(2,1)S(1)}, bf16[128,256]{1,0:T(8,128)(2,1)S(1)}, u32[]{:S(2)}, u32[]{:S(2)}) %collective-permute-start.1) | collective-permute-done | bytes 65568 | tf_op jit(solution)/shard_map/ppermute | solution.py:498
  104.1 2.5 %all-to-all-done.3 = bf16[640,2,128]{2,1,0:T(2,128)(2,1)S(1)} async-done(((bf16[640,2,128]{2,1,0:T(2,128)(2,1)}), bf16[640,2,128]{2,1,0:T(2,128)(2,1)S(1)}, u32[]{:S(2)}, u32[]{:S(2)}) %all-to-all-start.3) | async-done | bytes 327712 | tf_op jit(solution)/shard_map/all_to_all | solution.py:459
  106.6 0.8 unpack.1
  (20 shorter events, 0.1 us)
Async XLA Ops:
  1.4 13.5 %copy-start = (bf16[3,64,256]{2,1,0:T(8,128)(2,1)S(1)}, bf16[3,64,256]{2,1,0:T(8,128)(2,1)}, u32[]{:S(2)}) copy-start(bf16[3,64,256]{2,1,0:T(8,128)(2,1)} %param.18) | copy-start | bytes 294916
  1.4 13.5 %copy-start.4 = (bf16[256,64]{0,1:T(8,128)(2,1)S(1)}, bf16[256,64]{0,1:T(8,128)(2,1)}, u32[]{:S(2)}) copy-start(bf16[256,64]{0,1:T(8,128)(2,1)} %param.19) | copy-start | bytes 98308
  1.4 13.5 %copy-start.7 = (f32[2,64,64]{2,1,0:T(8,128)S(1)}, f32[2,64,64]{2,1,0:T(8,128)}, u32[]{:S(2)}) copy-start(f32[2,64,64]{2,1,0:T(8,128)} %param.21) | copy-start | bytes 98308
  1.4 13.5 %copy-start.8 = (f32[33,64]{1,0:T(8,128)S(1)}, f32[33,64]{1,0:T(8,128)}, u32[]{:S(2)}) copy-start(f32[33,64]{1,0:T(8,128)} %filt_in.1) | copy-start | bytes 25348
  14.9 0.7 copy-start.10
  14.9 0.7 copy-start.12
  14.9 0.7 copy-start.9
  14.9 0.7 copy-start.11
  16.9 32.1 %copy-start.1 = (bf16[256,512]{1,0:T(8,128)(2,1)S(1)}, bf16[256,512]{1,0:T(8,128)(2,1)}, u32[]{:S(2)}) copy-start(bf16[256,512]{1,0:T(8,128)(2,1)} %constant.21.clone.inner) | copy-start | bytes 786436
  16.9 32.1 %copy-start.2 = (f32[128,256]{1,0:T(8,128)S(1)}, f32[128,256]{1,0:T(8,128)}, u32[]{:S(2)}) copy-start(f32[128,256]{1,0:T(8,128)} %constant.23.clone.twist_sin) | copy-start | bytes 393220
  16.9 32.1 %copy-start.3 = (f32[128,256]{1,0:T(8,128)S(1)}, f32[128,256]{1,0:T(8,128)}, u32[]{:S(2)}) copy-start(f32[128,256]{1,0:T(8,128)} %constant.22.clone.twist_cos) | copy-start | bytes 393220
  17.0 32.1 %copy-start.5 = (bf16[128,256]{1,0:T(8,128)(2,1)S(1)}, bf16[128,256]{1,0:T(8,128)(2,1)}, u32[]{:S(2)}) copy-start(bf16[128,256]{1,0:T(8,128)(2,1)} %constant.20.clone.synthesis) | copy-start | bytes 196612
  17.0 32.1 %copy-start.6 = (bf16[256,128]{1,0:T(8,128)(2,1)S(1)}, bf16[256,128]{1,0:T(8,128)(2,1)}, u32[]{:S(2)}) copy-start(bf16[256,128]{1,0:T(8,128)(2,1)} %constant.19.clone.analysis) | copy-start | bytes 196612
  68.7 15.5 %all-to-all-start.2 = ((bf16[320,2,128]{2,1,0:T(2,128)(2,1)}), bf16[320,2,128]{2,1,0:T(2,128)(2,1)S(1)}, u32[]{:S(2)}, u32[]{:S(2)}) async-start(bf16[320,2,128]{2,1,0:T(2,128)(2,1)} %bitcast.11), calls=%async_computation.2 | async-start | bytes 327680 | tf_op jit(solution)/shard_map/all_to_all | solution.py:459
  73.9 3.2 %collective-permute-start = (bf16[256,256]{1,0:T(8,128)(2,1)S(1)}, bf16[256,256]{1,0:T(8,128)(2,1)S(1)}, u32[]{:S(2)}, u32[]{:S(2)}) collective-permute-start(bf16[256,256]{1,0:T(8,128)(2,1)S(1)} %get-tuple-element.36), channel_id=1, source_target_pairs={{0,1},{1,0},{2,3},{3,2},{4,5},{5,4},{6,7},{7,6},{8,9},{9,8},{10,11... | collective-permute-start | bytes 393224 | tf_op jit(solution)/shard_map/ppermute | solution.py:494
  85.0 21.6 %all-to-all-start.3 = ((bf16[640,2,128]{2,1,0:T(2,128)(2,1)}), bf16[640,2,128]{2,1,0:T(2,128)(2,1)S(1)}, u32[]{:S(2)}, u32[]{:S(2)}) async-start(bf16[640,2,128]{2,1,0:T(2,128)(2,1)} %bitcast.13), calls=%async_computation.3 | async-start | bytes 655360 | tf_op jit(solution)/shard_map/all_to_all | solution.py:459
  92.8 11.3 %collective-permute-start.1 = (bf16[128,256]{1,0:T(8,128)(2,1)S(1)}, bf16[128,256]{1,0:T(8,128)(2,1)S(1)}, u32[]{:S(2)}, u32[]{:S(2)}) collective-permute-start(bf16[128,256]{1,0:T(8,128)(2,1)S(1)} %get-tuple-element.40), channel_id=1, source_target_pairs={{0,2},{2,0},{1,3},{3,1},{4,6},{6,4},{5,7},{7,5},{8,10},{10,8},{9,1... | collective-permute-start | bytes 196616 | tf_op jit(solution)/shard_map/ppermute | solution.py:498

commit v6 on v5

--- a/solution.py
+++ b/solution.py
@@ -23,7 +23,7 @@
 BANDS = 16
 CLIPS = 16
 SEND_ROWS = 12
-BACK_ROWS = 12
+BACK_ROWS = 10
 PART_ROWS = 10
 PARTS = 64
 
@@ -38,11 +38,13 @@
     twist = 2.0 * np.pi * k1 * u / TOTAL
     k2 = np.arange(CHUNK)
     second = 2.0 * np.pi * ((k2[:, None] * k2[None, :]) % CHUNK) / CHUNK
-    inner = np.concatenate([np.cos(second), np.sin(second)], 1).astype(np.float32)
+    cosines, sines = np.cos(second), np.sin(second)
+    forward = np.block([[cosines, -sines], [sines, cosines]]).astype(np.float32)
     return (
         analysis.astype(BF16),
         synthesis.astype(BF16),
-        inner.astype(BF16),
+        forward.astype(BF16),
+        forward.T.astype(BF16),
         np.cos(twist).astype(np.float32),
         np.sin(twist).astype(np.float32),
     )
@@ -152,43 +154,35 @@
     send[LOCAL * SEND_ROWS :, :] = packed
 
 
-def turn(values, count, inner):
-    product = dot(values.astype(BF16), inner[...])
-    pieces = []
-    for at in range(count):
-        real = product[256 * at : 256 * at + 128, :]
-        imag = product[256 * at + 128 : 256 * at + 256, :]
-        pieces.append((real[:, :256], real[:, 256:], imag[:, :256], imag[:, 256:]))
-    return pieces
-
-
 def to_spectrum(signals, cosines, sines, analysis, inner):
     rows = dot(analysis[...], jnp.concatenate(signals, 1).astype(BF16))
     twisted = []
     for at in range(len(signals)):
         real = rows[:128, 256 * at : 256 * at + 256]
         imag = rows[128:, 256 * at : 256 * at + 256]
-        twisted.append(cosines * real + sines * imag)
-        twisted.append(cosines * imag - sines * real)
-    pieces = turn(jnp.concatenate(twisted, 0), len(signals), inner)
-    return [(rc + is_, ic - rs) for rc, rs, ic, is_ in pieces]
+        parts = [cosines * real + sines * imag, cosines * imag - sines * real]
+        twisted.append(jnp.concatenate(parts, 1).astype(BF16))
+    spectra = dot(jnp.concatenate(twisted, 0), inner[...])
+    pairs = [spectra[128 * at : 128 * at + 128, :] for at in range(len(signals))]
+    return [(pair[:, :256], pair[:, 256:]) for pair in pairs]
 
 
 def to_signal(spectra, cosines, sines, synthesis, inner):
-    stacked = jnp.concatenate([part for pair in spectra for part in pair], 0)
+    stacked = [jnp.concatenate(pair, 1).astype(BF16) for pair in spectra]
+    rows = dot(jnp.concatenate(stacked, 0), inner[...])
     columns = []
-    for rc, rs, ic, is_ in turn(stacked, len(spectra), inner):
-        real = rc - is_
-        imag = ic + rs
-        columns.append(
-            jnp.concatenate([cosines * real - sines * imag, cosines * imag + sines * real], 0)
-        )
-    rows = dot(synthesis, jnp.concatenate(columns, 1).astype(BF16))
-    return [rows[:, 256 * at : 256 * at + 256] for at in range(len(spectra))]
+    for at in range(len(spectra)):
+        real = rows[128 * at : 128 * at + 128, :256]
+        imag = rows[128 * at : 128 * at + 128, 256:]
+        parts = [cosines * real - sines * imag, cosines * imag + sines * real]
+        columns.append(jnp.concatenate(parts, 0).astype(BF16))
+    signals = dot(synthesis, jnp.concatenate(columns, 1))
+    return [signals[:, 256 * at : 256 * at + 256] for at in range(len(spectra))]
 
 
 def series_kernel(
-    notes, received, analysis, synthesis, inner, twist_cos, twist_sin, back, scratch, packed
+    notes, received, analysis, synthesis, forward, backward, twist_cos, twist_sin,
+    back, skips, scratch, packed,
 ):
     starts = notes[:1, :]
     counts = jnp.maximum(notes[1:2, :], 1.0)
@@ -218,10 +212,10 @@
     sines = twist_sin[...]
 
     def analyse(signals):
-        return to_spectrum(signals, cosines, sines, analysis, inner)
+        return to_spectrum(signals, cosines, sines, analysis, forward)
 
     def synthesise(parts, table):
-        return to_signal(parts, cosines, sines, table, inner)
+        return to_signal(parts, cosines, sines, table, backward)
 
     def times(a, b, sign):
         return (a[0] * b[0] - sign * (a[1] * b[1]), a[1] * b[0] + sign * (a[0] * b[1]))
@@ -273,47 +267,40 @@
     for at, values in enumerate([carry_two, shape_two, value_grad, shape_one, gate_grad]):
         packed[pl.ds(2 * at, PARTS, stride=BACK_ROWS), :] = values[:, :128]
         packed[pl.ds(2 * at + 1, PARTS, stride=BACK_ROWS), :] = values[:, 128:]
-    packed[pl.ds(10, PARTS, stride=BACK_ROWS), :] = jnp.broadcast_to(skip_row, (PARTS, 128))
-    packed[pl.ds(11, PARTS, stride=BACK_ROWS), :] = jnp.zeros((PARTS, 128), F32)
+    skips[...] = jnp.broadcast_to(skip_row, (8, 128))
     back[...] = packed[...].astype(BF16)
 
 
-def back_kernel(
-    place, received, full, in_proj, out_proj, gate_in, grad_in, hidden, window,
-    given, kept, weights, skip_out, scratch, packed,
+def returned_signal(scratch, at):
+    rows = [scratch[pl.ds(2 * at + half, LOCAL, stride=BACK_ROWS), :] for half in range(2)]
+    return jnp.concatenate(rows, 1)
+
+
+def weight_kernel(
+    received, full, gate_in, grad_in, hidden, window, weights, gated_out, scaled_out,
+    scratch, packed,
 ):
     scratch[...] = received[...].astype(F32)
-
-    def plane(row):
-        return scratch[pl.ds(row, LOCAL, stride=BACK_ROWS), :]
-
-    def signal(at):
-        return jnp.concatenate([plane(2 * at), plane(2 * at + 1)], 1)
-
-    carry = signal(0)
+    carry = returned_signal(scratch, 0)
     gated = (gate_in[...] * carry).astype(BF16)
     scaled_grad = jnp.concatenate(
-        [signal(2).astype(BF16), signal(4).astype(BF16), (grad_in[...] * carry).astype(BF16)], 0
-    )
+        [
+            returned_signal(scratch, 2).astype(BF16),
+            returned_signal(scratch, 4).astype(BF16),
+            (grad_in[...] * carry).astype(BF16),
+        ],
+        0,
+    )
+    gated_out[...] = gated
+    scaled_out[...] = scaled_grad
     inputs = jnp.concatenate([full[128 * j : 128 * j + 64, :] for j in range(4)], 0)
     cotangent = jnp.concatenate([full[128 * j + 64 : 128 * j + 128, :] for j in range(4)], 0)
-    first = ((0,), (0,))
     last = ((1,), (1,))
-    mixed = dot(out_proj[...], gated, first)
-    grad_inputs = dot(in_proj[...], scaled_grad, first)
-    even = place[0] % 2 == 0
-    for at in range(2):
-        for to, values in enumerate([mixed, grad_inputs]):
-            low = values[128 * at : 128 * at + 64, :]
-            high = values[128 * at + 64 : 128 * at + 128, :]
-            rows = slice(128 * at + 64 * to, 128 * at + 64 * to + 64)
-            given[rows, :] = jnp.where(even, high, low).astype(BF16)
-            kept[rows, :] = jnp.where(even, low, high)
     in_weight = dot(scaled_grad, inputs, last)
     out_weight = dot(gated, cotangent, last)
     blank = jnp.zeros((LOCAL, CHUNK), F32)
-    shape_one = signal(3) * window[:LOCAL, :]
-    shape_two = signal(1) * window[LOCAL:, :]
+    shape_one = returned_signal(scratch, 3) * window[:LOCAL, :]
+    shape_two = returned_signal(scratch, 1) * window[LOCAL:, :]
     filter_grad = dot(
         shape_one, jnp.concatenate([hidden[...], blank], 0), last, HIGHEST
     ) + dot(shape_two, jnp.concatenate([blank, hidden[...]], 0), last, HIGHEST)
@@ -326,10 +313,20 @@
     for at, values in enumerate(rows):
         packed[pl.ds(at, PARTS, stride=PART_ROWS), :] = values
     weights[...] = packed[...].astype(BF16)
-    lane = lax.broadcasted_iota(jnp.int32, (8, 128), 1)
-    order = lax.broadcasted_iota(jnp.int32, (8, 128), 0)
-    pick = jnp.where((lane >= 3 * order) & (lane < 3 * order + 3), 1.0, 0.0).astype(BF16)
-    skip_out[...] = dot(pick, plane(10).astype(BF16), last)[:2, :] * TOTAL ** (-0.5)
+
+
+def channel_kernel(place, gated, scaled_grad, in_proj, out_proj, given, kept):
+    first = ((0,), (0,))
+    mixed = dot(out_proj[...], gated[...], first)
+    grad_inputs = dot(in_proj[...], scaled_grad[...], first)
+    even = place[0] % 2 == 0
+    for at in range(2):
+        for to, values in enumerate([mixed, grad_inputs]):
+            low = values[128 * at : 128 * at + 64, :]
+            high = values[128 * at + 64 : 128 * at + 128, :]
+            rows = slice(128 * at + 64 * to, 128 * at + 64 * to + 64)
+            given[rows, :] = jnp.where(even, high, low).astype(BF16)
+            kept[rows, :] = jnp.where(even, low, high)
 
 
 def core_kernel(place, received, kept, given, left):
@@ -339,17 +336,20 @@
     left[...] = jnp.where(near, total[:128, :], total[128:, :])
 
 
-def sum_kernel(received, spread):
+def sum_kernel(received, skips, spread):
     four = 4 * PART_ROWS
     parts = jnp.sum(received[...].astype(F32).reshape(PARTS // 4, four, 128), 0)
     total = sum(parts[PART_ROWS * at : PART_ROWS * at + PART_ROWS, :] for at in range(4))
-    total = jnp.concatenate([total * TOTAL ** (-0.5)] * 4, 0)
+    row = lax.broadcasted_iota(jnp.int32, (PART_ROWS, 128), 0)
+    total = jnp.where(row == PART_ROWS - 1, skips[:1, :], total * TOTAL ** (-0.5))
+    total = jnp.concatenate([total] * 4, 0)
     total = jnp.broadcast_to(total[None], (SEQ // 4, four, 128)).reshape(SEQ * PART_ROWS, 128)
     spread[...] = total.astype(BF16)
 
 
 def last_kernel(
-    received, over_chips, left, mixed, grad_inputs, in_weight, out_weight, filter_grad, scratch
+    received, over_chips, left, mixed, grad_inputs, in_weight, out_weight, filter_grad, skip_grad,
+    scratch,
 ):
     summed = (left[...] + over_chips[...].astype(F32)).astype(BF16)
     mixed[...] = summed[:64, :]
@@ -367,6 +367,11 @@
     filters = block(8)
     filter_grad[:LOCAL, :] = filters[:, :HIDDEN]
     filter_grad[LOCAL:, :] = filters[:, HIDDEN:]
+    lane = lax.broadcasted_iota(jnp.int32, (8, 128), 1)
+    order = lax.broadcasted_iota(jnp.int32, (8, 128), 0)
+    pick = jnp.where((lane >= 3 * order) & (lane < 3 * order + 3), 1.0, 0.0).astype(BF16)
+    skips = scratch[pl.ds(PART_ROWS - 1, PARTS, stride=PART_ROWS), :].astype(BF16)
+    skip_grad[...] = dot(pick, skips, ((1,), (1,)))[:2, :] * TOTAL ** (-0.5)
 
 
 def call(kernel, name, outs, scalars, arrays, scratch=()):
@@ -406,27 +411,30 @@
     return call(
         series_kernel,
         "convolve",
-        [((PARTS * BACK_ROWS, 128), BF16)],
+        [((PARTS * BACK_ROWS, 128), BF16), ((8, 128), F32)],
         0,
-        7,
+        8,
         [(SEQ * SEND_ROWS, 128), (PARTS * BACK_ROWS, 128)],
     )
 
 
-def rear():
+def weighing():
     return call(
-        back_kernel,
+        weight_kernel,
         "weigh",
         [
-            ((256, CHUNK), BF16),
-            ((256, CHUNK), F32),
             ((PARTS * PART_ROWS, 128), BF16),
-            ((2, LOCAL), F32),
+            ((LOCAL, CHUNK), BF16),
+            ((3 * LOCAL, CHUNK), BF16),
         ],
-        1,
-        8,
+        0,
+        6,
         [(PARTS * BACK_ROWS, 128), (PARTS * PART_ROWS, 128)],
     )
+
+
+def channels():
+    return call(channel_kernel, "mix", [((256, CHUNK), BF16), ((256, CHUNK), F32)], 1, 4)
 
 
 def core_sum():
@@ -434,7 +442,7 @@
 
 
 def total():
-    return call(sum_kernel, "add_up", [((SEQ * PART_ROWS, 128), BF16)], 0, 1)
+    return call(sum_kernel, "add_up", [((SEQ * PART_ROWS, 128), BF16)], 0, 2)
 
 
 def finish():
@@ -447,6 +455,7 @@
             ((3 * LOCAL, WIDTH), F32),
             ((LOCAL, WIDTH), F32),
             ((2 * LOCAL, HIDDEN), F32),
+            ((2, LOCAL), F32),
         ],
         0,
         3,
@@ -486,17 +495,18 @@
         out_rows, filt_in, filt_out.reshape(2 * LOCAL, HIDDEN), decay_rate,
     )
     received = swap(send, 4)
-    (back,) = series()(notes, received, *[jnp.asarray(x) for x in tables()])
-    returned = swap(back, 4, halves)
-    given, kept, weights, grad_skip = rear()(
-        place, returned, full, in_rows, out_rows, gate_two, out_grad, hidden, window
-    )
+    back, skips = series()(notes, received, *[jnp.asarray(x) for x in tables()])
+    returned = swap(back, 2, halves)
+    weights, gated, scaled_grad = weighing()(
+        returned, full, gate_two, out_grad, hidden, window
+    )
+    given, kept = channels()(place, gated, scaled_grad, in_rows, out_rows)
     over_cores = lax.ppermute(given, "ch", [(0, 1), (1, 0), (2, 3), (3, 2)])
     given, left = core_sum()(place, over_cores, kept)
-    (spread,) = total()(swap(weights, 2, halves))
+    (spread,) = total()(swap(weights, 2, halves), skips)
     spread, given = lax.optimization_barrier((spread, given))
     over_chips = lax.ppermute(given, "ch", [(0, 2), (2, 0), (1, 3), (3, 1)])
-    mixed, grad_inputs, in_weight, out_weight, filter_grad = finish()(
+    mixed, grad_inputs, in_weight, out_weight, filter_grad, grad_skip = finish()(
         swap(spread, 2), over_chips, left
     )
     return (

time: 108 us -> 107 us (level)
    pallas_call x3 -> x4, Pallas kernels: 4.79 us -> 4.5 us  [the longest x1 2.4 us: shards(): back, skips = series()(notes, received, *[jnp.asarray(x) for x in tables()])]
where the time goes in v6:
time: 107 us
  blocking collectives  60.9 us (57%)
  starting transfers between devices  21.9 us (20%)
  waiting for transfers between devices  15 us (14%)
  Pallas kernels  6.62 us (6%)
    all_to_all x2, blocking collectives, swap(): lax.all_to_all(tiles, 'seq', split_axis=0, concat_axis=0, axis_index_grou...  47.4 us
    all_gather x1, blocking collectives, shards(): lax.all_gather(jnp.concatenate([inputs, cotangent], 0), 'ch', axis=0, til...  13.5 us
    all_to_all x2, starting transfers between devices, swap(): lax.all_to_all(tiles, 'seq', split_axis=0, concat_axis=0, axis_index_grou...  13.1 us
    all_to_all x2, waiting for transfers between devices, swap(): lax.all_to_all(tiles, 'seq', split_axis=0, concat_axis=0, axis_index_grou...  9.49 us
    ppermute x1, starting transfers between devices, shards(): over_chips = lax.ppermute(given, 'ch', [(0, 2), (2, 0), (1, 3), (3, 1)])  6.91 us
    ppermute x1, waiting for transfers between devices, shards(): over_chips = lax.ppermute(given, 'ch', [(0, 2), (2, 0), (1, 3), (3, 1)])  4.21 us
    pallas_call x1, Pallas kernels, shards(): back, skips = series()(notes, received, *[jnp.asarray(x) for x in tables()])  2.4 us
  transfers between devices with their start and end apart: 4, of which 4 were waited for; matrix products, arithmetic and copies ran while one was open for 0% of the time, Pallas kernels for 0%

profile of v6, /device:TPU:8, one launch (start us, length us, event | category | flops | bytes accessed | tf_op | source)
XLA Modules:
  0.0 106.8 jit_solution(14272982167619716997)
XLA Ops:
  0.7 0.8 pad_maximum_fusion
  1.5 0.0 copy-start.4
  1.5 0.0 copy-start.7
  1.5 13.5 %all_gather.3.full = bf16[512,256]{1,0:T(8,128)(2,1)S(1)} all-gather(bf16[128,256]{1,0:T(8,128)(2,1)S(1)} %pad_maximum_fusion), channel_id=1, replica_groups=mesh['seq'=128,'ch'=4] {'ch'}, dimensions={0}, use_global_device_ids=true | all-gather | bytes 327680 | tf_op jit(solution)/shard_map/all_gather | solution.py:492
  15.0 0.6 copy-done.11
  15.7 0.0 copy-done.10
  15.7 1.3 %project.1 = (bf16[1536,128]{1,0:T(8,128)(2,1)S(1)}, f32[64,256]{1,0:T(8,128)S(1)}, f32[64,256]{1,0:T(8,128)S(1)}, f32[64,256]{1,0:T(8,128)S(1)}, f32[128,256]{1,0:T(8,128)S(1)}, /*index=5*/f32[8,128]{1,0:T(8,128)S(1)}) custom-call(s32[1]{0:T(128)} %bitcast.rank, s32[1,16]{1,0:T(1,128)S(1)} %bitcast.29, s32[1,16]{1,0:T(1,128)S(1)} %bitcast.30, ...), custom_call_target="tpu_custom_call" | custom-call | tf_op jit(solution)/shard_map/project/pallas_call | solution.py:493
  17.0 0.0 copy-start.3
  17.0 0.0 copy-start.6
  17.0 32.0 %all_to_all.20 = bf16[384,4,128]{2,1,0:T(4,128)(2,1)S(1)} all-to-all(bf16[384,4,128]{2,1,0:T(4,128)(2,1)S(1)} %bitcast.22), channel_id=1, replica_groups=mesh['seq'=128,'ch'=4] {'seq'}, dimensions={0} | all-to-all | bytes 786432 | tf_op jit(solution)/shard_map/all_to_all | solution.py:468
  49.1 2.4 %convolve.1 = (bf16[640,128]{1,0:T(8,128)(2,1)S(1)}, f32[8,128]{1,0:T(8,128)S(1)}) custom-call(f32[8,128]{1,0:T(8,128)S(1)} %get-tuple-element.32.notes, bf16[1536,128]{1,0:T(8,128)(2,1)S(1)} %bitcast.18, bf16[256,128]{1,0:T(8,128)(2,1)S(1)} %copy-done.7, bf16[128,256]{1,0:T(8,128)(2,1)S(1)} %copy-done.6, bf16[512,512]{1,0:T(8,128)(2,1)S(1)} %copy-done.1, ...), custom_call_target="tpu_custom_call" | custom-call | tf_op jit(solution)/shard_map/convolve/pallas_call | solution.py:498
  51.5 15.4 %all_to_all.21 = bf16[320,2,128]{2,1,0:T(2,128)(2,1)S(1)} all-to-all(bf16[320,2,128]{2,1,0:T(2,128)(2,1)S(1)} %bitcast.25), channel_id=1, replica_groups={{0,4,8,12,16,20,24,28,32,36,40,44,48,52,56,60,64,68,72,76,80,84,88,92,9..., dimensions={0} | all-to-all | bytes 327680 | tf_op jit(solution)/shard_map/all_to_all | solution.py:468
  66.9 1.1 %weigh.1 = (bf16[640,128]{1,0:T(8,128)(2,1)}, bf16[64,256]{1,0:T(8,128)(2,1)S(1)}, bf16[192,256]{1,0:T(8,128)(2,1)S(1)}) custom-call(bf16[640,128]{1,0:T(8,128)(2,1)S(1)} %bitcast.21, bf16[512,256]{1,0:T(8,128)(2,1)S(1)} %all_gather.3.full, f32[64,256]{1,0:T(8,128)S(1)} %get-tuple-element.35.gate_in, f32[64,256]{1,0:T(8,128)S(1)} %get-tuple-element.36.grad_in, ...), custom_call_target="tpu_custom_call" | custom-call | tf_op jit(solution)/shard_map/weigh/pallas_call | solution.py:500
  68.0 5.2 %all-to-all-start.2 = ((bf16[320,2,128]{2,1,0:T(2,128)(2,1)}), bf16[320,2,128]{2,1,0:T(2,128)(2,1)S(1)}, u32[]{:S(2)}, u32[]{:S(2)}) async-start(bf16[320,2,128]{2,1,0:T(2,128)(2,1)} %bitcast.11), calls=%async_computation.2 | async-start | bytes 327680 | tf_op jit(solution)/shard_map/all_to_all | solution.py:468
  73.2 0.3 mix.1
  73.5 1.9 %collective-permute-start = (bf16[256,256]{1,0:T(8,128)(2,1)S(1)}, bf16[256,256]{1,0:T(8,128)(2,1)S(1)}, u32[]{:S(2)}, u32[]{:S(2)}) collective-permute-start(bf16[256,256]{1,0:T(8,128)(2,1)S(1)} %get-tuple-element.44), channel_id=1, source_target_pairs={{0,1},{1,0},{2,3},{3,2},{4,5},{5,4},{6,7},{7,6},{8,9},{9,8},{10,11... | collective-permute-start | bytes 393224 | tf_op jit(solution)/shard_map/ppermute | solution.py:504
  75.4 1.3 %collective-permute-done.received = bf16[256,256]{1,0:T(8,128)(2,1)S(1)} collective-permute-done((bf16[256,256]{1,0:T(8,128)(2,1)S(1)}, bf16[256,256]{1,0:T(8,128)(2,1)S(1)}, u32[]{:S(2)}, u32[]{:S(2)}) %collective-permute-start) | collective-permute-done | bytes 131104 | tf_op jit(solution)/shard_map/ppermute | solution.py:504
  76.8 6.8 %all-to-all-done.2 = bf16[320,2,128]{2,1,0:T(2,128)(2,1)S(1)} async-done(((bf16[320,2,128]{2,1,0:T(2,128)(2,1)}), bf16[320,2,128]{2,1,0:T(2,128)(2,1)S(1)}, u32[]{:S(2)}, u32[]{:S(2)}) %all-to-all-start.2) | async-done | bytes 163872 | tf_op jit(solution)/shard_map/all_to_all | solution.py:468
  83.5 0.8 add_up.1
  84.3 7.8 %all-to-all-start.3 = ((bf16[640,2,128]{2,1,0:T(2,128)(2,1)}), bf16[640,2,128]{2,1,0:T(2,128)(2,1)S(1)}, u32[]{:S(2)}, u32[]{:S(2)}) async-start(bf16[640,2,128]{2,1,0:T(2,128)(2,1)} %bitcast.13), calls=%async_computation.3 | async-start | bytes 655360 | tf_op jit(solution)/shard_map/all_to_all | solution.py:468
  92.1 6.9 %collective-permute-start.1 = (bf16[128,256]{1,0:T(8,128)(2,1)S(1)}, bf16[128,256]{1,0:T(8,128)(2,1)S(1)}, u32[]{:S(2)}, u32[]{:S(2)}) collective-permute-start(bf16[128,256]{1,0:T(8,128)(2,1)S(1)} %get-tuple-element.48), channel_id=1, source_target_pairs={{0,2},{2,0},{1,3},{3,1},{4,6},{6,4},{5,7},{7,5},{8,10},{10,8},{9,1... | collective-permute-start | bytes 196616 | tf_op jit(solution)/shard_map/ppermute | solution.py:508
  99.1 4.2 %collective-permute-done.1.over_chips = bf16[128,256]{1,0:T(8,128)(2,1)S(1)} collective-permute-done((bf16[128,256]{1,0:T(8,128)(2,1)S(1)}, bf16[128,256]{1,0:T(8,128)(2,1)S(1)}, u32[]{:S(2)}, u32[]{:S(2)}) %collective-permute-start.1) | collective-permute-done | bytes 65568 | tf_op jit(solution)/shard_map/ppermute | solution.py:508
  103.3 2.7 %all-to-all-done.3 = bf16[640,2,128]{2,1,0:T(2,128)(2,1)S(1)} async-done(((bf16[640,2,128]{2,1,0:T(2,128)(2,1)}), bf16[640,2,128]{2,1,0:T(2,128)(2,1)S(1)}, u32[]{:S(2)}, u32[]{:S(2)}) %all-to-all-start.3) | async-done | bytes 327712 | tf_op jit(solution)/shard_map/all_to_all | solution.py:468
  106.0 0.8 unpack.1
  (23 shorter events, 0.1 us)
Async XLA Ops:
  0.6 14.4 %copy-start.8 = (f32[2,64,64]{2,1,0:T(8,128)S(1)}, f32[2,64,64]{2,1,0:T(8,128)}, u32[]{:S(2)}) copy-start(f32[2,64,64]{2,1,0:T(8,128)} %param.22) | copy-start | bytes 98308
  0.6 14.4 %copy-start.9 = (f32[33,64]{1,0:T(8,128)S(1)}, f32[33,64]{1,0:T(8,128)}, u32[]{:S(2)}) copy-start(f32[33,64]{1,0:T(8,128)} %filt_in.1) | copy-start | bytes 25348
  1.5 13.6 %copy-start.2 = (bf16[3,64,256]{2,1,0:T(8,128)(2,1)S(1)}, bf16[3,64,256]{2,1,0:T(8,128)(2,1)}, u32[]{:S(2)}) copy-start(bf16[3,64,256]{2,1,0:T(8,128)(2,1)} %param.19) | copy-start | bytes 294916
  1.5 13.6 %copy-start.5 = (bf16[256,64]{0,1:T(8,128)(2,1)S(1)}, bf16[256,64]{0,1:T(8,128)(2,1)}, u32[]{:S(2)}) copy-start(bf16[256,64]{0,1:T(8,128)(2,1)} %param.20) | copy-start | bytes 98308
  1.5 47.5 %copy-start.4 = (f32[128,256]{1,0:T(8,128)S(1)}, f32[128,256]{1,0:T(8,128)}, u32[]{:S(2)}) copy-start(f32[128,256]{1,0:T(8,128)} %constant.25.clone.twist_cos) | copy-start | bytes 393220
  1.5 47.5 %copy-start.7 = (bf16[256,128]{1,0:T(8,128)(2,1)S(1)}, bf16[256,128]{1,0:T(8,128)(2,1)}, u32[]{:S(2)}) copy-start(bf16[256,128]{1,0:T(8,128)(2,1)} %constant.21.clone.analysis) | copy-start | bytes 196612
  15.0 0.7 copy-start.11
  15.0 0.7 copy-start.13
  15.0 0.7 copy-start.10
  15.0 0.7 copy-start.12
  15.7 33.3 %copy-start = (bf16[512,512]{1,0:T(8,128)(2,1)S(1)}, bf16[512,512]{1,0:T(8,128)(2,1)}, u32[]{:S(2)}) copy-start(bf16[512,512]{1,0:T(8,128)(2,1)} %constant.24.clone.backward) | copy-start | bytes 1572868
  15.7 33.3 %copy-start.1 = (bf16[512,512]{1,0:T(8,128)(2,1)S(1)}, bf16[512,512]{1,0:T(8,128)(2,1)}, u32[]{:S(2)}) copy-start(bf16[512,512]{1,0:T(8,128)(2,1)} %constant.23.clone.forward) | copy-start | bytes 1572868
  17.0 32.1 %copy-start.3 = (f32[128,256]{1,0:T(8,128)S(1)}, f32[128,256]{1,0:T(8,128)}, u32[]{:S(2)}) copy-start(f32[128,256]{1,0:T(8,128)} %constant.26.clone.twist_sin) | copy-start | bytes 393220
  17.0 32.1 %copy-start.6 = (bf16[128,256]{1,0:T(8,128)(2,1)S(1)}, bf16[128,256]{1,0:T(8,128)(2,1)}, u32[]{:S(2)}) copy-start(bf16[128,256]{1,0:T(8,128)(2,1)} %constant.22.clone.synthesis) | copy-start | bytes 196612
  68.0 15.6 %all-to-all-start.2 = ((bf16[320,2,128]{2,1,0:T(2,128)(2,1)}), bf16[320,2,128]{2,1,0:T(2,128)(2,1)S(1)}, u32[]{:S(2)}, u32[]{:S(2)}) async-start(bf16[320,2,128]{2,1,0:T(2,128)(2,1)} %bitcast.11), calls=%async_computation.2 | async-start | bytes 327680 | tf_op jit(solution)/shard_map/all_to_all | solution.py:468
  73.5 3.2 %collective-permute-start = (bf16[256,256]{1,0:T(8,128)(2,1)S(1)}, bf16[256,256]{1,0:T(8,128)(2,1)S(1)}, u32[]{:S(2)}, u32[]{:S(2)}) collective-permute-start(bf16[256,256]{1,0:T(8,128)(2,1)S(1)} %get-tuple-element.44), channel_id=1, source_target_pairs={{0,1},{1,0},{2,3},{3,2},{4,5},{5,4},{6,7},{7,6},{8,9},{9,8},{10,11... | collective-permute-start | bytes 393224 | tf_op jit(solution)/shard_map/ppermute | solution.py:504
  84.3 21.7 %all-to-all-start.3 = ((bf16[640,2,128]{2,1,0:T(2,128)(2,1)}), bf16[640,2,128]{2,1,0:T(2,128)(2,1)S(1)}, u32[]{:S(2)}, u32[]{:S(2)}) async-start(bf16[640,2,128]{2,1,0:T(2,128)(2,1)} %bitcast.13), calls=%async_computation.3 | async-start | bytes 655360 | tf_op jit(solution)/shard_map/all_to_all | solution.py:468
  92.1 11.1 %collective-permute-start.1 = (bf16[128,256]{1,0:T(8,128)(2,1)S(1)}, bf16[128,256]{1,0:T(8,128)(2,1)S(1)}, u32[]{:S(2)}, u32[]{:S(2)}) collective-permute-start(bf16[128,256]{1,0:T(8,128)(2,1)S(1)} %get-tuple-element.48), channel_id=1, source_target_pairs={{0,2},{2,0},{1,3},{3,1},{4,6},{6,4},{5,7},{7,5},{8,10},{10,8},{9,1... | collective-permute-start | bytes 196616 | tf_op jit(solution)/shard_map/ppermute | solution.py:508

commit v7 on v6

--- a/solution.py
+++ b/solution.py
@@ -22,7 +22,7 @@
 HIDDEN = 64
 BANDS = 16
 CLIPS = 16
-SEND_ROWS = 12
+SEND_ROWS = 8
 BACK_ROWS = 10
 PART_ROWS = 10
 PARTS = 64
@@ -50,6 +50,52 @@
     )
 
 
+def wave_tables():
+    f = np.arange(1, BANDS + 1)
+    count = 2 * BANDS + 2
+    chunk = 2.0 * np.pi * (f[None, :] * np.arange(SEQ)[:, None] % SEQ) / SEQ
+    sample = 2.0 * np.pi * f[:, None] * np.arange(CHUNK)[None, :] / TOTAL
+    cosines, sines = np.cos(chunk), np.sin(chunk)
+    ramp = np.arange(SEQ)[:, None] / SEQ
+    ones = np.ones((SEQ, 1))
+    first = np.concatenate([cosines, cosines, ramp, ones], 1)
+    second = np.concatenate([sines, -sines, 0 * ones, 0 * ones], 1)
+    inner = np.concatenate(
+        [
+            np.cos(sample),
+            np.sin(sample),
+            np.ones((1, CHUNK)),
+            np.arange(CHUNK)[None, :] / TOTAL,
+        ],
+        0,
+    ).astype(np.float32)
+    high = inner.astype(BF16)
+    low = (inner - high.astype(np.float32)).astype(BF16)
+    pick_first = np.zeros((1 + 2 * BANDS, count))
+    pick_second = np.zeros((1 + 2 * BANDS, count))
+    for band in range(BANDS):
+        pick_first[1 + band, band] = 1
+        pick_first[1 + BANDS + band, BANDS + band] = 1
+        pick_second[1 + BANDS + band, band] = 1
+        pick_second[1 + band, BANDS + band] = 1
+    pick_first[0, 2 * BANDS :] = 1
+
+    def lanes(table):
+        wide = np.zeros((table.shape[0], 128), np.float32)
+        wide[:, : 3 * count] = np.concatenate([table] * 3, 1)
+        return wide
+
+    def rows(table):
+        wide = np.zeros((40, 128), np.float32)
+        wide[:32] = lanes(table)[:32]
+        wide[39] = lanes(table)[32]
+        return wide
+
+    factors = np.zeros((128, CHUNK), BF16)
+    factors[: 3 * count] = np.concatenate([high, low, high], 0)
+    return lanes(first), lanes(second), rows(pick_first), rows(pick_second), factors
+
+
 def dot(a, b, dims=((1,), (0,)), precision=None):
     return lax.dot_general(a, b, (dims, ((), ())), precision=precision, preferred_element_type=F32)
 
@@ -80,7 +126,7 @@
 
 
 def front_kernel(
-    rank, clip_len, clip_order, skip_gain, full, in_proj, out_proj, filt_in, filt_out, decay,
+    rank, clip_len, clip_order, skip_gain, full, in_proj, out_proj, filt_in, decay,
     send, gate_out, grad_out, hidden_out, window_out, notes, scratch,
 ):
     first = ((0,), (0,))
@@ -118,14 +164,11 @@
     hidden_out[...] = hidden
     rows = lax.broadcasted_iota(jnp.int32, (LOCAL, LOCAL), 0)
     columns = lax.broadcasted_iota(jnp.int32, (LOCAL, LOCAL), 1)
-    shapes = []
     for i in range(2):
         spread = jnp.broadcast_to(decay[i : i + 1, :], (LOCAL, LOCAL))
         rate = jnp.sum(jnp.where(rows == columns, spread, 0.0), 1, keepdims=True)
         window = jnp.exp(-rate * ramp[:1, :]) * TOTAL ** (-0.5)
         window_out[i * LOCAL : (i + 1) * LOCAL, :] = window
-        weights = filt_out[i * LOCAL : (i + 1) * LOCAL, :]
-        shapes.append(dot(weights, hidden, precision=HIGHEST) * window)
 
     channel = lax.broadcasted_iota(jnp.int32, (1, LOCAL), 1) == rank[0] % LOCAL
     skips = jnp.sum(jnp.where(channel, skip_gain[...], 0.0), 1, keepdims=True)
@@ -141,12 +184,12 @@
     ]
     notes[...] = jnp.concatenate(rows, 0)
 
-    arrays = [raw[:LOCAL, :], raw[LOCAL : 2 * LOCAL, :], gate_two * out_grad, *shapes]
+    arrays = [raw[:LOCAL, :], raw[LOCAL : 2 * LOCAL, :], gate_two * out_grad]
     for at, values in enumerate(arrays):
         scratch[pl.ds(2 * at, LOCAL, stride=SEND_ROWS), :] = values[:, :128]
         scratch[pl.ds(2 * at + 1, LOCAL, stride=SEND_ROWS), :] = values[:, 128:]
     for at, values in enumerate([high, low]):
-        scratch[pl.ds(10 + at, LOCAL, stride=SEND_ROWS), :] = jnp.broadcast_to(
+        scratch[pl.ds(6 + at, LOCAL, stride=SEND_ROWS), :] = jnp.broadcast_to(
             values.astype(F32), (LOCAL, 128)
         )
     packed = scratch[...].astype(BF16)
@@ -180,8 +223,78 @@
     return [signals[:, 256 * at : 256 * at + 256] for at in range(len(spectra))]
 
 
+WAVE = (6.2831826, -41.341423, 81.59618, -76.5801, 41.205395, -12.271262)
+
+
+def sine(turns):
+    rest = turns - jnp.floor(turns + 0.5)
+    square = rest * rest
+    value = jnp.full_like(rest, WAVE[-1])
+    for factor in WAVE[-2::-1]:
+        value = value * square + factor
+    return value * rest
+
+
+def filter_kernel(
+    rank, filt_in, filt_out, decay, wave_first, wave_second, pick_first, pick_second, factors,
+    analysis, forward, twist_cos, twist_sin, spectra, weight_one, weight_two, out_one, out_two,
+    shapes,
+):
+    channel = rank[0] % LOCAL
+    first = ((0,), (0,))
+    groups = 8 * HIDDEN
+    row = lax.broadcasted_iota(jnp.int32, (groups, HIDDEN), 0)
+    column = lax.broadcasted_iota(jnp.int32, (groups, HIDDEN), 1)
+    repeat = jnp.where(row // 8 == column, 1.0, 0.0)
+    for pick, target in [(pick_first, weight_one), (pick_second, weight_two)]:
+        weights = dot(filt_in[:32, :], pick[:32, :], first, HIGHEST) + dot(
+            filt_in[25:33, :], pick[32:, :], first, HIGHEST
+        )
+        target[...] = dot(repeat, weights * (0.5 / math.pi), precision=HIGHEST)
+    lane = lax.broadcasted_iota(jnp.int32, (1, LOCAL), 1)
+    here = lax.broadcasted_iota(jnp.int32, (LOCAL, HIDDEN), 0) == channel
+    for i, target in enumerate([out_one, out_two]):
+        mine = jnp.where(here, filt_out[i * LOCAL : (i + 1) * LOCAL, :], 0.0)
+        spread = jnp.broadcast_to(
+            to_column(jnp.sum(mine, 0, keepdims=True), HIDDEN), (HIDDEN, 128)
+        )
+        target[...] = dot(repeat, spread, precision=HIGHEST)
+    rates = jnp.sum(jnp.where(lane == channel, decay[...], 0.0), 1, keepdims=True)
+    count = 2 * BANDS + 2
+    exact = lax.broadcasted_iota(jnp.int32, (groups, 128), 1) < 2 * count
+
+    def block(at, carry):
+        rows = pl.ds(pl.multiple_of(at * 8, 8), 8)
+
+        def repeated(values):
+            return jnp.broadcast_to(values[None], (HIDDEN, 8, 128)).reshape(groups, 128)
+
+        sums = repeated(wave_first[rows, :]) * weight_one[...]
+        sums = sums + repeated(wave_second[rows, :]) * weight_two[...]
+        high = sums.astype(BF16).astype(F32)
+        hidden = sine(dot(jnp.where(exact, high, sums - high).astype(BF16), factors[...]))
+        for i, target in enumerate([out_one, out_two]):
+            factor = target[...]
+            product = hidden * jnp.concatenate([factor, factor], 1)
+            shapes[i, rows, :] = jnp.sum(product.reshape(HIDDEN, 8, CHUNK), 0)
+        return carry
+
+    lax.fori_loop(0, SEQ // 8, block, 0)
+    time = lax.broadcasted_iota(jnp.int32, (SEQ, CHUNK), 0) * CHUNK + lax.broadcasted_iota(
+        jnp.int32, (SEQ, CHUNK), 1
+    )
+    ramp = time.astype(F32) * (1.0 / TOTAL)
+    windows = [jnp.exp(-rates[i : i + 1, :] * ramp) * TOTAL ** (-0.5) for i in range(2)]
+    both = to_spectrum(
+        [shapes[i] * windows[i] for i in range(2)], twist_cos[...], twist_sin[...], analysis, forward
+    )
+    for i, (real, imag) in enumerate(both):
+        spectra[128 * i : 128 * i + 128, :256] = real
+        spectra[128 * i : 128 * i + 128, 256:] = imag
+
+
 def series_kernel(
-    notes, received, analysis, synthesis, forward, backward, twist_cos, twist_sin,
+    notes, received, filters, analysis, synthesis, forward, backward, twist_cos, twist_sin,
     back, skips, scratch, packed,
 ):
     starts = notes[:1, :]
@@ -197,7 +310,7 @@
     def signal(at):
         return jnp.concatenate([plane(2 * at), plane(2 * at + 1)], 1)
 
-    power = jnp.sum(plane(10) + plane(11), 0, keepdims=True)
+    power = jnp.sum(plane(6) + plane(7), 0, keepdims=True)
     time = lax.broadcasted_iota(jnp.int32, (SEQ, CHUNK), 0) * CHUNK + lax.broadcasted_iota(
         jnp.int32, (SEQ, CHUNK), 1
     )
@@ -228,9 +341,11 @@
     value = signal(0) * scale
     gate_one = signal(1) * scale
     scaled_two = signal(2) * scale
-    value_spec, second_spec, filter_one, filter_two = analyse(
-        [value, scaled_two, signal(3), signal(4)]
-    )
+    value_spec, second_spec = analyse([value, scaled_two])
+    filter_one, filter_two = [
+        (filters[128 * i : 128 * i + 128, :256], filters[128 * i : 128 * i + 128, 256:])
+        for i in range(2)
+    ]
     carry_one, level_grad = synthesise(
         [times(value_spec, filter_one, 1.0), times(second_spec, filter_two, -1.0)],
         synthesis[...],
@@ -402,8 +517,19 @@
             ((8, 128), F32),
         ],
         1,
-        9,
+        8,
         [(LOCAL * SEND_ROWS, 128)],
+    )
+
+
+def filtering():
+    return call(
+        filter_kernel,
+        "filters",
+        [((2 * SEQ, 2 * CHUNK), F32)],
+        1,
+        12,
+        [(8 * HIDDEN, 128)] * 4 + [(2, SEQ, CHUNK)],
     )
 
 
@@ -413,7 +539,7 @@
         "convolve",
         [((PARTS * BACK_ROWS, 128), BF16), ((8, 128), F32)],
         0,
-        8,
+        9,
         [(SEQ * SEND_ROWS, 128), (PARTS * BACK_ROWS, 128)],
     )
 
@@ -492,10 +618,19 @@
     full = lax.all_gather(jnp.concatenate([inputs, cotangent], 0), "ch", axis=0, tiled=True)
     send, gate_two, out_grad, hidden, window, notes = front()(
         rank, clip_len.reshape(1, CLIPS), clip_order.reshape(1, CLIPS), skip_gain, full, in_rows,
-        out_rows, filt_in, filt_out.reshape(2 * LOCAL, HIDDEN), decay_rate,
+        out_rows, filt_in, decay_rate,
     )
     received = swap(send, 4)
-    back, skips = series()(notes, received, *[jnp.asarray(x) for x in tables()])
+    analysis, synthesis, forward, backward, twist_cos, twist_sin = [
+        jnp.asarray(x) for x in tables()
+    ]
+    (spectra,) = filtering()(
+        rank, filt_in, filt_out.reshape(2 * LOCAL, HIDDEN), decay_rate,
+        *[jnp.asarray(x) for x in wave_tables()], analysis, forward, twist_cos, twist_sin,
+    )
+    back, skips = series()(
+        notes, received, spectra, analysis, synthesis, forward, backward, twist_cos, twist_sin
+    )
     returned = swap(back, 2, halves)
     weights, gated, scaled_grad = weighing()(
         returned, full, gate_two, out_grad, hidden, window

time: 107 us -> 105 us (0.981)
  blocking collectives: 60.9 us -> 29.3 us
  starting transfers between devices: 21.9 us -> 36.8 us
  Pallas kernels: 6.62 us -> 15.7 us
  waiting for transfers between devices: 15 us -> 20.7 us
    all_to_all x2 -> x1, blocking collectives: 47.4 us -> 15.8 us  [swap(): lax.all_to_all(tiles, 'seq', split_axis=0, concat_axis=0, axis_index_grou...]
    all_to_all x2 -> x3, starting transfers between devices: 13.1 us -> 28 us  [swap(): lax.all_to_all(tiles, 'seq', split_axis=0, concat_axis=0, axis_index_grou...]
    pallas_call x1 -> x2, Pallas kernels: 2.4 us -> 11.6 us  [the longest x1 9.46 us: shards(): filtering()]
    all_to_all x2 -> x3, waiting for transfers between devices: 9.49 us -> 15 us  [swap(): lax.all_to_all(tiles, 'seq', split_axis=0, concat_axis=0, axis_index_grou...]
  transfers between devices with their start and end apart: 4 -> 5, of which waited for: 4 -> 5; matrix products, arithmetic and copies ran while one was open for 0% -> 0% of each run, Pallas kernels for 0% -> 9%
where the time goes in v7:
time: 105 us; the launch traced here: 104 us
  starting transfers between devices  36.8 us (35%)
  blocking collectives  29.3 us (28%)
  waiting for transfers between devices  20.7 us (20%)
  Pallas kernels  15.7 us (15%)
    all_to_all x3, starting transfers between devices, swap(): lax.all_to_all(tiles, 'seq', split_axis=0, concat_axis=0, axis_index_grou...  28 us
    all_to_all x1, blocking collectives, swap(): lax.all_to_all(tiles, 'seq', split_axis=0, concat_axis=0, axis_index_grou...  15.8 us
    all_to_all x3, waiting for transfers between devices, swap(): lax.all_to_all(tiles, 'seq', split_axis=0, concat_axis=0, axis_index_grou...  15 us
    all_gather x1, blocking collectives, shards(): lax.all_gather(jnp.concatenate([inputs, cotangent], 0), 'ch', axis=0, til...  13.5 us
    pallas_call x1, Pallas kernels, shards(): filtering()  9.46 us
    ppermute x1, starting transfers between devices, shards(): over_chips = lax.ppermute(given, 'ch', [(0, 2), (2, 0), (1, 3), (3, 1)])  6.92 us
    ppermute x1, waiting for transfers between devices, shards(): over_chips = lax.ppermute(given, 'ch', [(0, 2), (2, 0), (1, 3), (3, 1)])  4.33 us
    pallas_call x1, Pallas kernels, shards(): series()  2.17 us
  transfers between devices with their start and end apart: 5, of which 5 were waited for; matrix products, arithmetic and copies ran while one was open for 0% of the time, Pallas kernels for 9%

profile of v7, /device:TPU:8, one launch (start us, length us, event | category | flops | bytes accessed | tf_op | source)
XLA Modules:
  0.0 104.4 jit_solution(7435289176276834852)
XLA Ops:
  0.7 0.0 copy-start.13
  0.7 0.0 copy-start.14
  0.7 0.8 pad_maximum_fusion
  1.5 0.0 copy-start.10
  1.5 0.0 copy-start.11
  1.6 13.5 %all_gather.3.full = bf16[512,256]{1,0:T(8,128)(2,1)S(1)} all-gather(bf16[128,256]{1,0:T(8,128)(2,1)S(1)} %pad_maximum_fusion), channel_id=1, replica_groups=mesh['seq'=128,'ch'=4] {'ch'}, dimensions={0}, use_global_device_ids=true | all-gather | bytes 327680 | tf_op jit(solution)/shard_map/all_gather | solution.py:618
  15.1 1.1 %project.1 = (bf16[1024,128]{1,0:T(8,128)(2,1)}, f32[64,256]{1,0:T(8,128)S(1)}, f32[64,256]{1,0:T(8,128)S(1)}, f32[64,256]{1,0:T(8,128)S(1)}, f32[128,256]{1,0:T(8,128)S(1)}, /*index=5*/f32[8,128]{1,0:T(8,128)S(1)}) custom-call(s32[1]{0:T(128)} %bitcast.rank, s32[1,16]{1,0:T(1,128)S(1)} %bitcast.28, s32[1,16]{1,0:T(1,128)S(1)} %bitcast.29, ...), custom_call_target="tpu_custom_call" | custom-call | tf_op jit(solution)/shard_map/project/pallas_call | solution.py:619
  16.3 14.6 %all-to-all-start = ((bf16[256,4,128]{2,1,0:T(4,128)(2,1)}), bf16[256,4,128]{2,1,0:T(4,128)(2,1)S(1)}, u32[]{:S(2)}, u32[]{:S(2)}) async-start(bf16[256,4,128]{2,1,0:T(4,128)(2,1)} %bitcast.6), calls=%async_computation | async-start | bytes 524288 | tf_op jit(solution)/shard_map/all_to_all | solution.py:594
  31.0 9.5 %filters.1 = f32[256,512]{1,0:T(8,128)S(1)} custom-call(s32[1]{0:T(128)} %bitcast.rank, f32[33,64]{1,0:T(8,128)S(1)} %copy-done.7, f32[128,64]{1,0:T(8,128)S(1)} %bitcast.27, f32[2,64]{1,0:T(2,128)S(1)} %copy-done.15, f32[128,128]{1,0:T(8,128)S(1)} %copy-done.10, f32[128,128]{1,0:T(8,128)S(1)} %copy-done.11, f32[40,128]{1,0:T(8,128)S(1)} %copy-done.13, ...), custom_call_target="tpu_custom_call" | custom-call | tf_op jit(solution)/shard_map/filters/pallas_call | solution.py:627
  40.5 5.4 %all-to-all-done = bf16[256,4,128]{2,1,0:T(4,128)(2,1)S(1)} async-done(((bf16[256,4,128]{2,1,0:T(4,128)(2,1)}), bf16[256,4,128]{2,1,0:T(4,128)(2,1)S(1)}, u32[]{:S(2)}, u32[]{:S(2)}) %all-to-all-start) | async-done | bytes 262176 | tf_op jit(solution)/shard_map/all_to_all | solution.py:594
  45.9 2.2 %convolve.1 = (bf16[640,128]{1,0:T(8,128)(2,1)S(1)}, f32[8,128]{1,0:T(8,128)S(1)}) custom-call(f32[8,128]{1,0:T(8,128)S(1)} %get-tuple-element.32.notes, bf16[1024,128]{1,0:T(8,128)(2,1)S(1)} %bitcast.19, f32[256,512]{1,0:T(8,128)S(1)} %filters.1, bf16[256,128]{1,0:T(8,128)(2,1)S(1)} %copy-done.5, bf16[128,256]{1,0:T(8,128)(2,1)S(1)} %copy-done.9, ...), custom_call_target="tpu_custom_call" | custom-call | tf_op jit(solution)/shard_map/convolve/pallas_call | solution.py:631
  48.0 15.8 %all_to_all.20 = bf16[320,2,128]{2,1,0:T(2,128)(2,1)S(1)} all-to-all(bf16[320,2,128]{2,1,0:T(2,128)(2,1)S(1)} %bitcast.24), channel_id=1, replica_groups={{0,4,8,12,16,20,24,28,32,36,40,44,48,52,56,60,64,68,72,76,80,84,88,92,9..., dimensions={0} | all-to-all | bytes 327680 | tf_op jit(solution)/shard_map/all_to_all | solution.py:594
  63.9 1.1 %weigh.1 = (bf16[640,128]{1,0:T(8,128)(2,1)}, bf16[64,256]{1,0:T(8,128)(2,1)S(1)}, bf16[192,256]{1,0:T(8,128)(2,1)S(1)}) custom-call(bf16[640,128]{1,0:T(8,128)(2,1)S(1)} %bitcast.21, bf16[512,256]{1,0:T(8,128)(2,1)S(1)} %all_gather.3.full, f32[64,256]{1,0:T(8,128)S(1)} %get-tuple-element.35.gate_in, f32[64,256]{1,0:T(8,128)S(1)} %get-tuple-element.36.grad_in, ...), custom_call_target="tpu_custom_call" | custom-call | tf_op jit(solution)/shard_map/weigh/pallas_call | solution.py:635
  64.9 5.5 %all-to-all-start.2 = ((bf16[320,2,128]{2,1,0:T(2,128)(2,1)}), bf16[320,2,128]{2,1,0:T(2,128)(2,1)S(1)}, u32[]{:S(2)}, u32[]{:S(2)}) async-start(bf16[320,2,128]{2,1,0:T(2,128)(2,1)} %bitcast.11), calls=%async_computation.2 | async-start | bytes 327680 | tf_op jit(solution)/shard_map/all_to_all | solution.py:594
  70.4 0.3 mix.1
  70.7 1.9 %collective-permute-start = (bf16[256,256]{1,0:T(8,128)(2,1)S(1)}, bf16[256,256]{1,0:T(8,128)(2,1)S(1)}, u32[]{:S(2)}, u32[]{:S(2)}) collective-permute-start(bf16[256,256]{1,0:T(8,128)(2,1)S(1)} %get-tuple-element.44), channel_id=1, source_target_pairs={{0,1},{1,0},{2,3},{3,2},{4,5},{5,4},{6,7},{7,6},{8,9},{9,8},{10,11... | collective-permute-start | bytes 393224 | tf_op jit(solution)/shard_map/ppermute | solution.py:639
  72.6 1.3 %collective-permute-done.received = bf16[256,256]{1,0:T(8,128)(2,1)S(1)} collective-permute-done((bf16[256,256]{1,0:T(8,128)(2,1)S(1)}, bf16[256,256]{1,0:T(8,128)(2,1)S(1)}, u32[]{:S(2)}, u32[]{:S(2)}) %collective-permute-start) | collective-permute-done | bytes 131104 | tf_op jit(solution)/shard_map/ppermute | solution.py:639
  74.0 6.8 %all-to-all-done.2 = bf16[320,2,128]{2,1,0:T(2,128)(2,1)S(1)} async-done(((bf16[320,2,128]{2,1,0:T(2,128)(2,1)}), bf16[320,2,128]{2,1,0:T(2,128)(2,1)S(1)}, u32[]{:S(2)}, u32[]{:S(2)}) %all-to-all-start.2) | async-done | bytes 163872 | tf_op jit(solution)/shard_map/all_to_all | solution.py:594
  80.8 0.8 add_up.1
  81.5 7.9 %all-to-all-start.3 = ((bf16[640,2,128]{2,1,0:T(2,128)(2,1)}), bf16[640,2,128]{2,1,0:T(2,128)(2,1)S(1)}, u32[]{:S(2)}, u32[]{:S(2)}) async-start(bf16[640,2,128]{2,1,0:T(2,128)(2,1)} %bitcast.13), calls=%async_computation.3 | async-start | bytes 655360 | tf_op jit(solution)/shard_map/all_to_all | solution.py:594
  89.4 6.9 %collective-permute-start.1 = (bf16[128,256]{1,0:T(8,128)(2,1)S(1)}, bf16[128,256]{1,0:T(8,128)(2,1)S(1)}, u32[]{:S(2)}, u32[]{:S(2)}) collective-permute-start(bf16[128,256]{1,0:T(8,128)(2,1)S(1)} %get-tuple-element.48), channel_id=1, source_target_pairs={{0,2},{2,0},{1,3},{3,1},{4,6},{6,4},{5,7},{7,5},{8,10},{10,8},{9,1... | collective-permute-start | bytes 196616 | tf_op jit(solution)/shard_map/ppermute | solution.py:643
  96.3 4.3 %collective-permute-done.1.over_chips = bf16[128,256]{1,0:T(8,128)(2,1)S(1)} collective-permute-done((bf16[128,256]{1,0:T(8,128)(2,1)S(1)}, bf16[128,256]{1,0:T(8,128)(2,1)S(1)}, u32[]{:S(2)}, u32[]{:S(2)}) %collective-permute-start.1) | collective-permute-done | bytes 65568 | tf_op jit(solution)/shard_map/ppermute | solution.py:643
  100.7 2.9 %all-to-all-done.3 = bf16[640,2,128]{2,1,0:T(2,128)(2,1)S(1)} async-done(((bf16[640,2,128]{2,1,0:T(2,128)(2,1)}), bf16[640,2,128]{2,1,0:T(2,128)(2,1)S(1)}, u32[]{:S(2)}, u32[]{:S(2)}) %all-to-all-start.3) | async-done | bytes 327712 | tf_op jit(solution)/shard_map/all_to_all | solution.py:594
  103.5 0.8 unpack.1
  (35 shorter events, 0.1 us)
Async XLA Ops:
  0.6 14.4 %copy-start.15 = (f32[2,64]{1,0:T(2,128)S(1)}, f32[2,64]{1,0:T(2,128)}, u32[]{:S(2)}) copy-start(f32[2,64]{1,0:T(2,128)} %decay.3) | copy-start | bytes 1540
  0.6 14.4 %copy-start.16 = (f32[2,64]{1,0:T(2,128)S(1)}, f32[2,64]{1,0:T(2,128)}, u32[]{:S(2)}) copy-start(f32[2,64]{1,0:T(2,128)} %skip_gain.1) | copy-start | bytes 1540
  0.7 14.4 %copy-start.17 = (s32[16]{0:T(128)S(1)}, s32[16]{0:T(128)}, u32[]{:S(2)}) copy-start(s32[16]{0:T(128)} %param.22) | copy-start | bytes 196
  0.7 14.4 %copy-start.18 = (s32[16]{0:T(128)S(1)}, s32[16]{0:T(128)}, u32[]{:S(2)}) copy-start(s32[16]{0:T(128)} %param.23) | copy-start | bytes 196
  0.7 30.2 %copy-start.13 = (f32[40,128]{1,0:T(8,128)S(1)}, f32[40,128]{1,0:T(8,128)}, u32[]{:S(2)}) copy-start(f32[40,128]{1,0:T(8,128)} %constant.39.clone.pick_first) | copy-start | bytes 61444
  0.7 30.2 %copy-start.14 = (f32[40,128]{1,0:T(8,128)S(1)}, f32[40,128]{1,0:T(8,128)}, u32[]{:S(2)}) copy-start(f32[40,128]{1,0:T(8,128)} %constant.40.clone.pick_second) | copy-start | bytes 61444
  1.5 13.6 %copy-start.4 = (bf16[3,64,256]{2,1,0:T(8,128)(2,1)S(1)}, bf16[3,64,256]{2,1,0:T(8,128)(2,1)}, u32[]{:S(2)}) copy-start(bf16[3,64,256]{2,1,0:T(8,128)(2,1)} %param.24) | copy-start | bytes 294916
  1.5 13.6 %copy-start.6 = (bf16[256,64]{0,1:T(8,128)(2,1)S(1)}, bf16[256,64]{0,1:T(8,128)(2,1)}, u32[]{:S(2)}) copy-start(bf16[256,64]{0,1:T(8,128)(2,1)} %param.25) | copy-start | bytes 98308
  1.5 13.6 %copy-start.7 = (f32[33,64]{1,0:T(8,128)S(1)}, f32[33,64]{1,0:T(8,128)}, u32[]{:S(2)}) copy-start(f32[33,64]{1,0:T(8,128)} %filt_in.3) | copy-start | bytes 25348
  1.5 29.4 %copy-start.10 = (f32[128,128]{1,0:T(8,128)S(1)}, f32[128,128]{1,0:T(8,128)}, u32[]{:S(2)}) copy-start(f32[128,128]{1,0:T(8,128)} %constant.37.clone.wave_first) | copy-start | bytes 196612
  1.5 29.4 %copy-start.11 = (f32[128,128]{1,0:T(8,128)S(1)}, f32[128,128]{1,0:T(8,128)}, u32[]{:S(2)}) copy-start(f32[128,128]{1,0:T(8,128)} %constant.38.clone.wave_second) | copy-start | bytes 196612
  1.6 29.4 %copy-start.12 = (bf16[128,256]{1,0:T(8,128)(2,1)S(1)}, bf16[128,256]{1,0:T(8,128)(2,1)}, u32[]{:S(2)}) copy-start(bf16[128,256]{1,0:T(8,128)(2,1)} %constant.41.clone.factors) | copy-start | bytes 196612
  15.1 15.9 %copy-start = (bf16[512,512]{1,0:T(8,128)(2,1)S(1)}, bf16[512,512]{1,0:T(8,128)(2,1)}, u32[]{:S(2)}) copy-start(bf16[512,512]{1,0:T(8,128)(2,1)} %constant.33.clone.forward) | copy-start | bytes 1572868
  16.3 14.7 %copy-start.2 = (f32[128,256]{1,0:T(8,128)S(1)}, f32[128,256]{1,0:T(8,128)}, u32[]{:S(2)}) copy-start(f32[128,256]{1,0:T(8,128)} %constant.35.clone.twist_cos) | copy-start | bytes 393220
  16.3 14.7 %copy-start.3 = (f32[128,256]{1,0:T(8,128)S(1)}, f32[128,256]{1,0:T(8,128)}, u32[]{:S(2)}) copy-start(f32[128,256]{1,0:T(8,128)} %constant.36.clone.twist_sin) | copy-start | bytes 393220
  16.3 14.7 %copy-start.5 = (bf16[256,128]{1,0:T(8,128)(2,1)S(1)}, bf16[256,128]{1,0:T(8,128)(2,1)}, u32[]{:S(2)}) copy-start(bf16[256,128]{1,0:T(8,128)(2,1)} %constant.31.clone.analysis) | copy-start | bytes 196612
  16.3 14.7 %copy-start.8 = (f32[2,64,64]{2,1,0:T(8,128)S(1)}, f32[2,64,64]{2,1,0:T(8,128)}, u32[]{:S(2)}) copy-start(f32[2,64,64]{2,1,0:T(8,128)} %param.27) | copy-start | bytes 98308
  16.3 29.6 %all-to-all-start = ((bf16[256,4,128]{2,1,0:T(4,128)(2,1)}), bf16[256,4,128]{2,1,0:T(4,128)(2,1)S(1)}, u32[]{:S(2)}, u32[]{:S(2)}) async-start(bf16[256,4,128]{2,1,0:T(4,128)(2,1)} %bitcast.6), calls=%async_computation | async-start | bytes 524288 | tf_op jit(solution)/shard_map/all_to_all | solution.py:594
  31.0 14.9 %copy-start.1 = (bf16[512,512]{1,0:T(8,128)(2,1)S(1)}, bf16[512,512]{1,0:T(8,128)(2,1)}, u32[]{:S(2)}) copy-start(bf16[512,512]{1,0:T(8,128)(2,1)} %constant.34.clone.backward) | copy-start | bytes 1572868
  31.0 14.9 %copy-start.9 = (bf16[128,256]{1,0:T(8,128)(2,1)S(1)}, bf16[128,256]{1,0:T(8,128)(2,1)}, u32[]{:S(2)}) copy-start(bf16[128,256]{1,0:T(8,128)(2,1)} %constant.32.clone.synthesis) | copy-start | bytes 196612
  64.9 15.8 %all-to-all-start.2 = ((bf16[320,2,128]{2,1,0:T(2,128)(2,1)}), bf16[320,2,128]{2,1,0:T(2,128)(2,1)S(1)}, u32[]{:S(2)}, u32[]{:S(2)}) async-start(bf16[320,2,128]{2,1,0:T(2,128)(2,1)} %bitcast.11), calls=%async_computation.2 | async-start | bytes 327680 | tf_op jit(solution)/shard_map/all_to_all | solution.py:594
  70.7 3.2 %collective-permute-start = (bf16[256,256]{1,0:T(8,128)(2,1)S(1)}, bf16[256,256]{1,0:T(8,128)(2,1)S(1)}, u32[]{:S(2)}, u32[]{:S(2)}) collective-permute-start(bf16[256,256]{1,0:T(8,128)(2,1)S(1)} %get-tuple-element.44), channel_id=1, source_target_pairs={{0,1},{1,0},{2,3},{3,2},{4,5},{5,4},{6,7},{7,6},{8,9},{9,8},{10,11... | collective-permute-start | bytes 393224 | tf_op jit(solution)/shard_map/ppermute | solution.py:639
  81.5 22.0 %all-to-all-start.3 = ((bf16[640,2,128]{2,1,0:T(2,128)(2,1)}), bf16[640,2,128]{2,1,0:T(2,128)(2,1)S(1)}, u32[]{:S(2)}, u32[]{:S(2)}) async-start(bf16[640,2,128]{2,1,0:T(2,128)(2,1)} %bitcast.13), calls=%async_computation.3 | async-start | bytes 655360 | tf_op jit(solution)/shard_map/all_to_all | solution.py:594
  89.4 11.3 %collective-permute-start.1 = (bf16[128,256]{1,0:T(8,128)(2,1)S(1)}, bf16[128,256]{1,0:T(8,128)(2,1)S(1)}, u32[]{:S(2)}, u32[]{:S(2)}) collective-permute-start(bf16[128,256]{1,0:T(8,128)(2,1)S(1)} %get-tuple-element.48), channel_id=1, source_target_pairs={{0,2},{2,0},{1,3},{3,1},{4,6},{6,4},{5,7},{7,5},{8,10},{10,8},{9,1... | collective-permute-start | bytes 196616 | tf_op jit(solution)/shard_map/ppermute | solution.py:643

commit v8 on v7

--- a/solution.py
+++ b/solution.py
@@ -24,6 +24,7 @@
 CLIPS = 16
 SEND_ROWS = 8
 BACK_ROWS = 10
+SPARE = 16
 PART_ROWS = 10
 PARTS = 64
 
@@ -192,7 +193,7 @@
         scratch[pl.ds(6 + at, LOCAL, stride=SEND_ROWS), :] = jnp.broadcast_to(
             values.astype(F32), (LOCAL, 128)
         )
-    packed = scratch[...].astype(BF16)
+    packed = scratch[: LOCAL * SEND_ROWS, :].astype(BF16)
     send[: LOCAL * SEND_ROWS, :] = packed
     send[LOCAL * SEND_ROWS :, :] = packed
 
@@ -302,7 +303,7 @@
     skip_one = notes[2:3, :1]
     skip_two = notes[3:4, :1]
     role = notes[4:5, :1]
-    scratch[...] = received[...].astype(F32)
+    scratch[: received.shape[0], :] = received[...].astype(F32)
 
     def plane(row):
         return scratch[pl.ds(row, SEQ, stride=SEND_ROWS), :]
@@ -383,7 +384,7 @@
         packed[pl.ds(2 * at, PARTS, stride=BACK_ROWS), :] = values[:, :128]
         packed[pl.ds(2 * at + 1, PARTS, stride=BACK_ROWS), :] = values[:, 128:]
     skips[...] = jnp.broadcast_to(skip_row, (8, 128))
-    back[...] = packed[...].astype(BF16)
+    back[...] = packed[: back.shape[0], :].astype(BF16)
 
 
 def returned_signal(scratch, at):
@@ -395,7 +396,7 @@
     received, full, gate_in, grad_in, hidden, window, weights, gated_out, scaled_out,
     scratch, packed,
 ):
-    scratch[...] = received[...].astype(F32)
+    scratch[: received.shape[0], :] = received[...].astype(F32)
     carry = returned_signal(scratch, 0)
     gated = (gate_in[...] * carry).astype(BF16)
     scaled_grad = jnp.concatenate(
@@ -427,7 +428,7 @@
     rows += [out_weight[:, :128], out_weight[:, 128:], filter_grad, jnp.zeros((PARTS, 128), F32)]
     for at, values in enumerate(rows):
         packed[pl.ds(at, PARTS, stride=PART_ROWS), :] = values
-    weights[...] = packed[...].astype(BF16)
+    weights[...] = packed[: weights.shape[0], :].astype(BF16)
 
 
 def channel_kernel(place, gated, scaled_grad, in_proj, out_proj, given, kept):
@@ -469,7 +470,7 @@
     summed = (left[...] + over_chips[...].astype(F32)).astype(BF16)
     mixed[...] = summed[:64, :]
     grad_inputs[...] = summed[64:, :]
-    scratch[...] = received[...].astype(F32)
+    scratch[: received.shape[0], :] = received[...].astype(F32)
 
     def block(at):
         first = scratch[pl.ds(at, PARTS, stride=PART_ROWS), :]
@@ -489,7 +490,7 @@
     skip_grad[...] = dot(pick, skips, ((1,), (1,)))[:2, :] * TOTAL ** (-0.5)
 
 
-def call(kernel, name, outs, scalars, arrays, scratch=()):
+def call(kernel, name, outs, scalars, arrays, scratch=(), spare=SPARE):
     def vmem():
         return pl.BlockSpec(memory_space=pltpu.VMEM)
 
@@ -499,7 +500,9 @@
         out_shape=[jax.ShapeDtypeStruct(shape, kind) for shape, kind in outs],
         in_specs=[pl.BlockSpec(memory_space=pltpu.SMEM)] * scalars + [vmem() for _ in range(arrays)],
         out_specs=[vmem() for _ in outs],
-        scratch_shapes=[pltpu.VMEM(shape, F32) for shape in scratch],
+        scratch_shapes=[
+            pltpu.VMEM((*shape[:-2], shape[-2] + spare, shape[-1]), F32) for shape in scratch
+        ],
         compiler_params=pltpu.CompilerParams(vmem_limit_bytes=32 * 1024 * 1024),
     )
 
@@ -530,6 +533,7 @@
         1,
         12,
         [(8 * HIDDEN, 128)] * 4 + [(2, SEQ, CHUNK)],
+        spare=0,
     )
 
 

time: 105 us -> 105 us (level)
  no operation moved by 1% of the time
where the time goes in v8:
time: 105 us; the launch traced here: 104 us
  starting transfers between devices  36.8 us (35%)
  blocking collectives  29.3 us (28%)
  waiting for transfers between devices  20.7 us (20%)
  Pallas kernels  15.7 us (15%)
    all_to_all x3, starting transfers between devices, swap(): lax.all_to_all(tiles, 'seq', split_axis=0, concat_axis=0, axis_index_grou...  28 us
    all_to_all x1, blocking collectives, swap(): lax.all_to_all(tiles, 'seq', split_axis=0, concat_axis=0, axis_index_grou...  15.8 us
    all_to_all x3, waiting for transfers between devices, swap(): lax.all_to_all(tiles, 'seq', split_axis=0, concat_axis=0, axis_index_grou...  15 us
    all_gather x1, blocking collectives, shards(): lax.all_gather(jnp.concatenate([inputs, cotangent], 0), 'ch', axis=0, til...  13.5 us
    pallas_call x1, Pallas kernels, shards(): filtering()  9.46 us
    ppermute x1, starting transfers between devices, shards(): over_chips = lax.ppermute(given, 'ch', [(0, 2), (2, 0), (1, 3), (3, 1)])  6.92 us
    ppermute x1, waiting for transfers between devices, shards(): over_chips = lax.ppermute(given, 'ch', [(0, 2), (2, 0), (1, 3), (3, 1)])  4.3 us
    pallas_call x1, Pallas kernels, shards(): series()  2.17 us
  transfers between devices with their start and end apart: 5, of which 5 were waited for; matrix products, arithmetic and copies ran while one was open for 0% of the time, Pallas kernels for 9%

profile of v8, /device:TPU:8, one launch (start us, length us, event | category | flops | bytes accessed | tf_op | source)
XLA Modules:
  0.0 104.4 jit_solution(11162031783009171855)
XLA Ops:
  0.7 0.0 copy-start.13
  0.7 0.0 copy-start.14
  0.7 0.8 pad_maximum_fusion
  1.5 0.0 copy-start.10
  1.5 0.0 copy-start.11
  1.6 13.5 %all_gather.3.full = bf16[512,256]{1,0:T(8,128)(2,1)S(1)} all-gather(bf16[128,256]{1,0:T(8,128)(2,1)S(1)} %pad_maximum_fusion), channel_id=1, replica_groups=mesh['seq'=128,'ch'=4] {'ch'}, dimensions={0}, use_global_device_ids=true | all-gather | bytes 327680 | tf_op jit(solution)/shard_map/all_gather | solution.py:622
  15.1 1.1 %project.1 = (bf16[1024,128]{1,0:T(8,128)(2,1)}, f32[64,256]{1,0:T(8,128)S(1)}, f32[64,256]{1,0:T(8,128)S(1)}, f32[64,256]{1,0:T(8,128)S(1)}, f32[128,256]{1,0:T(8,128)S(1)}, /*index=5*/f32[8,128]{1,0:T(8,128)S(1)}) custom-call(s32[1]{0:T(128)} %bitcast.rank, s32[1,16]{1,0:T(1,128)S(1)} %bitcast.28, s32[1,16]{1,0:T(1,128)S(1)} %bitcast.29, ...), custom_call_target="tpu_custom_call" | custom-call | tf_op jit(solution)/shard_map/project/pallas_call | solution.py:623
  16.3 14.6 %all-to-all-start = ((bf16[256,4,128]{2,1,0:T(4,128)(2,1)}), bf16[256,4,128]{2,1,0:T(4,128)(2,1)S(1)}, u32[]{:S(2)}, u32[]{:S(2)}) async-start(bf16[256,4,128]{2,1,0:T(4,128)(2,1)} %bitcast.6), calls=%async_computation | async-start | bytes 524288 | tf_op jit(solution)/shard_map/all_to_all | solution.py:598
  31.0 9.5 %filters.1 = f32[256,512]{1,0:T(8,128)S(1)} custom-call(s32[1]{0:T(128)} %bitcast.rank, f32[33,64]{1,0:T(8,128)S(1)} %copy-done.7, f32[128,64]{1,0:T(8,128)S(1)} %bitcast.27, f32[2,64]{1,0:T(2,128)S(1)} %copy-done.15, f32[128,128]{1,0:T(8,128)S(1)} %copy-done.10, f32[128,128]{1,0:T(8,128)S(1)} %copy-done.11, f32[40,128]{1,0:T(8,128)S(1)} %copy-done.13, ...), custom_call_target="tpu_custom_call" | custom-call | tf_op jit(solution)/shard_map/filters/pallas_call | solution.py:631
  40.5 5.4 %all-to-all-done = bf16[256,4,128]{2,1,0:T(4,128)(2,1)S(1)} async-done(((bf16[256,4,128]{2,1,0:T(4,128)(2,1)}), bf16[256,4,128]{2,1,0:T(4,128)(2,1)S(1)}, u32[]{:S(2)}, u32[]{:S(2)}) %all-to-all-start) | async-done | bytes 262176 | tf_op jit(solution)/shard_map/all_to_all | solution.py:598
  45.9 2.2 %convolve.1 = (bf16[640,128]{1,0:T(8,128)(2,1)S(1)}, f32[8,128]{1,0:T(8,128)S(1)}) custom-call(f32[8,128]{1,0:T(8,128)S(1)} %get-tuple-element.32.notes, bf16[1024,128]{1,0:T(8,128)(2,1)S(1)} %bitcast.19, f32[256,512]{1,0:T(8,128)S(1)} %filters.1, bf16[256,128]{1,0:T(8,128)(2,1)S(1)} %copy-done.5, bf16[128,256]{1,0:T(8,128)(2,1)S(1)} %copy-done.9, ...), custom_call_target="tpu_custom_call" | custom-call | tf_op jit(solution)/shard_map/convolve/pallas_call | solution.py:635
  48.0 15.8 %all_to_all.20 = bf16[320,2,128]{2,1,0:T(2,128)(2,1)S(1)} all-to-all(bf16[320,2,128]{2,1,0:T(2,128)(2,1)S(1)} %bitcast.24), channel_id=1, replica_groups={{0,4,8,12,16,20,24,28,32,36,40,44,48,52,56,60,64,68,72,76,80,84,88,92,9..., dimensions={0} | all-to-all | bytes 327680 | tf_op jit(solution)/shard_map/all_to_all | solution.py:598
  63.9 1.1 %weigh.1 = (bf16[640,128]{1,0:T(8,128)(2,1)}, bf16[64,256]{1,0:T(8,128)(2,1)S(1)}, bf16[192,256]{1,0:T(8,128)(2,1)S(1)}) custom-call(bf16[640,128]{1,0:T(8,128)(2,1)S(1)} %bitcast.21, bf16[512,256]{1,0:T(8,128)(2,1)S(1)} %all_gather.3.full, f32[64,256]{1,0:T(8,128)S(1)} %get-tuple-element.35.gate_in, f32[64,256]{1,0:T(8,128)S(1)} %get-tuple-element.36.grad_in, ...), custom_call_target="tpu_custom_call" | custom-call | tf_op jit(solution)/shard_map/weigh/pallas_call | solution.py:639
  64.9 5.5 %all-to-all-start.2 = ((bf16[320,2,128]{2,1,0:T(2,128)(2,1)}), bf16[320,2,128]{2,1,0:T(2,128)(2,1)S(1)}, u32[]{:S(2)}, u32[]{:S(2)}) async-start(bf16[320,2,128]{2,1,0:T(2,128)(2,1)} %bitcast.11), calls=%async_computation.2 | async-start | bytes 327680 | tf_op jit(solution)/shard_map/all_to_all | solution.py:598
  70.4 0.3 mix.1
  70.7 1.9 %collective-permute-start = (bf16[256,256]{1,0:T(8,128)(2,1)S(1)}, bf16[256,256]{1,0:T(8,128)(2,1)S(1)}, u32[]{:S(2)}, u32[]{:S(2)}) collective-permute-start(bf16[256,256]{1,0:T(8,128)(2,1)S(1)} %get-tuple-element.44), channel_id=1, source_target_pairs={{0,1},{1,0},{2,3},{3,2},{4,5},{5,4},{6,7},{7,6},{8,9},{9,8},{10,11... | collective-permute-start | bytes 393224 | tf_op jit(solution)/shard_map/ppermute | solution.py:643
  72.6 1.3 %collective-permute-done.received = bf16[256,256]{1,0:T(8,128)(2,1)S(1)} collective-permute-done((bf16[256,256]{1,0:T(8,128)(2,1)S(1)}, bf16[256,256]{1,0:T(8,128)(2,1)S(1)}, u32[]{:S(2)}, u32[]{:S(2)}) %collective-permute-start) | collective-permute-done | bytes 131104 | tf_op jit(solution)/shard_map/ppermute | solution.py:643
  74.0 6.8 %all-to-all-done.2 = bf16[320,2,128]{2,1,0:T(2,128)(2,1)S(1)} async-done(((bf16[320,2,128]{2,1,0:T(2,128)(2,1)}), bf16[320,2,128]{2,1,0:T(2,128)(2,1)S(1)}, u32[]{:S(2)}, u32[]{:S(2)}) %all-to-all-start.2) | async-done | bytes 163872 | tf_op jit(solution)/shard_map/all_to_all | solution.py:598
  80.8 0.8 add_up.1
  81.5 7.9 %all-to-all-start.3 = ((bf16[640,2,128]{2,1,0:T(2,128)(2,1)}), bf16[640,2,128]{2,1,0:T(2,128)(2,1)S(1)}, u32[]{:S(2)}, u32[]{:S(2)}) async-start(bf16[640,2,128]{2,1,0:T(2,128)(2,1)} %bitcast.13), calls=%async_computation.3 | async-start | bytes 655360 | tf_op jit(solution)/shard_map/all_to_all | solution.py:598
  89.4 6.9 %collective-permute-start.1 = (bf16[128,256]{1,0:T(8,128)(2,1)S(1)}, bf16[128,256]{1,0:T(8,128)(2,1)S(1)}, u32[]{:S(2)}, u32[]{:S(2)}) collective-permute-start(bf16[128,256]{1,0:T(8,128)(2,1)S(1)} %get-tuple-element.48), channel_id=1, source_target_pairs={{0,2},{2,0},{1,3},{3,1},{4,6},{6,4},{5,7},{7,5},{8,10},{10,8},{9,1... | collective-permute-start | bytes 196616 | tf_op jit(solution)/shard_map/ppermute | solution.py:647
  96.3 4.3 %collective-permute-done.1.over_chips = bf16[128,256]{1,0:T(8,128)(2,1)S(1)} collective-permute-done((bf16[128,256]{1,0:T(8,128)(2,1)S(1)}, bf16[128,256]{1,0:T(8,128)(2,1)S(1)}, u32[]{:S(2)}, u32[]{:S(2)}) %collective-permute-start.1) | collective-permute-done | bytes 65568 | tf_op jit(solution)/shard_map/ppermute | solution.py:647
  100.7 2.9 %all-to-all-done.3 = bf16[640,2,128]{2,1,0:T(2,128)(2,1)S(1)} async-done(((bf16[640,2,128]{2,1,0:T(2,128)(2,1)}), bf16[640,2,128]{2,1,0:T(2,128)(2,1)S(1)}, u32[]{:S(2)}, u32[]{:S(2)}) %all-to-all-start.3) | async-done | bytes 327712 | tf_op jit(solution)/shard_map/all_to_all | solution.py:598
  103.6 0.8 unpack.1
  (35 shorter events, 0.1 us)
Async XLA Ops:
  0.6 14.4 %copy-start.15 = (f32[2,64]{1,0:T(2,128)S(1)}, f32[2,64]{1,0:T(2,128)}, u32[]{:S(2)}) copy-start(f32[2,64]{1,0:T(2,128)} %decay.3) | copy-start | bytes 1540
  0.6 14.4 %copy-start.16 = (f32[2,64]{1,0:T(2,128)S(1)}, f32[2,64]{1,0:T(2,128)}, u32[]{:S(2)}) copy-start(f32[2,64]{1,0:T(2,128)} %skip_gain.1) | copy-start | bytes 1540
  0.7 14.4 %copy-start.17 = (s32[16]{0:T(128)S(1)}, s32[16]{0:T(128)}, u32[]{:S(2)}) copy-start(s32[16]{0:T(128)} %param.22) | copy-start | bytes 196
  0.7 14.4 %copy-start.18 = (s32[16]{0:T(128)S(1)}, s32[16]{0:T(128)}, u32[]{:S(2)}) copy-start(s32[16]{0:T(128)} %param.23) | copy-start | bytes 196
  0.7 30.2 %copy-start.13 = (f32[40,128]{1,0:T(8,128)S(1)}, f32[40,128]{1,0:T(8,128)}, u32[]{:S(2)}) copy-start(f32[40,128]{1,0:T(8,128)} %constant.39.clone.pick_first) | copy-start | bytes 61444
  0.7 30.2 %copy-start.14 = (f32[40,128]{1,0:T(8,128)S(1)}, f32[40,128]{1,0:T(8,128)}, u32[]{:S(2)}) copy-start(f32[40,128]{1,0:T(8,128)} %constant.40.clone.pick_second) | copy-start | bytes 61444
  1.5 13.6 %copy-start.4 = (bf16[3,64,256]{2,1,0:T(8,128)(2,1)S(1)}, bf16[3,64,256]{2,1,0:T(8,128)(2,1)}, u32[]{:S(2)}) copy-start(bf16[3,64,256]{2,1,0:T(8,128)(2,1)} %param.24) | copy-start | bytes 294916
  1.5 13.6 %copy-start.6 = (bf16[256,64]{0,1:T(8,128)(2,1)S(1)}, bf16[256,64]{0,1:T(8,128)(2,1)}, u32[]{:S(2)}) copy-start(bf16[256,64]{0,1:T(8,128)(2,1)} %param.25) | copy-start | bytes 98308
  1.5 13.6 %copy-start.7 = (f32[33,64]{1,0:T(8,128)S(1)}, f32[33,64]{1,0:T(8,128)}, u32[]{:S(2)}) copy-start(f32[33,64]{1,0:T(8,128)} %filt_in.3) | copy-start | bytes 25348
  1.5 29.4 %copy-start.10 = (f32[128,128]{1,0:T(8,128)S(1)}, f32[128,128]{1,0:T(8,128)}, u32[]{:S(2)}) copy-start(f32[128,128]{1,0:T(8,128)} %constant.37.clone.wave_first) | copy-start | bytes 196612
  1.5 29.4 %copy-start.11 = (f32[128,128]{1,0:T(8,128)S(1)}, f32[128,128]{1,0:T(8,128)}, u32[]{:S(2)}) copy-start(f32[128,128]{1,0:T(8,128)} %constant.38.clone.wave_second) | copy-start | bytes 196612
  1.6 29.4 %copy-start.12 = (bf16[128,256]{1,0:T(8,128)(2,1)S(1)}, bf16[128,256]{1,0:T(8,128)(2,1)}, u32[]{:S(2)}) copy-start(bf16[128,256]{1,0:T(8,128)(2,1)} %constant.41.clone.factors) | copy-start | bytes 196612
  15.1 15.9 %copy-start = (bf16[512,512]{1,0:T(8,128)(2,1)S(1)}, bf16[512,512]{1,0:T(8,128)(2,1)}, u32[]{:S(2)}) copy-start(bf16[512,512]{1,0:T(8,128)(2,1)} %constant.33.clone.forward) | copy-start | bytes 1572868
  16.3 14.7 %copy-start.2 = (f32[128,256]{1,0:T(8,128)S(1)}, f32[128,256]{1,0:T(8,128)}, u32[]{:S(2)}) copy-start(f32[128,256]{1,0:T(8,128)} %constant.35.clone.twist_cos) | copy-start | bytes 393220
  16.3 14.7 %copy-start.3 = (f32[128,256]{1,0:T(8,128)S(1)}, f32[128,256]{1,0:T(8,128)}, u32[]{:S(2)}) copy-start(f32[128,256]{1,0:T(8,128)} %constant.36.clone.twist_sin) | copy-start | bytes 393220
  16.3 14.7 %copy-start.5 = (bf16[256,128]{1,0:T(8,128)(2,1)S(1)}, bf16[256,128]{1,0:T(8,128)(2,1)}, u32[]{:S(2)}) copy-start(bf16[256,128]{1,0:T(8,128)(2,1)} %constant.31.clone.analysis) | copy-start | bytes 196612
  16.3 14.7 %copy-start.8 = (f32[2,64,64]{2,1,0:T(8,128)S(1)}, f32[2,64,64]{2,1,0:T(8,128)}, u32[]{:S(2)}) copy-start(f32[2,64,64]{2,1,0:T(8,128)} %param.27) | copy-start | bytes 98308
  16.3 29.6 %all-to-all-start = ((bf16[256,4,128]{2,1,0:T(4,128)(2,1)}), bf16[256,4,128]{2,1,0:T(4,128)(2,1)S(1)}, u32[]{:S(2)}, u32[]{:S(2)}) async-start(bf16[256,4,128]{2,1,0:T(4,128)(2,1)} %bitcast.6), calls=%async_computation | async-start | bytes 524288 | tf_op jit(solution)/shard_map/all_to_all | solution.py:598
  31.0 14.9 %copy-start.1 = (bf16[512,512]{1,0:T(8,128)(2,1)S(1)}, bf16[512,512]{1,0:T(8,128)(2,1)}, u32[]{:S(2)}) copy-start(bf16[512,512]{1,0:T(8,128)(2,1)} %constant.34.clone.backward) | copy-start | bytes 1572868
  31.0 14.9 %copy-start.9 = (bf16[128,256]{1,0:T(8,128)(2,1)S(1)}, bf16[128,256]{1,0:T(8,128)(2,1)}, u32[]{:S(2)}) copy-start(bf16[128,256]{1,0:T(8,128)(2,1)} %constant.32.clone.synthesis) | copy-start | bytes 196612
  64.9 15.8 %all-to-all-start.2 = ((bf16[320,2,128]{2,1,0:T(2,128)(2,1)}), bf16[320,2,128]{2,1,0:T(2,128)(2,1)S(1)}, u32[]{:S(2)}, u32[]{:S(2)}) async-start(bf16[320,2,128]{2,1,0:T(2,128)(2,1)} %bitcast.11), calls=%async_computation.2 | async-start | bytes 327680 | tf_op jit(solution)/shard_map/all_to_all | solution.py:598
  70.7 3.2 %collective-permute-start = (bf16[256,256]{1,0:T(8,128)(2,1)S(1)}, bf16[256,256]{1,0:T(8,128)(2,1)S(1)}, u32[]{:S(2)}, u32[]{:S(2)}) collective-permute-start(bf16[256,256]{1,0:T(8,128)(2,1)S(1)} %get-tuple-element.44), channel_id=1, source_target_pairs={{0,1},{1,0},{2,3},{3,2},{4,5},{5,4},{6,7},{7,6},{8,9},{9,8},{10,11... | collective-permute-start | bytes 393224 | tf_op jit(solution)/shard_map/ppermute | solution.py:643
  81.5 22.0 %all-to-all-start.3 = ((bf16[640,2,128]{2,1,0:T(2,128)(2,1)}), bf16[640,2,128]{2,1,0:T(2,128)(2,1)S(1)}, u32[]{:S(2)}, u32[]{:S(2)}) async-start(bf16[640,2,128]{2,1,0:T(2,128)(2,1)} %bitcast.13), calls=%async_computation.3 | async-start | bytes 655360 | tf_op jit(solution)/shard_map/all_to_all | solution.py:598
  89.4 11.2 %collective-permute-start.1 = (bf16[128,256]{1,0:T(8,128)(2,1)S(1)}, bf16[128,256]{1,0:T(8,128)(2,1)S(1)}, u32[]{:S(2)}, u32[]{:S(2)}) collective-permute-start(bf16[128,256]{1,0:T(8,128)(2,1)S(1)} %get-tuple-element.48), channel_id=1, source_target_pairs={{0,2},{2,0},{1,3},{3,1},{4,6},{6,4},{5,7},{7,5},{8,10},{10,8},{9,1... | collective-permute-start | bytes 196616 | tf_op jit(solution)/shard_map/ppermute | solution.py:647

commit v9 on v8

--- a/solution.py
+++ b/solution.py
@@ -280,7 +280,7 @@
             shapes[i, rows, :] = jnp.sum(product.reshape(HIDDEN, 8, CHUNK), 0)
         return carry
 
-    lax.fori_loop(0, SEQ // 8, block, 0)
+    lax.fori_loop(0, SEQ // 8, block, 0, unroll=2)
     time = lax.broadcasted_iota(jnp.int32, (SEQ, CHUNK), 0) * CHUNK + lax.broadcasted_iota(
         jnp.int32, (SEQ, CHUNK), 1
     )

time: 105 us -> 104 us (level)
  no operation moved by 1% of the time
where the time goes in v9:
time: 104 us; the launch traced here: 103 us
  starting transfers between devices  36.5 us (35%)
  blocking collectives  28.8 us (28%)
  waiting for transfers between devices  21.4 us (21%)
  Pallas kernels  14.7 us (14%)
    all_to_all x3, starting transfers between devices, swap(): lax.all_to_all(tiles, 'seq', split_axis=0, concat_axis=0, axis_index_grou...  27.7 us
    all_to_all x3, waiting for transfers between devices, swap(): lax.all_to_all(tiles, 'seq', split_axis=0, concat_axis=0, axis_index_grou...  15.8 us
    all_to_all x1, blocking collectives, swap(): lax.all_to_all(tiles, 'seq', split_axis=0, concat_axis=0, axis_index_grou...  15.3 us
    all_gather x1, blocking collectives, shards(): lax.all_gather(jnp.concatenate([inputs, cotangent], 0), 'ch', axis=0, til...  13.5 us
    pallas_call x1, Pallas kernels, shards(): filtering()  8.48 us
    ppermute x1, starting transfers between devices, shards(): over_chips = lax.ppermute(given, 'ch', [(0, 2), (2, 0), (1, 3), (3, 1)])  6.91 us
    ppermute x1, waiting for transfers between devices, shards(): over_chips = lax.ppermute(given, 'ch', [(0, 2), (2, 0), (1, 3), (3, 1)])  4.19 us
    pallas_call x1, Pallas kernels, shards(): series()  2.17 us
  transfers between devices with their start and end apart: 5, of which 5 were waited for; matrix products, arithmetic and copies ran while one was open for 0% of the time, Pallas kernels for 9%

profile of v9, /device:TPU:8, one launch (start us, length us, event | category | flops | bytes accessed | tf_op | source)
XLA Modules:
  0.0 103.2 jit_solution(13413687831421506333)
XLA Ops:
  0.7 0.0 copy-start.14
  0.7 0.8 pad_maximum_fusion
  1.5 0.0 copy-start.10
  1.5 0.0 copy-start.11
  1.6 0.0 copy-start.12
  1.6 13.5 %all_gather.3.full = bf16[512,256]{1,0:T(8,128)(2,1)S(1)} all-gather(bf16[128,256]{1,0:T(8,128)(2,1)S(1)} %pad_maximum_fusion), channel_id=1, replica_groups=mesh['seq'=128,'ch'=4] {'ch'}, dimensions={0}, use_global_device_ids=true | all-gather | bytes 327680 | tf_op jit(solution)/shard_map/all_gather | solution.py:622
  15.1 1.1 %project.1 = (bf16[1024,128]{1,0:T(8,128)(2,1)}, f32[64,256]{1,0:T(8,128)S(1)}, f32[64,256]{1,0:T(8,128)S(1)}, f32[64,256]{1,0:T(8,128)S(1)}, f32[128,256]{1,0:T(8,128)S(1)}, /*index=5*/f32[8,128]{1,0:T(8,128)S(1)}) custom-call(s32[1]{0:T(128)} %bitcast.rank, s32[1,16]{1,0:T(1,128)S(1)} %bitcast.28, s32[1,16]{1,0:T(1,128)S(1)} %bitcast.29, ...), custom_call_target="tpu_custom_call" | custom-call | tf_op jit(solution)/shard_map/project/pallas_call | solution.py:623
  16.3 14.6 %all-to-all-start = ((bf16[256,4,128]{2,1,0:T(4,128)(2,1)}), bf16[256,4,128]{2,1,0:T(4,128)(2,1)S(1)}, u32[]{:S(2)}, u32[]{:S(2)}) async-start(bf16[256,4,128]{2,1,0:T(4,128)(2,1)} %bitcast.6), calls=%async_computation | async-start | bytes 524288 | tf_op jit(solution)/shard_map/all_to_all | solution.py:598
  31.0 8.5 %filters.1 = f32[256,512]{1,0:T(8,128)S(1)} custom-call(s32[1]{0:T(128)} %bitcast.rank, f32[33,64]{1,0:T(8,128)S(1)} %copy-done.7, f32[128,64]{1,0:T(8,128)S(1)} %bitcast.27, f32[2,64]{1,0:T(2,128)S(1)} %copy-done.15, f32[128,128]{1,0:T(8,128)S(1)} %copy-done.10, f32[128,128]{1,0:T(8,128)S(1)} %copy-done.11, f32[40,128]{1,0:T(8,128)S(1)} %copy-done.13, ...), custom_call_target="tpu_custom_call" | custom-call | tf_op jit(solution)/shard_map/filters/pallas_call | solution.py:631
  39.5 6.4 %all-to-all-done = bf16[256,4,128]{2,1,0:T(4,128)(2,1)S(1)} async-done(((bf16[256,4,128]{2,1,0:T(4,128)(2,1)}), bf16[256,4,128]{2,1,0:T(4,128)(2,1)S(1)}, u32[]{:S(2)}, u32[]{:S(2)}) %all-to-all-start) | async-done | bytes 262176 | tf_op jit(solution)/shard_map/all_to_all | solution.py:598
  45.9 2.2 %convolve.1 = (bf16[640,128]{1,0:T(8,128)(2,1)S(1)}, f32[8,128]{1,0:T(8,128)S(1)}) custom-call(f32[8,128]{1,0:T(8,128)S(1)} %get-tuple-element.32.notes, bf16[1024,128]{1,0:T(8,128)(2,1)S(1)} %bitcast.19, f32[256,512]{1,0:T(8,128)S(1)} %filters.1, bf16[256,128]{1,0:T(8,128)(2,1)S(1)} %copy-done.5, bf16[128,256]{1,0:T(8,128)(2,1)S(1)} %copy-done.9, ...), custom_call_target="tpu_custom_call" | custom-call | tf_op jit(solution)/shard_map/convolve/pallas_call | solution.py:635
  48.0 15.3 %all_to_all.20 = bf16[320,2,128]{2,1,0:T(2,128)(2,1)S(1)} all-to-all(bf16[320,2,128]{2,1,0:T(2,128)(2,1)S(1)} %bitcast.24), channel_id=1, replica_groups={{0,4,8,12,16,20,24,28,32,36,40,44,48,52,56,60,64,68,72,76,80,84,88,92,9..., dimensions={0} | all-to-all | bytes 327680 | tf_op jit(solution)/shard_map/all_to_all | solution.py:598
  63.3 1.1 %weigh.1 = (bf16[640,128]{1,0:T(8,128)(2,1)}, bf16[64,256]{1,0:T(8,128)(2,1)S(1)}, bf16[192,256]{1,0:T(8,128)(2,1)S(1)}) custom-call(bf16[640,128]{1,0:T(8,128)(2,1)S(1)} %bitcast.21, bf16[512,256]{1,0:T(8,128)(2,1)S(1)} %all_gather.3.full, f32[64,256]{1,0:T(8,128)S(1)} %get-tuple-element.35.gate_in, f32[64,256]{1,0:T(8,128)S(1)} %get-tuple-element.36.grad_in, ...), custom_call_target="tpu_custom_call" | custom-call | tf_op jit(solution)/shard_map/weigh/pallas_call | solution.py:639
  64.4 5.2 %all-to-all-start.2 = ((bf16[320,2,128]{2,1,0:T(2,128)(2,1)}), bf16[320,2,128]{2,1,0:T(2,128)(2,1)S(1)}, u32[]{:S(2)}, u32[]{:S(2)}) async-start(bf16[320,2,128]{2,1,0:T(2,128)(2,1)} %bitcast.11), calls=%async_computation.2 | async-start | bytes 327680 | tf_op jit(solution)/shard_map/all_to_all | solution.py:598
  69.6 0.3 mix.1
  69.9 1.9 %collective-permute-start = (bf16[256,256]{1,0:T(8,128)(2,1)S(1)}, bf16[256,256]{1,0:T(8,128)(2,1)S(1)}, u32[]{:S(2)}, u32[]{:S(2)}) collective-permute-start(bf16[256,256]{1,0:T(8,128)(2,1)S(1)} %get-tuple-element.44), channel_id=1, source_target_pairs={{0,1},{1,0},{2,3},{3,2},{4,5},{5,4},{6,7},{7,6},{8,9},{9,8},{10,11... | collective-permute-start | bytes 393224 | tf_op jit(solution)/shard_map/ppermute | solution.py:643
  71.8 1.3 %collective-permute-done.received = bf16[256,256]{1,0:T(8,128)(2,1)S(1)} collective-permute-done((bf16[256,256]{1,0:T(8,128)(2,1)S(1)}, bf16[256,256]{1,0:T(8,128)(2,1)S(1)}, u32[]{:S(2)}, u32[]{:S(2)}) %collective-permute-start) | collective-permute-done | bytes 131104 | tf_op jit(solution)/shard_map/ppermute | solution.py:643
  73.2 6.8 %all-to-all-done.2 = bf16[320,2,128]{2,1,0:T(2,128)(2,1)S(1)} async-done(((bf16[320,2,128]{2,1,0:T(2,128)(2,1)}), bf16[320,2,128]{2,1,0:T(2,128)(2,1)S(1)}, u32[]{:S(2)}, u32[]{:S(2)}) %all-to-all-start.2) | async-done | bytes 163872 | tf_op jit(solution)/shard_map/all_to_all | solution.py:598
  80.0 0.8 add_up.1
  80.7 7.8 %all-to-all-start.3 = ((bf16[640,2,128]{2,1,0:T(2,128)(2,1)}), bf16[640,2,128]{2,1,0:T(2,128)(2,1)S(1)}, u32[]{:S(2)}, u32[]{:S(2)}) async-start(bf16[640,2,128]{2,1,0:T(2,128)(2,1)} %bitcast.13), calls=%async_computation.3 | async-start | bytes 655360 | tf_op jit(solution)/shard_map/all_to_all | solution.py:598
  88.6 6.9 %collective-permute-start.1 = (bf16[128,256]{1,0:T(8,128)(2,1)S(1)}, bf16[128,256]{1,0:T(8,128)(2,1)S(1)}, u32[]{:S(2)}, u32[]{:S(2)}) collective-permute-start(bf16[128,256]{1,0:T(8,128)(2,1)S(1)} %get-tuple-element.48), channel_id=1, source_target_pairs={{0,2},{2,0},{1,3},{3,1},{4,6},{6,4},{5,7},{7,5},{8,10},{10,8},{9,1... | collective-permute-start | bytes 196616 | tf_op jit(solution)/shard_map/ppermute | solution.py:647
  95.5 4.2 %collective-permute-done.1.over_chips = bf16[128,256]{1,0:T(8,128)(2,1)S(1)} collective-permute-done((bf16[128,256]{1,0:T(8,128)(2,1)S(1)}, bf16[128,256]{1,0:T(8,128)(2,1)S(1)}, u32[]{:S(2)}, u32[]{:S(2)}) %collective-permute-start.1) | collective-permute-done | bytes 65568 | tf_op jit(solution)/shard_map/ppermute | solution.py:647
  99.7 2.7 %all-to-all-done.3 = bf16[640,2,128]{2,1,0:T(2,128)(2,1)S(1)} async-done(((bf16[640,2,128]{2,1,0:T(2,128)(2,1)}), bf16[640,2,128]{2,1,0:T(2,128)(2,1)S(1)}, u32[]{:S(2)}, u32[]{:S(2)}) %all-to-all-start.3) | async-done | bytes 327712 | tf_op jit(solution)/shard_map/all_to_all | solution.py:598
  102.4 0.8 unpack.1
  (35 shorter events, 0.1 us)
Async XLA Ops:
  0.6 14.4 %copy-start.15 = (f32[2,64]{1,0:T(2,128)S(1)}, f32[2,64]{1,0:T(2,128)}, u32[]{:S(2)}) copy-start(f32[2,64]{1,0:T(2,128)} %decay.3) | copy-start | bytes 1540
  0.6 14.4 %copy-start.16 = (f32[2,64]{1,0:T(2,128)S(1)}, f32[2,64]{1,0:T(2,128)}, u32[]{:S(2)}) copy-start(f32[2,64]{1,0:T(2,128)} %skip_gain.1) | copy-start | bytes 1540
  0.7 14.4 %copy-start.17 = (s32[16]{0:T(128)S(1)}, s32[16]{0:T(128)}, u32[]{:S(2)}) copy-start(s32[16]{0:T(128)} %param.22) | copy-start | bytes 196
  0.7 14.4 %copy-start.18 = (s32[16]{0:T(128)S(1)}, s32[16]{0:T(128)}, u32[]{:S(2)}) copy-start(s32[16]{0:T(128)} %param.23) | copy-start | bytes 196
  0.7 30.2 %copy-start.13 = (f32[40,128]{1,0:T(8,128)S(1)}, f32[40,128]{1,0:T(8,128)}, u32[]{:S(2)}) copy-start(f32[40,128]{1,0:T(8,128)} %constant.39.clone.pick_first) | copy-start | bytes 61444
  0.7 30.2 %copy-start.14 = (f32[40,128]{1,0:T(8,128)S(1)}, f32[40,128]{1,0:T(8,128)}, u32[]{:S(2)}) copy-start(f32[40,128]{1,0:T(8,128)} %constant.40.clone.pick_second) | copy-start | bytes 61444
  1.5 13.6 %copy-start.4 = (bf16[3,64,256]{2,1,0:T(8,128)(2,1)S(1)}, bf16[3,64,256]{2,1,0:T(8,128)(2,1)}, u32[]{:S(2)}) copy-start(bf16[3,64,256]{2,1,0:T(8,128)(2,1)} %param.24) | copy-start | bytes 294916
  1.5 13.6 %copy-start.6 = (bf16[256,64]{0,1:T(8,128)(2,1)S(1)}, bf16[256,64]{0,1:T(8,128)(2,1)}, u32[]{:S(2)}) copy-start(bf16[256,64]{0,1:T(8,128)(2,1)} %param.25) | copy-start | bytes 98308
  1.5 13.6 %copy-start.7 = (f32[33,64]{1,0:T(8,128)S(1)}, f32[33,64]{1,0:T(8,128)}, u32[]{:S(2)}) copy-start(f32[33,64]{1,0:T(8,128)} %filt_in.3) | copy-start | bytes 25348
  1.5 29.4 %copy-start.10 = (f32[128,128]{1,0:T(8,128)S(1)}, f32[128,128]{1,0:T(8,128)}, u32[]{:S(2)}) copy-start(f32[128,128]{1,0:T(8,128)} %constant.37.clone.wave_first) | copy-start | bytes 196612
  1.5 29.4 %copy-start.11 = (f32[128,128]{1,0:T(8,128)S(1)}, f32[128,128]{1,0:T(8,128)}, u32[]{:S(2)}) copy-start(f32[128,128]{1,0:T(8,128)} %constant.38.clone.wave_second) | copy-start | bytes 196612
  1.6 29.4 %copy-start.12 = (bf16[128,256]{1,0:T(8,128)(2,1)S(1)}, bf16[128,256]{1,0:T(8,128)(2,1)}, u32[]{:S(2)}) copy-start(bf16[128,256]{1,0:T(8,128)(2,1)} %constant.41.clone.factors) | copy-start | bytes 196612
  15.1 15.9 %copy-start = (bf16[512,512]{1,0:T(8,128)(2,1)S(1)}, bf16[512,512]{1,0:T(8,128)(2,1)}, u32[]{:S(2)}) copy-start(bf16[512,512]{1,0:T(8,128)(2,1)} %constant.33.clone.forward) | copy-start | bytes 1572868
  16.3 14.7 %copy-start.2 = (f32[128,256]{1,0:T(8,128)S(1)}, f32[128,256]{1,0:T(8,128)}, u32[]{:S(2)}) copy-start(f32[128,256]{1,0:T(8,128)} %constant.35.clone.twist_cos) | copy-start | bytes 393220
  16.3 14.7 %copy-start.3 = (f32[128,256]{1,0:T(8,128)S(1)}, f32[128,256]{1,0:T(8,128)}, u32[]{:S(2)}) copy-start(f32[128,256]{1,0:T(8,128)} %constant.36.clone.twist_sin) | copy-start | bytes 393220
  16.3 14.7 %copy-start.5 = (bf16[256,128]{1,0:T(8,128)(2,1)S(1)}, bf16[256,128]{1,0:T(8,128)(2,1)}, u32[]{:S(2)}) copy-start(bf16[256,128]{1,0:T(8,128)(2,1)} %constant.31.clone.analysis) | copy-start | bytes 196612
  16.3 14.7 %copy-start.8 = (f32[2,64,64]{2,1,0:T(8,128)S(1)}, f32[2,64,64]{2,1,0:T(8,128)}, u32[]{:S(2)}) copy-start(f32[2,64,64]{2,1,0:T(8,128)} %param.27) | copy-start | bytes 98308
  16.3 29.6 %all-to-all-start = ((bf16[256,4,128]{2,1,0:T(4,128)(2,1)}), bf16[256,4,128]{2,1,0:T(4,128)(2,1)S(1)}, u32[]{:S(2)}, u32[]{:S(2)}) async-start(bf16[256,4,128]{2,1,0:T(4,128)(2,1)} %bitcast.6), calls=%async_computation | async-start | bytes 524288 | tf_op jit(solution)/shard_map/all_to_all | solution.py:598
  31.0 14.9 %copy-start.1 = (bf16[512,512]{1,0:T(8,128)(2,1)S(1)}, bf16[512,512]{1,0:T(8,128)(2,1)}, u32[]{:S(2)}) copy-start(bf16[512,512]{1,0:T(8,128)(2,1)} %constant.34.clone.backward) | copy-start | bytes 1572868
  31.0 14.9 %copy-start.9 = (bf16[128,256]{1,0:T(8,128)(2,1)S(1)}, bf16[128,256]{1,0:T(8,128)(2,1)}, u32[]{:S(2)}) copy-start(bf16[128,256]{1,0:T(8,128)(2,1)} %constant.32.clone.synthesis) | copy-start | bytes 196612
  64.4 15.6 %all-to-all-start.2 = ((bf16[320,2,128]{2,1,0:T(2,128)(2,1)}), bf16[320,2,128]{2,1,0:T(2,128)(2,1)S(1)}, u32[]{:S(2)}, u32[]{:S(2)}) async-start(bf16[320,2,128]{2,1,0:T(2,128)(2,1)} %bitcast.11), calls=%async_computation.2 | async-start | bytes 327680 | tf_op jit(solution)/shard_map/all_to_all | solution.py:598
  69.9 3.2 %collective-permute-start = (bf16[256,256]{1,0:T(8,128)(2,1)S(1)}, bf16[256,256]{1,0:T(8,128)(2,1)S(1)}, u32[]{:S(2)}, u32[]{:S(2)}) collective-permute-start(bf16[256,256]{1,0:T(8,128)(2,1)S(1)} %get-tuple-element.44), channel_id=1, source_target_pairs={{0,1},{1,0},{2,3},{3,2},{4,5},{5,4},{6,7},{7,6},{8,9},{9,8},{10,11... | collective-permute-start | bytes 393224 | tf_op jit(solution)/shard_map/ppermute | solution.py:643
  80.7 21.7 %all-to-all-start.3 = ((bf16[640,2,128]{2,1,0:T(2,128)(2,1)}), bf16[640,2,128]{2,1,0:T(2,128)(2,1)S(1)}, u32[]{:S(2)}, u32[]{:S(2)}) async-start(bf16[640,2,128]{2,1,0:T(2,128)(2,1)} %bitcast.13), calls=%async_computation.3 | async-start | bytes 655360 | tf_op jit(solution)/shard_map/all_to_all | solution.py:598
  88.6 11.1 %collective-permute-start.1 = (bf16[128,256]{1,0:T(8,128)(2,1)S(1)}, bf16[128,256]{1,0:T(8,128)(2,1)S(1)}, u32[]{:S(2)}, u32[]{:S(2)}) collective-permute-start(bf16[128,256]{1,0:T(8,128)(2,1)S(1)} %get-tuple-element.48), channel_id=1, source_target_pairs={{0,2},{2,0},{1,3},{3,1},{4,6},{6,4},{5,7},{7,5},{8,10},{10,8},{9,1... | collective-permute-start | bytes 196616 | tf_op jit(solution)/shard_map/ppermute | solution.py:647

commit v10 on v9

--- a/solution.py
+++ b/solution.py
@@ -280,7 +280,7 @@
             shapes[i, rows, :] = jnp.sum(product.reshape(HIDDEN, 8, CHUNK), 0)
         return carry
 
-    lax.fori_loop(0, SEQ // 8, block, 0, unroll=2)
+    lax.fori_loop(0, SEQ // 8, block, 0, unroll=4)
     time = lax.broadcasted_iota(jnp.int32, (SEQ, CHUNK), 0) * CHUNK + lax.broadcasted_iota(
         jnp.int32, (SEQ, CHUNK), 1
     )

time: 104 us -> 104 us (level)
  transfers between devices with their start and end apart: 5 -> 5, of which waited for: 5 -> 5; matrix products, arithmetic and copies ran while one was open for 0% -> 0% of each run, Pallas kernels for 9% -> 8%
where the time goes in v10:
time: 104 us; the launch traced here: 103 us
  starting transfers between devices  36.5 us (35%)
  blocking collectives  28.8 us (28%)
  waiting for transfers between devices  21.6 us (21%)
  Pallas kernels  14.5 us (14%)
    all_to_all x3, starting transfers between devices, swap(): lax.all_to_all(tiles, 'seq', split_axis=0, concat_axis=0, axis_index_grou...  27.7 us
    all_to_all x3, waiting for transfers between devices, swap(): lax.all_to_all(tiles, 'seq', split_axis=0, concat_axis=0, axis_index_grou...  16.1 us
    all_to_all x1, blocking collectives, swap(): lax.all_to_all(tiles, 'seq', split_axis=0, concat_axis=0, axis_index_grou...  15.3 us
    all_gather x1, blocking collectives, shards(): lax.all_gather(jnp.concatenate([inputs, cotangent], 0), 'ch', axis=0, til...  13.5 us
    pallas_call x1, Pallas kernels, shards(): filtering()  8.19 us
    ppermute x1, starting transfers between devices, shards(): over_chips = lax.ppermute(given, 'ch', [(0, 2), (2, 0), (1, 3), (3, 1)])  6.91 us
    ppermute x1, waiting for transfers between devices, shards(): over_chips = lax.ppermute(given, 'ch', [(0, 2), (2, 0), (1, 3), (3, 1)])  4.19 us
    pallas_call x1, Pallas kernels, shards(): series()  2.17 us
  transfers between devices with their start and end apart: 5, of which 5 were waited for; matrix products, arithmetic and copies ran while one was open for 0% of the time, Pallas kernels for 8%

profile of v10, /device:TPU:8, one launch (start us, length us, event | category | flops | bytes accessed | tf_op | source)
XLA Modules:
  0.0 103.2 jit_solution(18423066693675997528)
XLA Ops:
  0.7 0.0 copy-start.14
  0.7 0.8 pad_maximum_fusion
  1.5 0.0 copy-start.10
  1.5 0.0 copy-start.11
  1.6 0.0 copy-start.12
  1.6 13.5 %all_gather.3.full = bf16[512,256]{1,0:T(8,128)(2,1)S(1)} all-gather(bf16[128,256]{1,0:T(8,128)(2,1)S(1)} %pad_maximum_fusion), channel_id=1, replica_groups=mesh['seq'=128,'ch'=4] {'ch'}, dimensions={0}, use_global_device_ids=true | all-gather | bytes 327680 | tf_op jit(solution)/shard_map/all_gather | solution.py:622
  15.1 1.1 %project.1 = (bf16[1024,128]{1,0:T(8,128)(2,1)}, f32[64,256]{1,0:T(8,128)S(1)}, f32[64,256]{1,0:T(8,128)S(1)}, f32[64,256]{1,0:T(8,128)S(1)}, f32[128,256]{1,0:T(8,128)S(1)}, /*index=5*/f32[8,128]{1,0:T(8,128)S(1)}) custom-call(s32[1]{0:T(128)} %bitcast.rank, s32[1,16]{1,0:T(1,128)S(1)} %bitcast.28, s32[1,16]{1,0:T(1,128)S(1)} %bitcast.29, ...), custom_call_target="tpu_custom_call" | custom-call | tf_op jit(solution)/shard_map/project/pallas_call | solution.py:623
  16.3 14.6 %all-to-all-start = ((bf16[256,4,128]{2,1,0:T(4,128)(2,1)}), bf16[256,4,128]{2,1,0:T(4,128)(2,1)S(1)}, u32[]{:S(2)}, u32[]{:S(2)}) async-start(bf16[256,4,128]{2,1,0:T(4,128)(2,1)} %bitcast.6), calls=%async_computation | async-start | bytes 524288 | tf_op jit(solution)/shard_map/all_to_all | solution.py:598
  31.0 8.2 %filters.1 = f32[256,512]{1,0:T(8,128)S(1)} custom-call(s32[1]{0:T(128)} %bitcast.rank, f32[33,64]{1,0:T(8,128)S(1)} %copy-done.7, f32[128,64]{1,0:T(8,128)S(1)} %bitcast.27, f32[2,64]{1,0:T(2,128)S(1)} %copy-done.15, f32[128,128]{1,0:T(8,128)S(1)} %copy-done.10, f32[128,128]{1,0:T(8,128)S(1)} %copy-done.11, f32[40,128]{1,0:T(8,128)S(1)} %copy-done.13, ...), custom_call_target="tpu_custom_call" | custom-call | tf_op jit(solution)/shard_map/filters/pallas_call | solution.py:631
  39.2 6.6 %all-to-all-done = bf16[256,4,128]{2,1,0:T(4,128)(2,1)S(1)} async-done(((bf16[256,4,128]{2,1,0:T(4,128)(2,1)}), bf16[256,4,128]{2,1,0:T(4,128)(2,1)S(1)}, u32[]{:S(2)}, u32[]{:S(2)}) %all-to-all-start) | async-done | bytes 262176 | tf_op jit(solution)/shard_map/all_to_all | solution.py:598
  45.9 2.2 %convolve.1 = (bf16[640,128]{1,0:T(8,128)(2,1)S(1)}, f32[8,128]{1,0:T(8,128)S(1)}) custom-call(f32[8,128]{1,0:T(8,128)S(1)} %get-tuple-element.32.notes, bf16[1024,128]{1,0:T(8,128)(2,1)S(1)} %bitcast.19, f32[256,512]{1,0:T(8,128)S(1)} %filters.1, bf16[256,128]{1,0:T(8,128)(2,1)S(1)} %copy-done.5, bf16[128,256]{1,0:T(8,128)(2,1)S(1)} %copy-done.9, ...), custom_call_target="tpu_custom_call" | custom-call | tf_op jit(solution)/shard_map/convolve/pallas_call | solution.py:635
  48.0 15.3 %all_to_all.20 = bf16[320,2,128]{2,1,0:T(2,128)(2,1)S(1)} all-to-all(bf16[320,2,128]{2,1,0:T(2,128)(2,1)S(1)} %bitcast.24), channel_id=1, replica_groups={{0,4,8,12,16,20,24,28,32,36,40,44,48,52,56,60,64,68,72,76,80,84,88,92,9..., dimensions={0} | all-to-all | bytes 327680 | tf_op jit(solution)/shard_map/all_to_all | solution.py:598
  63.3 1.1 %weigh.1 = (bf16[640,128]{1,0:T(8,128)(2,1)}, bf16[64,256]{1,0:T(8,128)(2,1)S(1)}, bf16[192,256]{1,0:T(8,128)(2,1)S(1)}) custom-call(bf16[640,128]{1,0:T(8,128)(2,1)S(1)} %bitcast.21, bf16[512,256]{1,0:T(8,128)(2,1)S(1)} %all_gather.3.full, f32[64,256]{1,0:T(8,128)S(1)} %get-tuple-element.35.gate_in, f32[64,256]{1,0:T(8,128)S(1)} %get-tuple-element.36.grad_in, ...), custom_call_target="tpu_custom_call" | custom-call | tf_op jit(solution)/shard_map/weigh/pallas_call | solution.py:639
  64.4 5.2 %all-to-all-start.2 = ((bf16[320,2,128]{2,1,0:T(2,128)(2,1)}), bf16[320,2,128]{2,1,0:T(2,128)(2,1)S(1)}, u32[]{:S(2)}, u32[]{:S(2)}) async-start(bf16[320,2,128]{2,1,0:T(2,128)(2,1)} %bitcast.11), calls=%async_computation.2 | async-start | bytes 327680 | tf_op jit(solution)/shard_map/all_to_all | solution.py:598
  69.6 0.3 mix.1
  69.9 1.9 %collective-permute-start = (bf16[256,256]{1,0:T(8,128)(2,1)S(1)}, bf16[256,256]{1,0:T(8,128)(2,1)S(1)}, u32[]{:S(2)}, u32[]{:S(2)}) collective-permute-start(bf16[256,256]{1,0:T(8,128)(2,1)S(1)} %get-tuple-element.44), channel_id=1, source_target_pairs={{0,1},{1,0},{2,3},{3,2},{4,5},{5,4},{6,7},{7,6},{8,9},{9,8},{10,11... | collective-permute-start | bytes 393224 | tf_op jit(solution)/shard_map/ppermute | solution.py:643
  71.8 1.3 %collective-permute-done.received = bf16[256,256]{1,0:T(8,128)(2,1)S(1)} collective-permute-done((bf16[256,256]{1,0:T(8,128)(2,1)S(1)}, bf16[256,256]{1,0:T(8,128)(2,1)S(1)}, u32[]{:S(2)}, u32[]{:S(2)}) %collective-permute-start) | collective-permute-done | bytes 131104 | tf_op jit(solution)/shard_map/ppermute | solution.py:643
  73.2 6.8 %all-to-all-done.2 = bf16[320,2,128]{2,1,0:T(2,128)(2,1)S(1)} async-done(((bf16[320,2,128]{2,1,0:T(2,128)(2,1)}), bf16[320,2,128]{2,1,0:T(2,128)(2,1)S(1)}, u32[]{:S(2)}, u32[]{:S(2)}) %all-to-all-start.2) | async-done | bytes 163872 | tf_op jit(solution)/shard_map/all_to_all | solution.py:598
  80.0 0.8 add_up.1
  80.7 7.8 %all-to-all-start.3 = ((bf16[640,2,128]{2,1,0:T(2,128)(2,1)}), bf16[640,2,128]{2,1,0:T(2,128)(2,1)S(1)}, u32[]{:S(2)}, u32[]{:S(2)}) async-start(bf16[640,2,128]{2,1,0:T(2,128)(2,1)} %bitcast.13), calls=%async_computation.3 | async-start | bytes 655360 | tf_op jit(solution)/shard_map/all_to_all | solution.py:598
  88.6 6.9 %collective-permute-start.1 = (bf16[128,256]{1,0:T(8,128)(2,1)S(1)}, bf16[128,256]{1,0:T(8,128)(2,1)S(1)}, u32[]{:S(2)}, u32[]{:S(2)}) collective-permute-start(bf16[128,256]{1,0:T(8,128)(2,1)S(1)} %get-tuple-element.48), channel_id=1, source_target_pairs={{0,2},{2,0},{1,3},{3,1},{4,6},{6,4},{5,7},{7,5},{8,10},{10,8},{9,1... | collective-permute-start | bytes 196616 | tf_op jit(solution)/shard_map/ppermute | solution.py:647
  95.5 4.2 %collective-permute-done.1.over_chips = bf16[128,256]{1,0:T(8,128)(2,1)S(1)} collective-permute-done((bf16[128,256]{1,0:T(8,128)(2,1)S(1)}, bf16[128,256]{1,0:T(8,128)(2,1)S(1)}, u32[]{:S(2)}, u32[]{:S(2)}) %collective-permute-start.1) | collective-permute-done | bytes 65568 | tf_op jit(solution)/shard_map/ppermute | solution.py:647
  99.7 2.7 %all-to-all-done.3 = bf16[640,2,128]{2,1,0:T(2,128)(2,1)S(1)} async-done(((bf16[640,2,128]{2,1,0:T(2,128)(2,1)}), bf16[640,2,128]{2,1,0:T(2,128)(2,1)S(1)}, u32[]{:S(2)}, u32[]{:S(2)}) %all-to-all-start.3) | async-done | bytes 327712 | tf_op jit(solution)/shard_map/all_to_all | solution.py:598
  102.4 0.8 unpack.1
  (35 shorter events, 0.1 us)
Async XLA Ops:
  0.6 14.4 %copy-start.15 = (f32[2,64]{1,0:T(2,128)S(1)}, f32[2,64]{1,0:T(2,128)}, u32[]{:S(2)}) copy-start(f32[2,64]{1,0:T(2,128)} %decay.3) | copy-start | bytes 1540
  0.6 14.4 %copy-start.16 = (f32[2,64]{1,0:T(2,128)S(1)}, f32[2,64]{1,0:T(2,128)}, u32[]{:S(2)}) copy-start(f32[2,64]{1,0:T(2,128)} %skip_gain.1) | copy-start | bytes 1540
  0.7 14.4 %copy-start.17 = (s32[16]{0:T(128)S(1)}, s32[16]{0:T(128)}, u32[]{:S(2)}) copy-start(s32[16]{0:T(128)} %param.22) | copy-start | bytes 196
  0.7 14.4 %copy-start.18 = (s32[16]{0:T(128)S(1)}, s32[16]{0:T(128)}, u32[]{:S(2)}) copy-start(s32[16]{0:T(128)} %param.23) | copy-start | bytes 196
  0.7 30.2 %copy-start.13 = (f32[40,128]{1,0:T(8,128)S(1)}, f32[40,128]{1,0:T(8,128)}, u32[]{:S(2)}) copy-start(f32[40,128]{1,0:T(8,128)} %constant.39.clone.pick_first) | copy-start | bytes 61444
  0.7 30.2 %copy-start.14 = (f32[40,128]{1,0:T(8,128)S(1)}, f32[40,128]{1,0:T(8,128)}, u32[]{:S(2)}) copy-start(f32[40,128]{1,0:T(8,128)} %constant.40.clone.pick_second) | copy-start | bytes 61444
  1.5 13.6 %copy-start.4 = (bf16[3,64,256]{2,1,0:T(8,128)(2,1)S(1)}, bf16[3,64,256]{2,1,0:T(8,128)(2,1)}, u32[]{:S(2)}) copy-start(bf16[3,64,256]{2,1,0:T(8,128)(2,1)} %param.24) | copy-start | bytes 294916
  1.5 13.6 %copy-start.6 = (bf16[256,64]{0,1:T(8,128)(2,1)S(1)}, bf16[256,64]{0,1:T(8,128)(2,1)}, u32[]{:S(2)}) copy-start(bf16[256,64]{0,1:T(8,128)(2,1)} %param.25) | copy-start | bytes 98308
  1.5 13.6 %copy-start.7 = (f32[33,64]{1,0:T(8,128)S(1)}, f32[33,64]{1,0:T(8,128)}, u32[]{:S(2)}) copy-start(f32[33,64]{1,0:T(8,128)} %filt_in.3) | copy-start | bytes 25348
  1.5 29.4 %copy-start.10 = (f32[128,128]{1,0:T(8,128)S(1)}, f32[128,128]{1,0:T(8,128)}, u32[]{:S(2)}) copy-start(f32[128,128]{1,0:T(8,128)} %constant.37.clone.wave_first) | copy-start | bytes 196612
  1.5 29.4 %copy-start.11 = (f32[128,128]{1,0:T(8,128)S(1)}, f32[128,128]{1,0:T(8,128)}, u32[]{:S(2)}) copy-start(f32[128,128]{1,0:T(8,128)} %constant.38.clone.wave_second) | copy-start | bytes 196612
  1.6 29.4 %copy-start.12 = (bf16[128,256]{1,0:T(8,128)(2,1)S(1)}, bf16[128,256]{1,0:T(8,128)(2,1)}, u32[]{:S(2)}) copy-start(bf16[128,256]{1,0:T(8,128)(2,1)} %constant.41.clone.factors) | copy-start | bytes 196612
  15.1 15.9 %copy-start = (bf16[512,512]{1,0:T(8,128)(2,1)S(1)}, bf16[512,512]{1,0:T(8,128)(2,1)}, u32[]{:S(2)}) copy-start(bf16[512,512]{1,0:T(8,128)(2,1)} %constant.33.clone.forward) | copy-start | bytes 1572868
  16.3 14.7 %copy-start.2 = (f32[128,256]{1,0:T(8,128)S(1)}, f32[128,256]{1,0:T(8,128)}, u32[]{:S(2)}) copy-start(f32[128,256]{1,0:T(8,128)} %constant.35.clone.twist_cos) | copy-start | bytes 393220
  16.3 14.7 %copy-start.3 = (f32[128,256]{1,0:T(8,128)S(1)}, f32[128,256]{1,0:T(8,128)}, u32[]{:S(2)}) copy-start(f32[128,256]{1,0:T(8,128)} %constant.36.clone.twist_sin) | copy-start | bytes 393220
  16.3 14.7 %copy-start.5 = (bf16[256,128]{1,0:T(8,128)(2,1)S(1)}, bf16[256,128]{1,0:T(8,128)(2,1)}, u32[]{:S(2)}) copy-start(bf16[256,128]{1,0:T(8,128)(2,1)} %constant.31.clone.analysis) | copy-start | bytes 196612
  16.3 14.7 %copy-start.8 = (f32[2,64,64]{2,1,0:T(8,128)S(1)}, f32[2,64,64]{2,1,0:T(8,128)}, u32[]{:S(2)}) copy-start(f32[2,64,64]{2,1,0:T(8,128)} %param.27) | copy-start | bytes 98308
  16.3 29.6 %all-to-all-start = ((bf16[256,4,128]{2,1,0:T(4,128)(2,1)}), bf16[256,4,128]{2,1,0:T(4,128)(2,1)S(1)}, u32[]{:S(2)}, u32[]{:S(2)}) async-start(bf16[256,4,128]{2,1,0:T(4,128)(2,1)} %bitcast.6), calls=%async_computation | async-start | bytes 524288 | tf_op jit(solution)/shard_map/all_to_all | solution.py:598
  31.0 14.9 %copy-start.1 = (bf16[512,512]{1,0:T(8,128)(2,1)S(1)}, bf16[512,512]{1,0:T(8,128)(2,1)}, u32[]{:S(2)}) copy-start(bf16[512,512]{1,0:T(8,128)(2,1)} %constant.34.clone.backward) | copy-start | bytes 1572868
  31.0 14.9 %copy-start.9 = (bf16[128,256]{1,0:T(8,128)(2,1)S(1)}, bf16[128,256]{1,0:T(8,128)(2,1)}, u32[]{:S(2)}) copy-start(bf16[128,256]{1,0:T(8,128)(2,1)} %constant.32.clone.synthesis) | copy-start | bytes 196612
  64.4 15.6 %all-to-all-start.2 = ((bf16[320,2,128]{2,1,0:T(2,128)(2,1)}), bf16[320,2,128]{2,1,0:T(2,128)(2,1)S(1)}, u32[]{:S(2)}, u32[]{:S(2)}) async-start(bf16[320,2,128]{2,1,0:T(2,128)(2,1)} %bitcast.11), calls=%async_computation.2 | async-start | bytes 327680 | tf_op jit(solution)/shard_map/all_to_all | solution.py:598
  69.9 3.2 %collective-permute-start = (bf16[256,256]{1,0:T(8,128)(2,1)S(1)}, bf16[256,256]{1,0:T(8,128)(2,1)S(1)}, u32[]{:S(2)}, u32[]{:S(2)}) collective-permute-start(bf16[256,256]{1,0:T(8,128)(2,1)S(1)} %get-tuple-element.44), channel_id=1, source_target_pairs={{0,1},{1,0},{2,3},{3,2},{4,5},{5,4},{6,7},{7,6},{8,9},{9,8},{10,11... | collective-permute-start | bytes 393224 | tf_op jit(solution)/shard_map/ppermute | solution.py:643
  80.7 21.7 %all-to-all-start.3 = ((bf16[640,2,128]{2,1,0:T(2,128)(2,1)}), bf16[640,2,128]{2,1,0:T(2,128)(2,1)S(1)}, u32[]{:S(2)}, u32[]{:S(2)}) async-start(bf16[640,2,128]{2,1,0:T(2,128)(2,1)} %bitcast.13), calls=%async_computation.3 | async-start | bytes 655360 | tf_op jit(solution)/shard_map/all_to_all | solution.py:598
  88.6 11.1 %collective-permute-start.1 = (bf16[128,256]{1,0:T(8,128)(2,1)S(1)}, bf16[128,256]{1,0:T(8,128)(2,1)S(1)}, u32[]{:S(2)}, u32[]{:S(2)}) collective-permute-start(bf16[128,256]{1,0:T(8,128)(2,1)S(1)} %get-tuple-element.48), channel_id=1, source_target_pairs={{0,2},{2,0},{1,3},{3,1},{4,6},{6,4},{5,7},{7,5},{8,10},{10,8},{9,1... | collective-permute-start | bytes 196616 | tf_op jit(solution)/shard_map/ppermute | solution.py:647
